TPU v7x, 768 devices: a whole 4x8x12 slice. The times are simulated.
768 devices in a mesh: lon: 192 (over y, x_hi, z), lat: 4 (over x_lo, core).
Axes of the slice: x: 4 (x_hi: 2, x_lo: 2; x = x_hi * 2 + x_lo), y: 8, z: 12, core: 2. Of those that a mesh axis runs over, the one named last changes fastest.
Arguments:
- thermal_anomaly: float32 [8, 3072, 1536], P(None, 'lon', 'lat'), may hold values from -6 to 6
- saltiness_anomaly: float32 [8, 3072, 1536], P(None, 'lon', 'lat'), may hold values from -6 to 6
- eastward_transit_ratio: float32 [8, 3072, 1536], P(None, 'lon', 'lat'), may hold values from -0.45 to 0.45
- poleward_transit_ratio: float32 [8, 3072, 1536], P(None, 'lon', 'lat'), may hold values from -0.45 to 0.45
- elevation_prior: float32 [3072, 1536], P('lon', 'lat'), may hold values from -12 to 12
- ocean_point_flag: int32 [3072, 1536], P('lon', 'lat'), may hold values 0 or 1
- depth_layers: int32 [3072, 1536], P('lon', 'lat'), may hold values from 1 to 8
- fold_counterpart: int32 [3072], P('lon'), may hold values from 0 to 3071, as said below
Outputs:
- temperature_next: float32 [8, 3072, 1536], P(None, 'lon', 'lat')
- salinity_next: float32 [8, 3072, 1536], P(None, 'lon', 'lat')
- surface_next: float32 [3072, 1536], P('lon', 'lat')
- surface_residual: float32 [3072, 1536], P('lon', 'lat')
Inputs may be any that keep to these rules, and one draw needn't show every extreme that they name: Partner is a mirror across the fold: fold_counterpart[i] = (s - i) mod 3072 for one s with s + 1 a multiple of 16, so fold_counterpart[fold_counterpart[i]] = i and fold_counterpart[i] != i.
All inputs are finite; a program needn't handle non-finite values. No bound on the sum of `ocean_point_flag` on one device may be relied on, other than what follows from the above.
Results may differ from a plain program's by a relative error of at most 0.00035.
Values sent between devices are 32-bit elements; how exact they have to be, the bound alone decides.
No kernel may reach another device: no remote copies, remote signals or barrier semaphores. Data moves between devices by JAX's collectives and lax.ppermute only.
A program may use at most 64 MiB of HBM per device.

v0:
```python
import jax
import jax.numpy as jnp
from jax import lax
from jax.sharding import PartitionSpec as P

ITERS = 3


def extended(value, sides, width):
    for axis, dim in sides:
        peers, length = (lax.axis_size(axis), value.shape[dim])
        up = [(i, (i + 1) % peers) for i in range(peers)]
        down = [(j, i) for i, j in up]
        last = lax.slice_in_dim(value, length - width, length, axis=dim)
        initial = lax.slice_in_dim(value, 0, width, axis=dim)
        before = lax.ppermute(last, axis, up)
        after = lax.ppermute(initial, axis, down)
        value = jnp.concatenate([before, value, after], axis=dim)
    return value


def weno_face(far_up, near_up, center, near_down, far_down):
    stencil_low = (2.0 * far_up - 7.0 * near_up + 11.0 * center) / 6.0
    stencil_mid = (-near_up + 5.0 * center + 2.0 * near_down) / 6.0
    stencil_top = (2.0 * center + 5.0 * near_down - far_down) / 6.0
    beta_low = (
        13.0 / 12.0 * (far_up - 2.0 * near_up + center) ** 2
        + 0.25 * (far_up - 4.0 * near_up + 3.0 * center) ** 2
    )
    beta_mid = (
        13.0 / 12.0 * (near_up - 2.0 * center + near_down) ** 2 + 0.25 * (near_up - near_down) ** 2
    )
    beta_top = (
        13.0 / 12.0 * (center - 2.0 * near_down + far_down) ** 2
        + 0.25 * (3.0 * center - 4.0 * near_down + far_down) ** 2
    )
    weight_low = 0.1 / (1e-06 + beta_low) ** 2
    weight_mid = 0.6 / (1e-06 + beta_mid) ** 2
    weight_top = 0.3 / (1e-06 + beta_top) ** 2
    summed = weight_low * stencil_low + weight_mid * stencil_mid + weight_top * stencil_top
    return summed / (weight_low + weight_mid + weight_top)


def face_flux(padded, speed, count, axis):
    shifted = [
        lax.slice_in_dim(padded, offset, offset + count + 1, axis=axis) for offset in range(6)
    ]
    upwind_left = weno_face(shifted[0], shifted[1], shifted[2], shifted[3], shifted[4])
    upwind_right = weno_face(shifted[5], shifted[4], shifted[3], shifted[2], shifted[1])
    return jnp.maximum(speed, 0.0) * upwind_left + jnp.minimum(speed, 0.0) * upwind_right


def fix_rims(padded, width, lat_index, lat_last, north_fill):
    south_rim = jnp.where(lat_index == 0, 0.0, padded[..., :width])
    north_rim = jnp.where(lat_index == lat_last, north_fill, padded[..., -width:])
    return jnp.concatenate([south_rim, padded[..., width:-width], north_rim], axis=-1)


def operate(scalar_quantity, coupler, lat_index, lat_last):
    scaled = coupler * scalar_quantity
    padded = extended(scaled, (("lon", 0), ("lat", 1)), 1)
    lon_pad = padded[:, 1:-1]
    lat_pad = fix_rims(padded[1:-1, :], 1, lat_index, lat_last, 0.0)
    laplace = 4.0 * scaled - lon_pad[2:] - lon_pad[:-2] - lat_pad[:, 2:] - lat_pad[:, :-2]
    return scalar_quantity + coupler * laplace


def two_sums(residual, product_field):
    return lax.psum(
        (jnp.sum(residual * residual), jnp.sum(residual * product_field)), ("lon", "lat")
    )


def on_device(
    thermal_anomaly,
    saltiness_anomaly,
    eastward_transit_ratio,
    poleward_transit_ratio,
    elevation_prior,
    ocean_point_flag,
    depth_layers,
    fold_counterpart,
):
    layer_number = thermal_anomaly.shape[0]
    meridian_number = thermal_anomaly.shape[1]
    parallel_number = thermal_anomaly.shape[2]
    lat_index = lax.axis_index("lat")
    lat_last = lax.axis_size("lat") - 1
    layer_positions = lax.broadcasted_iota(jnp.int32, thermal_anomaly.shape, 0)
    ocean_indicator = jnp.where(
        (ocean_point_flag[None] == 1) & (layer_positions < depth_layers[None]), 1.0, 0.0
    ).astype(jnp.float32)
    scalar_bundle = jnp.stack(
        [thermal_anomaly * ocean_indicator, saltiness_anomaly * ocean_indicator]
    )
    speeds = jnp.stack(
        [eastward_transit_ratio * ocean_indicator, poleward_transit_ratio * ocean_indicator]
    )
    top_rows = jnp.flip(scalar_bundle[..., parallel_number - 3 :], axis=3)
    upper_rows = jnp.transpose(top_rows, (0, 1, 3, 2))
    gathered = lax.all_gather(upper_rows, "lon", axis=3, tiled=True)
    folded = jnp.transpose(jnp.take(gathered, fold_counterpart, axis=3), (0, 1, 3, 2))
    stacked = extended(jnp.concatenate([scalar_bundle, speeds]), (("lon", 2), ("lat", 3)), 3)
    tracer_pad = stacked[:2]
    speed_pad = stacked[2:]
    speed_width = 3
    zonal_pad = tracer_pad[..., 3 : parallel_number + 3]
    merid_pad = fix_rims(
        tracer_pad[:, :, 3 : meridian_number + 3, :], 3, lat_index, lat_last, folded
    )
    east_faces = speed_pad[
        0,
        :,
        speed_width - 1 : speed_width + meridian_number,
        speed_width : speed_width + parallel_number,
    ]
    north_raw = speed_pad[
        1,
        :,
        speed_width : speed_width + meridian_number,
        speed_width - 1 : speed_width + parallel_number,
    ]
    south_face = jnp.where(lat_index == 0, 0.0, north_raw[..., :1])
    north_faces = jnp.concatenate([south_face, north_raw[..., 1:]], axis=-1)
    flux_x = face_flux(zonal_pad, east_faces[None], meridian_number, 2)
    flux_y = face_flux(merid_pad, north_faces[None], parallel_number, 3)
    updated = (
        scalar_bundle
        - (flux_x[:, :, 1:] - flux_x[:, :, :-1])
        - (flux_y[..., 1:] - flux_y[..., :-1])
    )
    updated = updated * ocean_indicator
    east_mean = jnp.sum(east_faces, axis=0) / layer_number
    north_mean = jnp.sum(north_faces, axis=0) / layer_number
    divergence = east_mean[1:] - east_mean[:-1] + north_mean[:, 1:] - north_mean[:, :-1]
    right_side = elevation_prior - divergence
    coupler = 2.0 * jnp.sqrt((depth_layers * ocean_point_flag).astype(jnp.float32) / layer_number)
    solution = jnp.zeros_like(right_side)
    residual = right_side
    product_field = operate(residual, coupler, lat_index, lat_last)
    norm_now, curvature = two_sums(residual, product_field)
    step_size = norm_now / curvature
    direction = residual
    along_image = product_field
    for iteration in range(ITERS):
        solution = solution + step_size * direction
        residual = residual - step_size * along_image
        if iteration + 1 < ITERS:
            product_field = operate(residual, coupler, lat_index, lat_last)
            norm_next, curvature = two_sums(residual, product_field)
            beta_ratio = norm_next / norm_now
            step_size = norm_next / (curvature - beta_ratio * norm_next / step_size)
            direction = residual + beta_ratio * direction
            along_image = product_field + beta_ratio * along_image
            norm_now = norm_next
    return (updated[0], updated[1], solution, residual)


def solution(mesh):
    placed = (
        P(None, "lon", "lat"),
        P(None, "lon", "lat"),
        P(None, "lon", "lat"),
        P(None, "lon", "lat"),
        P("lon", "lat"),
        P("lon", "lat"),
        P("lon", "lat"),
        P("lon"),
    )
    return jax.shard_map(
        on_device,
        mesh=mesh,
        in_specs=placed,
        out_specs=(P(None, "lon", "lat"), P(None, "lon", "lat"), P("lon", "lat"), P("lon", "lat")),
        check_vma=False,
    )
```

profile of v0, /device:TPU:1, one launch (start us, length us, event | category | flops | bytes accessed | tf_op | source)
XLA Modules:
  0.0 1022.2 jit_solution(17887674696287169931)
XLA Ops:
  0.6 0.7 broadcast_compare_fusion
  1.4 1.3 fusion.73
  2.7 0.1 pad_maximum_fusion
  2.8 0.1 fusion.104
  2.9 4.8 collective-permute-start
  7.7 17.6 %collective-permute-start.1 = (f32[4,8,3,384]{3,1,2,0:T(8,128)S(1)}, f32[4,8,3,384]{3,1,2,0:T(8,128)S(1)}, u32[]{:S(2)}, u32[]{:S(2)}) collective-permute-start(f32[4,8,3,384]{3,1,2,0:T(8,128)S(1)} %copy.130), channel_id=1, source_target_pairs={{4,0},{8,4},{12,8},{16,12},{20,16},{24,20},{28,24},{32,28},{36,32}... | collective-permute-start | bytes 442376 | tf_op jit(solution)/shard_map/ppermute | solution.py:17
  25.3 0.1 fusion.77
  25.5 0.1 copy.120
  25.6 0.3 copy.123
  25.9 0.1 copy.110
  26.0 495.7 %all_gather.3 = f32[2,8,3,3072]{1,0,2,3:T(2,128)S(1)} all-gather(f32[2,8,3,16]{1,0,2,3:T(2,128)S(1)} %reverse_bitcast_fusion), channel_id=1, replica_groups=mesh['lon'=192,'lat'=4] {'lon'}, dimensions={3}, use_global_device_ids=true | all-gather | bytes 592896 | tf_op jit(solution)/shard_map/all_gather | solution.py:101
  521.7 4.5 copy.116
  526.2 4.3 gather_fusion
  530.5 0.3 copy.117
  530.8 0.3 constant_dynamic-update-slice_fusion
  531.1 0.1 slice_reduce_fusion
  531.2 0.2 fusion.103
  531.4 84.1 %collective-permute-start.2 = (f32[4,8,22,3]{3,1,2,0:T(8,128)S(1)}, f32[4,8,22,3]{3,1,2,0:T(8,128)S(1)}, u32[]{:S(2)}, u32[]{:S(2)}) collective-permute-start(f32[4,8,22,3]{3,1,2,0:T(8,128)S(1)} %get-tuple-element.41), channel_id=1, source_target_pairs={{0,1},{1,2},{2,3},{3,0},{4,5},{5,6},{6,7},{7,4},{8,9},{9,10},{10,1... | collective-permute-start | bytes 25352 | tf_op jit(solution)/shard_map/ppermute | solution.py:16
  615.5 1.9 collective-permute-start.3
  617.4 1.8 multiply_add_fusion.3
  619.2 0.6 collective-permute-done.2
  619.9 0.1 pad_maximum_fusion.4
  620.0 0.0 copy-start
  620.0 0.2 copy.131
  620.2 0.1 slice.343
  620.3 0.1 fusion.74
  620.5 0.2 copy-done
  620.8 0.0 copy-done.1
  620.8 0.0 copy-done.2
  620.8 0.1 fusion.101
  620.9 2.1 collective-permute-start.5
  623.0 8.9 collective-permute-start.4
  631.9 0.2 copy.119
  632.1 0.2 copy.113
  632.3 0.1 slice_select_fusion
  632.4 2.7 multiply_add_fusion
  635.1 0.1 pad_maximum_fusion.26
  635.1 5.7 collective-permute-start.6
  640.9 1.9 collective-permute-start.7
  642.8 1.1 collective-permute-done.7
  644.0 0.7 multiply_reduce_fusion.4
  644.7 107.8 %all-reduce.2 = (f32[]{:T(128)}, f32[]{:T(128)}) all-reduce(f32[]{:T(128)} %get-tuple-element.25, f32[]{:T(128)} %get-tuple-element.24), channel_id=1, replica_groups=mesh['lon'=192,'lat'=4] {'lon','lat'}, use_global_device_ids=true, to_apply=%region_3.4 | all-reduce | flops 2 | bytes 16 | tf_op jit(solution)/shard_map/psum | solution.py:69
  753.8 1.9 collective-permute-start.9
  755.7 9.1 collective-permute-start.8
  764.8 0.2 fusion.66
  765.1 0.5 collective-permute-done.8
  765.5 0.1 pad_maximum_fusion.23
  765.6 3.7 collective-permute-start.10
  769.3 2.3 collective-permute-start.11
  771.6 0.8 collective-permute-done.11
  772.4 0.7 multiply_reduce_fusion.2
  773.1 109.7 %all-reduce.1 = (f32[]{:T(128)}, f32[]{:T(128)}) all-reduce(f32[]{:T(128)} %get-tuple-element.23, f32[]{:T(128)} %get-tuple-element.22), channel_id=1, replica_groups=mesh['lon'=192,'lat'=4] {'lon','lat'}, use_global_device_ids=true, to_apply=%region_7.8 | all-reduce | flops 2 | bytes 16 | tf_op jit(solution)/shard_map/psum | solution.py:69
  887.4 1.9 collective-permute-start.13
  889.3 9.1 collective-permute-start.12
  898.5 0.7 copy.122
  899.2 0.7 copy.121
  899.9 0.1 pad_maximum_fusion.20
  900.0 3.1 collective-permute-start.14
  903.1 2.8 collective-permute-start.15
  906.0 0.8 collective-permute-done.15
  906.7 0.7 multiply_reduce_fusion
  907.4 109.5 %all-reduce = (f32[]{:T(128)}, f32[]{:T(128)}) all-reduce(f32[]{:T(128)} %get-tuple-element.21, f32[]{:T(128)} %get-tuple-element.20), channel_id=1, replica_groups=mesh['lon'=192,'lat'=4] {'lon','lat'}, use_global_device_ids=true, to_apply=%region_11.12 | all-reduce | flops 2 | bytes 16 | tf_op jit(solution)/shard_map/psum | solution.py:69
  1020.9 0.6 multiply_add_fusion.6
  1021.5 0.7 multiply_subtract_fusion.4
  (40 shorter events, 0.3 us)
Async XLA Ops:
  2.8 22.6 %copy-start.3 = (s32[16]{0:T(128)S(1)}, s32[16]{0:T(128)}, u32[]{:S(2)}) copy-start(s32[16]{0:T(128)} %param.15) | copy-start | bytes 196
  2.9 527.9 %collective-permute-start = (f32[4,8,3,384]{3,1,2,0:T(8,128)S(1)}, f32[4,8,3,384]{3,1,2,0:T(8,128)S(1)}, u32[]{:S(2)}, u32[]{:S(2)}) collective-permute-start(f32[4,8,3,384]{3,1,2,0:T(8,128)S(1)} %copy.129), channel_id=1, source_target_pairs={{0,4},{4,8},{8,12},{12,16},{16,20},{20,24},{24,28},{28,32},{32,36}... | collective-permute-start | bytes 442376 | tf_op jit(solution)/shard_map/ppermute | solution.py:16
  7.7 523.4 %collective-permute-start.1 = (f32[4,8,3,384]{3,1,2,0:T(8,128)S(1)}, f32[4,8,3,384]{3,1,2,0:T(8,128)S(1)}, u32[]{:S(2)}, u32[]{:S(2)}) collective-permute-start(f32[4,8,3,384]{3,1,2,0:T(8,128)S(1)} %copy.130), channel_id=1, source_target_pairs={{4,0},{8,4},{12,8},{16,12},{20,16},{24,20},{28,24},{32,28},{36,32}... | collective-permute-start | bytes 442376 | tf_op jit(solution)/shard_map/ppermute | solution.py:17
  531.4 88.5 %collective-permute-start.2 = (f32[4,8,22,3]{3,1,2,0:T(8,128)S(1)}, f32[4,8,22,3]{3,1,2,0:T(8,128)S(1)}, u32[]{:S(2)}, u32[]{:S(2)}) collective-permute-start(f32[4,8,22,3]{3,1,2,0:T(8,128)S(1)} %get-tuple-element.41), channel_id=1, source_target_pairs={{0,1},{1,2},{2,3},{3,0},{4,5},{5,6},{6,7},{7,4},{8,9},{9,10},{10,1... | collective-permute-start | bytes 25352 | tf_op jit(solution)/shard_map/ppermute | solution.py:16
  615.5 16.7 %collective-permute-start.3 = (f32[4,8,22,3]{3,1,2,0:T(8,128)S(1)}, f32[4,8,22,3]{3,1,2,0:T(8,128)S(1)}, u32[]{:S(2)}, u32[]{:S(2)}) collective-permute-start(f32[4,8,22,3]{3,1,2,0:T(8,128)S(1)} %get-tuple-element.42), channel_id=1, source_target_pairs={{1,0},{2,1},{3,2},{0,3},{5,4},{6,5},{7,6},{4,7},{9,8},{10,9},{11,1... | collective-permute-start | bytes 25352 | tf_op jit(solution)/shard_map/ppermute | solution.py:17
  620.0 0.7 copy-start
  620.0 0.7 copy-start.1
  620.0 0.8 copy-start.2
  620.9 14.2 %collective-permute-start.5 = (f32[1,384]{1,0:T(1,128)S(1)}, f32[1,384]{1,0:T(1,128)S(1)}, u32[]{:S(2)}, u32[]{:S(2)}) collective-permute-start(f32[1,384]{1,0:T(1,128)S(1)} %get-tuple-element.75), channel_id=1, source_target_pairs={{0,4},{4,8},{8,12},{12,16},{16,20},{20,24},{24,28},{28,32},{32,36}... | collective-permute-start | bytes 4616 | tf_op jit(solution)/shard_map/ppermute | solution.py:16
  623.0 12.1 %collective-permute-start.4 = (f32[1,384]{1,0:T(1,128)S(1)}, f32[1,384]{1,0:T(1,128)S(1)}, u32[]{:S(2)}, u32[]{:S(2)}) collective-permute-start(f32[1,384]{1,0:T(1,128)S(1)} %get-tuple-element.76), channel_id=1, source_target_pairs={{4,0},{8,4},{12,8},{16,12},{20,16},{24,20},{28,24},{32,28},{36,32}... | collective-permute-start | bytes 4616 | tf_op jit(solution)/shard_map/ppermute | solution.py:17
  635.1 7.7 collective-permute-start.6
  640.9 3.1 collective-permute-start.7
  753.8 11.2 %collective-permute-start.9 = (f32[1,384]{1,0:T(1,128)S(1)}, f32[1,384]{1,0:T(1,128)S(1)}, u32[]{:S(2)}, u32[]{:S(2)}) collective-permute-start(f32[1,384]{1,0:T(1,128)S(1)} %get-tuple-element.73), channel_id=1, source_target_pairs={{0,4},{4,8},{8,12},{12,16},{16,20},{20,24},{24,28},{28,32},{32,36}... | collective-permute-start | bytes 4616 | tf_op jit(solution)/shard_map/ppermute | solution.py:16
  755.7 9.8 collective-permute-start.8
  765.6 6.0 collective-permute-start.10
  769.3 3.1 collective-permute-start.11
  887.4 12.5 %collective-permute-start.13 = (f32[1,384]{1,0:T(1,128)S(1)}, f32[1,384]{1,0:T(1,128)S(1)}, u32[]{:S(2)}, u32[]{:S(2)}) collective-permute-start(f32[1,384]{1,0:T(1,128)S(1)} %get-tuple-element.71), channel_id=1, source_target_pairs={{0,4},{4,8},{8,12},{12,16},{16,20},{20,24},{24,28},{28,32},{32,36}... | collective-permute-start | bytes 4616 | tf_op jit(solution)/shard_map/ppermute | solution.py:16
  889.3 10.6 %collective-permute-start.12 = (f32[1,384]{1,0:T(1,128)S(1)}, f32[1,384]{1,0:T(1,128)S(1)}, u32[]{:S(2)}, u32[]{:S(2)}) collective-permute-start(f32[1,384]{1,0:T(1,128)S(1)} %get-tuple-element.72), channel_id=1, source_target_pairs={{4,0},{8,4},{12,8},{16,12},{20,16},{24,20},{28,24},{32,28},{36,32}... | collective-permute-start | bytes 4616 | tf_op jit(solution)/shard_map/ppermute | solution.py:17
  900.0 6.0 collective-permute-start.14
  903.1 3.6 collective-permute-start.15
where the time goes:
time: 1020 us
  blocking collectives  823 us (81%)
  starting transfers between devices  161 us (16%)
  local copies, waits for them, and re-layouts  12.5 us (1%)
  other arithmetic  11.2 us (1%)
  between operations  11 us (1%)
    all_gather x1, blocking collectives, on_device(): gathered = lax.all_gather(upper_rows, 'lon', axis=3, tiled=True)  496 us
    psum x3, blocking collectives, two_sums(): lax.psum((jnp.sum(residual * residual), jnp.sum(residual * product_field)...  327 us
    ppermute x8, starting transfers between devices, extended(): before = lax.ppermute(last, axis, up)  102 us
    ppermute x8, starting transfers between devices, extended(): after = lax.ppermute(initial, axis, down)  59.2 us
  transfers between devices with their start and end apart: 16, of which 5 were waited for; matrix products, arithmetic and copies ran while one was open for 2% of the time, Pallas kernels for 0%

commit v1 on v0

v1 whole, which is shorter than its diff:
```python
import jax
import jax.numpy as jnp
from jax import lax
from jax.sharding import Mesh, PartitionSpec as P

ITERS = 3
LON = ("y", "xh", "z")
LAT = ("xl", "core")
ALL = LON + LAT
SIZES = (8, 2, 12, 2, 2)
NLON = 192
NLAT = 4
SHIFT = 17.0
SCALE = 16.0


def weno_upwind(a, b, c, d, e):
    d0, d1, d2, d3 = b - a, c - b, d - c, e - d
    s0, s1, s2 = d1 - d0, d2 - d1, d3 - d2
    t0 = s0 + 2.0 * d1
    t1 = d1 + d2
    t2 = s2 - 2.0 * d2
    k = 13.0 / 12.0
    e0 = 1e-06 + k * s0 * s0 + 0.25 * t0 * t0
    e1 = 1e-06 + k * s1 * s1 + 0.25 * t1 * t1
    e2 = 1e-06 + k * s2 * s2 + 0.25 * t2 * t2
    w0, w1, w2 = e1 * e2, e0 * e2, e0 * e1
    w0, w1, w2 = 0.1 * w0 * w0, 0.6 * w1 * w1, 0.3 * w2 * w2
    top = w0 * (5.0 * d1 - 2.0 * d0) + w1 * (d1 + 2.0 * d2) + w2 * (4.0 * d2 - d3)
    return c + top / (6.0 * (w0 + w1 + w2))


def face_flux(padded, speed, count, axis):
    q = [lax.slice_in_dim(padded, o, o + count + 1, axis=axis) for o in range(6)]
    pos = speed > 0.0
    a, b, c, d, e = (
        jnp.where(pos, q[i], q[5 - i]) for i in range(5)
    )
    return speed * weno_upwind(a, b, c, d, e)


def sum_over(value, axes, count):
    spread = jnp.broadcast_to(value[None], (count,) + value.shape)
    return jnp.sum(lax.all_to_all(spread, axes, 0, 0), axis=0)


def coefficients(gram):
    def form(p, q):
        total = 0.0
        for i in range(4):
            for j in range(4):
                if p[i] is not None and q[j] is not None:
                    total = total + p[i] * q[j] * gram[min(i, j)][max(i, j)]
        return total

    def add(p, s, q):
        return [
            (p[i] if q[i] is None else (s * q[i] if p[i] is None else p[i] + s * q[i]))
            for i in range(4)
        ]

    def image(p):
        out = [None] * 4

        def put(i, x):
            out[i] = x if out[i] is None else out[i] + x

        for i in range(3):
            if p[i] is None:
                continue
            put(i, SHIFT * p[i])
            if i == 0:
                put(1, SCALE * p[0])
            else:
                put(i + 1, 0.5 * SCALE * p[i])
                put(i - 1, 0.5 * SCALE * p[i])
        return out

    one = jnp.float32(1.0)
    x = [None] * 4
    r = [one, None, None, None]
    p = list(r)
    norm = form(r, r)
    for it in range(ITERS):
        ap = image(p)
        step = norm / form(p, ap)
        x = add(x, step, p)
        r = add(r, -step, ap)
        if it + 1 < ITERS:
            new = form(r, r)
            p = add(r, new / norm, p)
            norm = new
    return x, r


def on_device(t, s, u, v, elev, flag, depth, fc):
    nl, ni, nj = t.shape
    lat = lax.axis_index(LAT)
    lon = lax.axis_index(LON)
    odd = (lat % 2) == 1
    last = lat == NLAT - 1
    level = lax.broadcasted_iota(jnp.int32, t.shape, 0)
    mask = jnp.where((flag[None] == 1) & (level < depth[None]), 1.0, 0.0).astype(jnp.float32)
    q = jnp.stack([t * mask, s * mask])
    ue = u * mask
    vn = v * mask
    em = jnp.sum(ue, axis=0) / nl
    nm = jnp.sum(vn, axis=0) / nl
    coupler = 2.0 * jnp.sqrt((depth * flag).astype(jnp.float32) / nl)
    part = elev - em - nm

    up = jnp.concatenate(
        [q[:, :, ni - 3 :].reshape(6 * nl, nj), ue[:, ni - 1], part[ni - 3 :], em[ni - 4 :], nm[ni - 3 :], coupler[ni - 3 :]]
    )
    down = jnp.concatenate([q[:, :, :3].reshape(6 * nl, nj), part[:3], em[:3], nm[:3], coupler[:3]])
    west = lax.ppermute(up, LON, [(i, (i + 1) % NLON) for i in range(NLON)])
    east = lax.ppermute(down, LON, [((i + 1) % NLON, i) for i in range(NLON)])
    n6 = 6 * nl
    q_west, q_east = west[:n6].reshape(2, nl, 3, nj), east[:n6].reshape(2, nl, 3, nj)
    u_west = west[n6 : n6 + nl]
    cw, ce = west[n6 + nl :], east[n6:]
    zero = jnp.zeros((1, nj), jnp.float32)
    fields = jnp.stack(
        [
            jnp.concatenate([zero, cw[0:3], part, ce[0:3]]),
            jnp.concatenate([cw[3:7], em, ce[3:6]]),
            jnp.concatenate([zero, cw[7:10], nm, ce[6:9]]),
            jnp.concatenate([zero, cw[10:13], coupler, ce[9:12]]),
        ]
    )
    rows = fields.shape[1]

    def edge(qpart, vcol, fpart):
        a = jnp.transpose(qpart, (0, 3, 1, 2)).reshape(6, nl * ni)
        b = vcol.reshape(1, nl * ni)
        c = jnp.pad(jnp.transpose(fpart, (0, 2, 1)).reshape(16, rows), ((0, 0), (0, nl * ni - rows)))
        return jnp.concatenate([a, b, c])

    to_north = edge(q[..., nj - 3 :], vn[..., nj - 1], fields[..., nj - 4 :])
    to_south = edge(q[..., :3], vn[..., 0], fields[..., :4])
    fold_edge = jnp.transpose(jnp.flip(q[..., nj - 3 :], axis=(2, 3)), (0, 3, 1, 2)).reshape(6, nl * ni)
    fold = jnp.concatenate([fold_edge, to_north[6:]])
    send_a = jnp.where(odd, to_south, to_north)
    send_b = jnp.where(lat == 1, to_north, jnp.where(lat == 2, to_south, fold))
    got_a = lax.ppermute(send_a, LAT, [(0, 1), (1, 0), (2, 3), (3, 2)])
    turn = jnp.mod(fc[0] // ni + lon, NLON)

    def branch(k):
        pairs = []
        for i in range(NLON):
            pairs += [(4 * i + 1, 4 * i + 2), (4 * i + 2, 4 * i + 1), (4 * i + 3, 4 * ((k - i) % NLON) + 3)]
        return lambda value: lax.ppermute(value, ALL, pairs)

    got_b = lax.switch(turn, [branch(k) for k in range(NLON)], send_b)
    north = jnp.where(odd, got_b, got_a)
    south = jnp.where(odd, got_a, got_b)

    def columns(msg):
        return jnp.transpose(msg[:6].reshape(2, 3, nl, ni), (0, 2, 3, 1))

    q_north, q_south = columns(north), columns(south)
    v_south = south[6].reshape(nl, ni, 1)
    keep = jnp.where(last, 0.0, 1.0)

    def fcols(msg):
        return jnp.transpose(msg[7:23, :rows].reshape(4, 4, rows), (0, 2, 1))

    full = jnp.concatenate([fcols(south), fields, fcols(north) * keep], axis=2)
    rhs = full[0, 1:, 1:] + full[1, :-1, 1:] + full[2, 1:, :-1]
    cpl = full[3, 1:, 1:]

    def operate(e):
        f = jnp.pad(cpl * e, ((1, 1), (1, 1)))
        lap = 4.0 * f[1:-1, 1:-1] - f[2:, 1:-1] - f[:-2, 1:-1] - f[1:-1, 2:] - f[1:-1, :-2]
        return e + cpl * lap

    def scaled(e):
        return (operate(e) - SHIFT * e) * (1.0 / SCALE)

    b0 = rhs
    b1 = scaled(b0)
    b2 = 2.0 * scaled(b1) - b0
    b3 = 2.0 * scaled(b2) - b1
    basis = [x[3 : 3 + ni, 3 : 3 + nj] for x in (b0, b1, b2, b3)]
    sums = jnp.stack([jnp.sum(basis[i] * basis[j]) for i in range(4) for j in range(i, 4)])
    sums = jnp.pad(sums, (0, 118)).reshape(1, 128)
    sums = sum_over(sums, "z", 12)
    sums = sum_over(sums, ("y", "xh") + LAT, 64)
    gram = [[None] * 4 for _ in range(4)]
    at = 0
    for i in range(4):
        for j in range(i, 4):
            gram[i][j] = sums[0, at]
            at += 1
    xc, rc = coefficients(gram)
    surface = sum(c * f for c, f in zip(xc, basis) if c is not None)
    residual = sum(c * f for c, f in zip(rc, basis) if c is not None)

    zonal = jnp.concatenate([q_west, q, q_east], axis=2)
    merid = jnp.concatenate([q_south, q, q_north], axis=3)
    speed_x = jnp.concatenate([u_west[:, None], ue], axis=1)
    speed_y = jnp.concatenate([v_south, vn], axis=2)
    flux_x = face_flux(zonal, speed_x[None], ni, 2)
    flux_y = face_flux(merid, speed_y[None], nj, 3)
    updated = q - (flux_x[:, :, 1:] - flux_x[:, :, :-1]) - (flux_y[..., 1:] - flux_y[..., :-1])
    updated = updated * mask
    return updated[0], updated[1], surface, residual


def solution(mesh):
    fine = Mesh(mesh.devices.reshape(SIZES), ALL)
    block, plane = P(None, LON, LAT), P(LON, LAT)
    return jax.shard_map(
        on_device,
        mesh=fine,
        in_specs=(block,) * 4 + (plane,) * 3 + (P(LON),),
        out_specs=(block, block, plane, plane),
        check_vma=False,
    )
```

time: 1020 us -> 173 us (0.17)
  blocking collectives: 823 us -> 0 us
  starting transfers between devices: 161 us -> 95.9 us
  waiting for transfers between devices: 3.82 us -> 31.8 us
    all_gather x1 -> x0, blocking collectives: 496 us -> none  [on_device(): gathered = lax.all_gather(upper_rows, 'lon', axis=3, tiled=True)]
    psum x3 -> x0, blocking collectives: 327 us -> none  [two_sums(): lax.psum((jnp.sum(residual * residual), jnp.sum(residual * product_field)...]
    ppermute x16 -> x4, starting transfers between devices: 161 us -> 73.1 us  [the longest x1 24.3 us: on_device(): east = lax.ppermute(down, LON, [((i + 1) % NLON, i) for i in range(NLON)])]
    all_to_all x0 -> x2, starting transfers between devices: none -> 22.7 us  [sum_over(): return jnp.sum(lax.all_to_all(spread, axes, 0, 0), axis=0)]
    all_to_all x0 -> x2, waiting for transfers between devices: none -> 14.7 us  [sum_over(): return jnp.sum(lax.all_to_all(spread, axes, 0, 0), axis=0)]
    ppermute x16 -> x4, waiting for transfers between devices: 3.82 us -> 17.1 us  [the longest x1 14 us: on_device(): west = lax.ppermute(up, LON, [(i, (i + 1) % NLON) for i in range(NLON)])]
  transfers between devices with their start and end apart: 16 -> 6, of which waited for: 5 -> 4; matrix products, arithmetic and copies ran while one was open for 2% -> 4% of each run, Pallas kernels for 0% -> 0%
where the time goes in v1:
time: 173 us; the launch traced here: 172 us
  starting transfers between devices  95.9 us (55%)
  waiting for transfers between devices  31.8 us (18%)
  between operations  20.9 us (12%)
  local copies, waits for them, and re-layouts  13.6 us (8%)
  other arithmetic  9.27 us (5%)
    ppermute x1, starting transfers between devices, on_device(): east = lax.ppermute(down, LON, [((i + 1) % NLON, i) for i in range(NLON)])  24.3 us
    all_to_all x2, starting transfers between devices, sum_over(): return jnp.sum(lax.all_to_all(spread, axes, 0, 0), axis=0)  22.7 us
    ppermute x1, starting transfers between devices, branch(): return lambda value: lax.ppermute(value, ALL, pairs)  20.5 us
    ppermute x1, starting transfers between devices, on_device(): west = lax.ppermute(up, LON, [(i, (i + 1) % NLON) for i in range(NLON)])  20.5 us
    all_to_all x2, waiting for transfers between devices, sum_over(): return jnp.sum(lax.all_to_all(spread, axes, 0, 0), axis=0)  14.7 us
    ppermute x1, waiting for transfers between devices, on_device(): west = lax.ppermute(up, LON, [(i, (i + 1) % NLON) for i in range(NLON)])  14 us
    ppermute x1, starting transfers between devices, on_device(): got_a = lax.ppermute(send_a, LAT, [(0, 1), (1, 0), (2, 3), (3, 2)])  7.86 us
    another operation x1, local copies, waits for them, and re-layouts, on_device(): jnp.stack([jnp.sum(basis[i] * basis[j]) for i in range(4) for j in range(...  6.35 us
  transfers between devices with their start and end apart: 6, of which 4 were waited for; matrix products, arithmetic and copies ran while one was open for 4% of the time, Pallas kernels for 0%

profile of v1, /device:TPU:1, one launch (start us, length us, event | category | flops | bytes accessed | tf_op | source)
XLA Modules:
  0.0 171.7 jit_solution(17224729902398848789)
XLA Ops:
  0.6 0.7 broadcast_compare_fusion.2
  1.4 0.8 sqrt_multiply_fusion
  2.2 1.6 fusion.20
  3.9 0.2 concatenate.71
  4.1 24.3 %collective-permute-start.193 = (f32[60,384]{1,0:T(8,128)S(1)}, f32[60,384]{1,0:T(8,128)S(1)}, u32[]{:S(2)}, u32[]{:S(2)}) collective-permute-start(f32[60,384]{1,0:T(8,128)S(1)} %concatenate.71), channel_id=1, source_target_pairs={{4,0},{8,4},{12,8},{16,12},{20,16},{24,20},{28,24},{32,28},{36,32}... | collective-permute-start | bytes 276488 | tf_op jit(solution)/shard_map/ppermute | solution.py:117
  28.5 0.2 concatenate.68
  28.7 20.5 %collective-permute-start.192 = (f32[69,384]{1,0:T(8,128)S(1)}, f32[69,384]{1,0:T(8,128)S(1)}, u32[]{:S(2)}, u32[]{:S(2)}) collective-permute-start(f32[69,384]{1,0:T(8,128)S(1)} %concatenate.68), channel_id=1, source_target_pairs={{0,4},{4,8},{8,12},{12,16},{16,20},{20,24},{24,28},{28,32},{32,36}... | collective-permute-start | bytes 317960 | tf_op jit(solution)/shard_map/ppermute | solution.py:116
  49.2 0.6 copy-done.2
  50.0 0.1 fusion.45
  50.1 0.1 copy.74
  50.2 0.1 reshape_squeeze.9
  50.3 0.1 copy.77
  50.5 0.1 reshape_squeeze.10
  50.5 0.1 fusion.22
  50.6 0.2 copy.73
  50.8 0.1 reshape.107
  50.9 0.1 rev.4
  51.0 0.2 copy.76
  51.2 0.1 reshape.109
  51.3 0.2 copy.79
  51.4 0.1 reshape.111
  51.6 14.0 %collective-permute-done.192 = f32[69,384]{1,0:T(8,128)S(1)} collective-permute-done((f32[69,384]{1,0:T(8,128)S(1)}, f32[69,384]{1,0:T(8,128)S(1)}, u32[]{:S(2)}, u32[]{:S(2)}) %collective-permute-start.192) | collective-permute-done | bytes 106016 | tf_op jit(solution)/shard_map/ppermute | solution.py:116
  65.8 0.1 maximum_bitcast_fusion.1
  65.9 0.1 maximum_bitcast_fusion
  66.0 0.1 copy.75
  66.1 0.1 copy.78
  66.2 7.9 %collective-permute-start.194 = (f32[23,128]{1,0:T(8,128)S(1)}, f32[23,128]{1,0:T(8,128)S(1)}, u32[]{:S(2)}, u32[]{:S(2)}) collective-permute-start(f32[23,128]{1,0:T(8,128)S(1)} %get-tuple-element.442), channel_id=1, source_target_pairs={{0,1},{1,0},{2,3},{3,2},{4,5},{5,4},{6,7},{7,6},{8,9},{9,8},{10,11... | collective-permute-start | bytes 35336 | tf_op jit(solution)/shard_map/ppermute | solution.py:145
  74.2 0.9 add_multiply_fusion.1
  75.0 23.8 %conditional.1 = (f32[23,128]{1,0:T(8,128)}) conditional(s32[]{:T(128)} %clamp.3, f32[23,128]{1,0:T(8,128)S(1)} %get-tuple-element.443, f32[23,128]{1,0:T(8,128)S(1)} %get-tuple-element.443, f32[23,128]{1,0:T(8,128)S(1)} %get-tuple-element.443, f32[23,128]{1,0:T(8,128)S(1)} %get-tuple-element.443, ...), branch_computations={%region_2.3_spmd, %region_3.4_spmd, %region_4.5_spmd, %region_5.6_... | conditional | bytes 47152 | solution.py:154
  75.3 20.5 %collective-permute-start.166 = (f32[23,128]{1,0:T(8,128)S(1)}, f32[23,128]{1,0:T(8,128)}, u32[]{:S(2)}, u32[]{:S(2)}) collective-permute-start(f32[23,128]{1,0:T(8,128)S(1)} %param.166), channel_id=1, source_target_pairs={{1,2},{2,1},{3,667},{5,6},{6,5},{7,663},{9,10},{10,9},{11,659},{13... | collective-permute-start | bytes 35336 | tf_op jit(solution)/shard_map/cond/branch_166_fun/ppermute | solution.py:152
  95.7 3.1 %collective-permute-done.166 = f32[23,128]{1,0:T(8,128)} collective-permute-done((f32[23,128]{1,0:T(8,128)S(1)}, f32[23,128]{1,0:T(8,128)}, u32[]{:S(2)}, u32[]{:S(2)}) %collective-permute-start.166) | collective-permute-done | bytes 11808 | tf_op jit(solution)/shard_map/cond/branch_166_fun/ppermute | solution.py:152
  98.8 0.7 broadcast_select_fusion.1
  99.6 0.1 reshape_squeeze.11
  99.7 0.1 copy.80
  99.8 0.1 broadcast_compare_fusion
  99.9 0.1 pad_maximum_fusion.3
  100.1 0.1 copy.85
  100.2 0.1 copy.86
  100.3 0.1 pad_maximum_fusion.5
  100.5 0.1 slice_bitcast_fusion
  100.6 0.1 fusion.39
  100.7 0.1 reshape.112
  100.8 0.1 reshape.113
  100.8 0.1 broadcast_multiply_fusion
  100.9 0.1 fusion.32
  101.0 0.1 fusion.38
  101.2 0.1 slice_subtract_fusion.2
  101.3 0.8 multiply_reduce_fusion.1
  102.1 6.3 %stack.75 = f32[10]{0:T(128)S(1)} concatenate(f32[1]{0:T(128)} %bitcast.25, f32[1]{0:T(128)} %bitcast.27, f32[1]{0:T(128)} %bitcast.28, f32[1]{0:T(128)} %bitcast.29, f32[1]{0:T(128)} %bitcast.30, f32[1]{0:T(128)} %bitcast.31, f32[1]{0:T(128)} %bitcast.32, f32[1]{0:T(128)} %bitcast.33, f32[1]{0:T(128)} %bitcast.34, f32[1]{0:T(128)} %bitcast.35), dimensions={0} | concatenate | bytes 80 | tf_op jit(solution)/shard_map/stack | solution.py:185
  108.4 0.6 broadcast_in_dim.76
  109.0 12.2 %all-to-all-start = ((f32[12,1,128]{2,1,0:T(1,128)}), f32[12,1,128]{2,1,0:T(1,128)S(1)}, u32[]{:S(2)}, u32[]{:S(2)}) async-start(f32[12,1,128]{2,1,0:T(1,128)} %broadcast_in_dim.76), calls=%async_computation | async-start | bytes 12288 | tf_op jit(solution)/shard_map/all_to_all | solution.py:44
  121.2 0.2 copy.82
  121.4 0.2 copy.81
  121.6 0.2 maximum_maximum_fusion
  121.8 1.2 add_multiply_fusion
  123.0 0.2 fusion.16
  123.2 6.8 %all-to-all-done = f32[12,1,128]{2,1,0:T(1,128)S(1)} async-done(((f32[12,1,128]{2,1,0:T(1,128)}), f32[12,1,128]{2,1,0:T(1,128)S(1)}, u32[]{:S(2)}, u32[]{:S(2)}) %all-to-all-start) | async-done | bytes 6176 | tf_op jit(solution)/shard_map/all_to_all | solution.py:44
  130.1 0.6 broadcast_in_dim.77
  130.7 10.6 %all-to-all-start.1 = ((f32[64,1,128]{2,1,0:T(1,128)}), f32[64,1,128]{2,1,0:T(1,128)S(1)}, u32[]{:S(2)}, u32[]{:S(2)}) async-start(f32[64,1,128]{2,1,0:T(1,128)} %broadcast_in_dim.77), calls=%async_computation.1 | async-start | bytes 65536 | tf_op jit(solution)/shard_map/all_to_all | solution.py:44
  141.3 0.7 copy.96
  142.0 0.7 copy.97
  142.7 7.9 %all-to-all-done.1 = f32[64,1,128]{2,1,0:T(1,128)S(1)} async-done(((f32[64,1,128]{2,1,0:T(1,128)}), f32[64,1,128]{2,1,0:T(1,128)S(1)}, u32[]{:S(2)}, u32[]{:S(2)}) %all-to-all-start.1) | async-done | bytes 32800 | tf_op jit(solution)/shard_map/all_to_all | solution.py:44
  150.7 0.7 fusion.51
  171.0 0.7 multiply_add_fusion
  (43 shorter events, 0.6 us)
Async XLA Ops:
  0.6 0.8 copy-start
  2.2 1.6 copy-start.1
  4.1 47.5 %collective-permute-start.193 = (f32[60,384]{1,0:T(8,128)S(1)}, f32[60,384]{1,0:T(8,128)S(1)}, u32[]{:S(2)}, u32[]{:S(2)}) collective-permute-start(f32[60,384]{1,0:T(8,128)S(1)} %concatenate.71), channel_id=1, source_target_pairs={{4,0},{8,4},{12,8},{16,12},{20,16},{24,20},{28,24},{32,28},{36,32}... | collective-permute-start | bytes 276488 | tf_op jit(solution)/shard_map/ppermute | solution.py:117
  28.7 37.0 %collective-permute-start.192 = (f32[69,384]{1,0:T(8,128)S(1)}, f32[69,384]{1,0:T(8,128)S(1)}, u32[]{:S(2)}, u32[]{:S(2)}) collective-permute-start(f32[69,384]{1,0:T(8,128)S(1)} %concatenate.68), channel_id=1, source_target_pairs={{0,4},{4,8},{8,12},{12,16},{16,20},{20,24},{24,28},{28,32},{32,36}... | collective-permute-start | bytes 317960 | tf_op jit(solution)/shard_map/ppermute | solution.py:116
  49.2 0.7 copy-start.2
  66.2 32.6 %collective-permute-start.194 = (f32[23,128]{1,0:T(8,128)S(1)}, f32[23,128]{1,0:T(8,128)S(1)}, u32[]{:S(2)}, u32[]{:S(2)}) collective-permute-start(f32[23,128]{1,0:T(8,128)S(1)} %get-tuple-element.442), channel_id=1, source_target_pairs={{0,1},{1,0},{2,3},{3,2},{4,5},{5,4},{6,7},{7,6},{8,9},{9,8},{10,11... | collective-permute-start | bytes 35336 | tf_op jit(solution)/shard_map/ppermute | solution.py:145
  75.3 23.6 %collective-permute-start.166 = (f32[23,128]{1,0:T(8,128)S(1)}, f32[23,128]{1,0:T(8,128)}, u32[]{:S(2)}, u32[]{:S(2)}) collective-permute-start(f32[23,128]{1,0:T(8,128)S(1)} %param.166), channel_id=1, source_target_pairs={{1,2},{2,1},{3,667},{5,6},{6,5},{7,663},{9,10},{10,9},{11,659},{13... | collective-permute-start | bytes 35336 | tf_op jit(solution)/shard_map/cond/branch_166_fun/ppermute | solution.py:152
  109.0 21.0 %all-to-all-start = ((f32[12,1,128]{2,1,0:T(1,128)}), f32[12,1,128]{2,1,0:T(1,128)S(1)}, u32[]{:S(2)}, u32[]{:S(2)}) async-start(f32[12,1,128]{2,1,0:T(1,128)} %broadcast_in_dim.76), calls=%async_computation | async-start | bytes 12288 | tf_op jit(solution)/shard_map/all_to_all | solution.py:44
  130.7 19.9 %all-to-all-start.1 = ((f32[64,1,128]{2,1,0:T(1,128)}), f32[64,1,128]{2,1,0:T(1,128)S(1)}, u32[]{:S(2)}, u32[]{:S(2)}) async-start(f32[64,1,128]{2,1,0:T(1,128)} %broadcast_in_dim.77), calls=%async_computation.1 | async-start | bytes 65536 | tf_op jit(solution)/shard_map/all_to_all | solution.py:44

commit v2 on v1

v2 whole, which is shorter than its diff:
```python
import jax
import jax.numpy as jnp
from jax import lax
from jax.experimental import pallas as pl
from jax.experimental.pallas import tpu as pltpu
from jax.sharding import Mesh, PartitionSpec as P

ITERS = 3
LON = ("y", "xh", "z")
LAT = ("xl", "core")
ALL = LON + LAT
SIZES = (8, 2, 12, 2, 2)
SHIFT = 17.0
SCALE = 16.0
PAIRS = [(i, j) for i in range(4) for j in range(i, 4)]


def weno_upwind(a, b, c, d, e):
    d0, d1, d2, d3 = b - a, c - b, d - c, e - d
    s0, s1, s2 = d1 - d0, d2 - d1, d3 - d2
    t0 = s0 + 2.0 * d1
    t1 = d1 + d2
    t2 = s2 - 2.0 * d2
    k = 13.0 / 12.0
    e0 = 1e-06 + k * s0 * s0 + 0.25 * t0 * t0
    e1 = 1e-06 + k * s1 * s1 + 0.25 * t1 * t1
    e2 = 1e-06 + k * s2 * s2 + 0.25 * t2 * t2
    w0, w1, w2 = e1 * e2, e0 * e2, e0 * e1
    w0, w1, w2 = 0.1 * w0 * w0, 0.6 * w1 * w1, 0.3 * w2 * w2
    top = w0 * (5.0 * d1 - 2.0 * d0) + w1 * (d1 + 2.0 * d2) + w2 * (4.0 * d2 - d3)
    return c + top / (6.0 * (w0 + w1 + w2))


def face_flux(padded, speed, count, axis):
    q = [lax.slice_in_dim(padded, o, o + count, axis=axis) for o in range(6)]
    pos = speed > 0.0
    a, b, c, d, e = (jnp.where(pos, q[i], q[5 - i]) for i in range(5))
    return speed * weno_upwind(a, b, c, d, e)


def spread_to(value, axes, count):
    return lax.all_to_all(jnp.broadcast_to(value[None], (count,) + value.shape), axes, 0, 0)


def coefficients(gram):
    def form(p, q):
        total = 0.0
        for i in range(4):
            for j in range(4):
                if p[i] is not None and q[j] is not None:
                    total = total + p[i] * q[j] * gram[min(i, j), max(i, j)]
        return total

    def add(p, s, q):
        return [
            (p[i] if q[i] is None else (s * q[i] if p[i] is None else p[i] + s * q[i]))
            for i in range(4)
        ]

    def image(p):
        out = [None] * 4

        def put(i, x):
            out[i] = x if out[i] is None else out[i] + x

        for i in range(3):
            if p[i] is None:
                continue
            put(i, SHIFT * p[i])
            if i == 0:
                put(1, SCALE * p[0])
            else:
                put(i + 1, 0.5 * SCALE * p[i])
                put(i - 1, 0.5 * SCALE * p[i])
        return out

    x = [None] * 4
    r = [jnp.ones_like(gram[0, 0]), None, None, None]
    p = list(r)
    norm = form(r, r)
    for it in range(ITERS):
        ap = image(p)
        step = norm / form(p, ap)
        x = add(x, step, p)
        r = add(r, -step, ap)
        if it + 1 < ITERS:
            new = form(r, r)
            p = add(r, new / norm, p)
            norm = new
    return x, r


def krylov_kernel(full_ref, basis_ref, sums_ref):
    ni, nj = basis_ref.shape[1:]
    part, em, nm, cpl = (full_ref[k] for k in range(4))
    rows, lanes = part.shape
    b0 = part + pltpu.roll(em, 1, 0) + pltpu.roll(nm, 1, 1)

    def scaled(e):
        f = cpl * e
        lap = (
            4.0 * f
            - pltpu.roll(f, 1, 0)
            - pltpu.roll(f, rows - 1, 0)
            - pltpu.roll(f, 1, 1)
            - pltpu.roll(f, lanes - 1, 1)
        )
        return ((1.0 - SHIFT) * e + cpl * lap) * (1.0 / SCALE)

    b1 = scaled(b0)
    b2 = 2.0 * scaled(b1) - b0
    b3 = 2.0 * scaled(b2) - b1
    basis = [b[8 : 8 + ni, :nj] for b in (b0, b1, b2, b3)]
    for k in range(4):
        basis_ref[k] = basis[k]
    row = lax.broadcasted_iota(jnp.int32, (8, 128), 0)
    col = lax.broadcasted_iota(jnp.int32, (8, 128), 1)
    total = jnp.zeros((8, 128), jnp.float32)
    for n, (i, j) in enumerate(PAIRS):
        prod = basis[i] * basis[j]
        prod = prod[:8] + prod[8:]
        acc = prod[:, :128]
        for k in range(1, nj // 128):
            acc = acc + prod[:, 128 * k : 128 * (k + 1)]
        one = jnp.sum(jnp.sum(acc, axis=0, keepdims=True), axis=1, keepdims=True)
        total = total + jnp.where((row == 6) & (col == n), one, 0.0)
    sums_ref[...] = total


def finish_kernel(basis_ref, sums_ref, surface_ref, residual_ref):
    total = sums_ref[0]
    for k in range(1, sums_ref.shape[0]):
        total = total + sums_ref[k]
    row = lax.broadcasted_iota(jnp.int32, (8, 128), 0)
    col = lax.broadcasted_iota(jnp.int32, (8, 128), 1)
    gram = {}
    for n, pair in enumerate(PAIRS):
        cell = jnp.where((row == 6) & (col == n), total, 0.0)
        gram[pair] = jnp.sum(jnp.sum(cell, axis=0, keepdims=True), axis=1, keepdims=True)
    xc, rc = coefficients(gram)
    basis = [basis_ref[k] for k in range(4)]
    surface_ref[...] = sum(c * f for c, f in zip(xc, basis) if c is not None)
    residual_ref[...] = sum(c * f for c, f in zip(rc, basis) if c is not None)


def make_on_device(sizes):
    ny, nxh, nz, nxl, ncore = sizes
    n_lon, n_lat = ny * nxh * nz, nxl * ncore

    def on_device(t, s, u, v, elev, flag, depth, fc):
        nl, ni, nj = t.shape
        lat = lax.axis_index(LAT)
        lon = lax.axis_index(LON)
        last = lat == n_lat - 1
        level = lax.broadcasted_iota(jnp.int32, t.shape, 0)
        mask = jnp.where((flag[None] == 1) & (level < depth[None]), 1.0, 0.0).astype(jnp.float32)
        q = jnp.stack([t * mask, s * mask])
        ue = u * mask
        vn = v * mask
        em = jnp.sum(ue, axis=0) / nl
        nm = jnp.sum(vn, axis=0) / nl
        coupler = 2.0 * jnp.sqrt((depth * flag).astype(jnp.float32) / nl)
        part = elev - em - nm

        up = jnp.concatenate(
            [
                q[:, :, ni - 3 :].reshape(6 * nl, nj),
                ue[:, ni - 1],
                part[ni - 3 :],
                em[ni - 4 :],
                nm[ni - 3 :],
                coupler[ni - 3 :],
            ]
        )
        down = jnp.concatenate(
            [q[:, :, :3].reshape(6 * nl, nj), part[:3], em[:3], nm[:3], coupler[:3]]
        )
        west = lax.ppermute(up, LON, [(i, (i + 1) % n_lon) for i in range(n_lon)])
        east = lax.ppermute(down, LON, [((i + 1) % n_lon, i) for i in range(n_lon)])
        n6 = 6 * nl
        q_west, q_east = west[:n6].reshape(2, nl, 3, nj), east[:n6].reshape(2, nl, 3, nj)
        u_west = west[n6 : n6 + nl]
        cw, ce = west[n6 + nl :], east[n6:]

        def blank(n):
            return jnp.zeros((n, nj), jnp.float32)

        fields = jnp.stack(
            [
                jnp.concatenate([blank(5), cw[0:3], part, ce[0:3], blank(5)]),
                jnp.concatenate([blank(4), cw[3:7], em, ce[3:6], blank(5)]),
                jnp.concatenate([blank(5), cw[7:10], nm, ce[6:9], blank(5)]),
                jnp.concatenate([blank(5), cw[10:13], coupler, ce[9:12], blank(5)]),
            ]
        )

        rows = fields.shape[1]

        def edge(qpart, vcol, fpart):
            a = jnp.transpose(qpart, (0, 3, 1, 2)).reshape(6, nl * ni)
            b = vcol.reshape(1, nl * ni)
            c = jnp.transpose(fpart, (2, 0, 1)).reshape(4, 4 * rows)
            return jnp.concatenate([a, b, jnp.zeros_like(b), c, jnp.zeros_like(c)])

        to_north = edge(q[..., nj - 3 :], vn[..., nj - 1], fields[..., nj - 4 :])
        to_south = edge(q[..., :3], vn[..., 0], fields[..., :4])
        slot = lax.broadcasted_iota(jnp.int32, (n_lat, 1, 1), 0)
        got = lax.all_to_all(
            jnp.where(slot > lat, to_north[None], to_south[None]), LAT, 0, 0
        )
        north = jnp.where(
            last, 0.0, lax.dynamic_index_in_dim(got, jnp.minimum(lat + 1, n_lat - 1), 0, False)
        )
        south = jnp.where(
            lat == 0, 0.0, lax.dynamic_index_in_dim(got, jnp.maximum(lat - 1, 0), 0, False)
        )

        def columns(msg):
            return jnp.transpose(msg[:6].reshape(2, 3, nl, ni), (0, 2, 3, 1))

        q_north, q_south = columns(north), columns(south)
        v_south = south[6].reshape(nl, ni, 1)

        def fcols(msg):
            return jnp.transpose(msg[8:12].reshape(4, 4, rows), (1, 2, 0))

        full = jnp.concatenate(
            [fields, fcols(north), jnp.zeros((4, rows, 120), jnp.float32), fcols(south)], axis=2
        )
        basis, sums = pl.pallas_call(
            krylov_kernel,
            out_shape=(
                jax.ShapeDtypeStruct((4, ni, nj), jnp.float32),
                jax.ShapeDtypeStruct((8, 128), jnp.float32),
            ),
            name="krylov",
        )(full)

        fold = jnp.transpose(jnp.flip(q[..., nj - 3 :], axis=(2, 3)), (0, 3, 1, 2)).reshape(6, nl * ni)
        source = jnp.mod(fc[0] // ni, n_lon)
        sums = jnp.sum(spread_to(sums[6:7], LAT, n_lat), axis=0)
        tail = jnp.zeros((1, 128), jnp.float32)
        got = spread_to(jnp.concatenate([fold, sums, tail]), "z", nz)
        fold = lax.dynamic_index_in_dim(got, source % nz, 0, False)[:6]
        sums = jnp.sum(got[:, 6:7], axis=0)
        got = spread_to(jnp.concatenate([fold, sums, tail]), ("y", "xh"), ny * nxh)
        fold = lax.dynamic_index_in_dim(got, source // nz, 0, False)[:6].reshape(2, 3, nl * ni)
        surface, residual = pl.pallas_call(
            finish_kernel,
            out_shape=(jax.ShapeDtypeStruct((ni, nj), jnp.float32),) * 2,
            name="finish",
        )(basis, got)

        zonal = jnp.concatenate([q_west, q, q_east], axis=2)
        merid = jnp.concatenate([q_south, q, q_north], axis=3)
        speed_x = jnp.concatenate([u_west[:, None], ue], axis=1)
        place = lax.broadcasted_iota(jnp.int32, (1, 1, nj + 1), 2)
        speed_y = jnp.concatenate([v_south, vn], axis=2)
        speed_y = jnp.where(last & (place > nj - 3), 0.0, speed_y)
        flux_x = face_flux(zonal, speed_x[None], ni + 1, 2)
        flux_y = face_flux(merid, speed_y[None], nj + 1, 3)
        updated = q - (flux_x[:, :, 1:] - flux_x[:, :, :-1]) - (flux_y[..., 1:] - flux_y[..., :-1])
        own = jnp.transpose(q[..., nj - 5 :], (0, 3, 1, 2)).reshape(2, 5, nl * ni)
        speed = jnp.transpose(vn[..., nj - 3 :], (2, 0, 1)).reshape(1, 3, nl * ni)
        beyond = face_flux(jnp.concatenate([own, fold], axis=1), jnp.where(last, speed, 0.0), 3, 1)
        change = jnp.concatenate([beyond[:, :1], beyond[:, 1:] - beyond[:, :-1]], axis=1)
        change = jnp.transpose(change.reshape(2, 3, nl, ni), (0, 2, 3, 1))
        updated = (updated - jnp.pad(change, ((0, 0), (0, 0), (0, 0), (nj - 3, 0)))) * mask
        return updated[0], updated[1], surface, residual

    return on_device


def solution(mesh, sizes=SIZES):
    fine = Mesh(mesh.devices.reshape(sizes), ALL)
    block, plane = P(None, LON, LAT), P(LON, LAT)
    return jax.shard_map(
        make_on_device(sizes),
        mesh=fine,
        in_specs=(block,) * 4 + (plane,) * 3 + (P(LON),),
        out_specs=(block, block, plane, plane),
        check_vma=False,
    )
```

time: 173 us -> 90.5 us (0.52)
  starting transfers between devices: 95.9 us -> 39.1 us
  between operations: 20.9 us -> 1.29 us
  local copies, waits for them, and re-layouts: 13.6 us -> 9.12 us
  waiting for transfers between devices: 31.8 us -> 28.1 us
  Pallas kernels: 0 us -> 3.67 us
    ppermute x4 -> x2, starting transfers between devices: 73.1 us -> 22.4 us  [the longest x1 20.5 us: on_device(): east = lax.ppermute(down, LON, [((i + 1) % n_lon, i) for i in range(n_lon)])]
    ppermute x4 -> x2, waiting for transfers between devices: 17.1 us -> 5.99 us  [the longest x1 5.99 us: on_device(): west = lax.ppermute(up, LON, [(i, (i + 1) % n_lon) for i in range(n_lon)])]
    all_to_all x2 -> x4, waiting for transfers between devices: 14.7 us -> 22.1 us  [the longest x3 19.8 us: spread_to(): lax.all_to_all(jnp.broadcast_to(value[None], (count,) + value.shape), axe...]
    another operation x3, local copies, waits for them, and re-layouts: 6.56 us -> 0.01 us  [the longest x1 6.35 us: on_device(): jnp.stack([jnp.sum(basis[i] * basis[j]) for i in range(4) for j in range(...]
    all_to_all x2 -> x4, starting transfers between devices: 22.7 us -> 16.7 us  [the longest x3 11.4 us: spread_to(): lax.all_to_all(jnp.broadcast_to(value[None], (count,) + value.shape), axe...]
    pallas_call x0 -> x2, Pallas kernels: none -> 3.67 us  [the longest x1 1.97 us: on_device(): pl.pallas_call(krylov_kernel, out_shape=(jax.ShapeDtypeStruct((4, ni, nj)...]
    slice x8, local copies, waits for them, and re-layouts: 2.17 us -> 0.25 us  [the longest x4 0.23 us: fcols(): return jnp.transpose(msg[8:12].reshape(4, 4, rows), (1, 2, 0))]
  transfers between devices with their start and end apart: 6 -> 6, of which waited for: 4 -> 5; matrix products, arithmetic and copies ran while one was open for 4% -> 6% of each run, Pallas kernels for 0% -> 0%
where the time goes in v2:
time: 90.5 us; the launch traced here: 89.2 us
  starting transfers between devices  39.1 us (43%)
  waiting for transfers between devices  28.1 us (31%)
  local copies, waits for them, and re-layouts  9.12 us (10%)
  other arithmetic  7.92 us (9%)
  Pallas kernels  3.67 us (4%)
  between operations  1.29 us (1%)
    ppermute x1, starting transfers between devices, on_device(): east = lax.ppermute(down, LON, [((i + 1) % n_lon, i) for i in range(n_lon)])  20.5 us
    all_to_all x3, waiting for transfers between devices, spread_to(): lax.all_to_all(jnp.broadcast_to(value[None], (count,) + value.shape), axe...  19.8 us
    all_to_all x3, starting transfers between devices, spread_to(): lax.all_to_all(jnp.broadcast_to(value[None], (count,) + value.shape), axe...  11.4 us
    ppermute x1, waiting for transfers between devices, on_device(): west = lax.ppermute(up, LON, [(i, (i + 1) % n_lon) for i in range(n_lon)])  5.99 us
    all_to_all x1, starting transfers between devices, on_device(): lax.all_to_all(jnp.where(slot > lat, to_north[None], to_south[None]), LAT...  5.34 us
    broadcast_in_dim x4, local copies, waits for them, and re-layouts, spread_to(): jnp.broadcast_to(value[None], (count,) + value.shape)  2.53 us
    unnamed x11, local copies, waits for them, and re-layouts  2.35 us
    all_to_all x1, waiting for transfers between devices, on_device(): lax.all_to_all(jnp.where(slot > lat, to_north[None], to_south[None]), LAT...  2.24 us
  transfers between devices with their start and end apart: 6, of which 5 were waited for; matrix products, arithmetic and copies ran while one was open for 6% of the time, Pallas kernels for 0%

profile of v2, /device:TPU:1, one launch (start us, length us, event | category | flops | bytes accessed | tf_op | source)
XLA Modules:
  0.0 89.2 jit_solution(9614884328161214659)
XLA Ops:
  0.6 0.7 broadcast_compare_fusion.2
  1.4 0.8 sqrt_multiply_fusion
  2.2 1.6 %fusion.21 = (f32[8,16,384]{2,0,1:T(8,128)S(1)}, f32[1,8,16,384]{3,1,2,0:T(8,128)S(1)}, f32[1,8,16,384]{3,1,2,0:T(8,128)S(1)}, f32[16,384]{1,0:T(8,128)S(1)}, f3...) fusion(s32[16,384]{1,0:T(8,128)S(1)} %copy-done.1, ...), kind=kLoop, calls=%fused_computation.72 | loop fusion | flops 430080 | bytes 1849344 | tf_op jit(solution)/shard_map/jit(_where)/select_n | solution.py:156
  3.9 0.2 concatenate.83
  4.1 20.5 %collective-permute-start.1 = (f32[60,384]{1,0:T(8,128)S(1)}, f32[60,384]{1,0:T(8,128)S(1)}, u32[]{:S(2)}, u32[]{:S(2)}) collective-permute-start(f32[60,384]{1,0:T(8,128)S(1)} %concatenate.83), channel_id=1, source_target_pairs={{4,0},{8,4},{12,8},{16,12},{20,16},{24,20},{28,24},{32,28},{36,32}... | collective-permute-start | bytes 276488 | tf_op jit(solution)/shard_map/ppermute | solution.py:179
  24.7 0.2 concatenate.80
  24.8 1.9 %collective-permute-start = (f32[69,384]{1,0:T(8,128)S(1)}, f32[69,384]{1,0:T(8,128)S(1)}, u32[]{:S(2)}, u32[]{:S(2)}) collective-permute-start(f32[69,384]{1,0:T(8,128)S(1)} %concatenate.80), channel_id=1, source_target_pairs={{0,4},{4,8},{8,12},{12,16},{16,20},{20,24},{24,28},{28,32},{32,36}... | collective-permute-start | bytes 317960 | tf_op jit(solution)/shard_map/ppermute | solution.py:178
  26.8 0.6 copy-done.3
  27.6 0.1 fusion.26
  27.7 0.1 fusion.22
  27.9 0.1 fusion.40
  28.0 0.1 fusion.29
  28.1 0.1 copy.98
  28.2 0.1 select_n.161
  28.3 0.2 copy.99
  28.4 0.1 reshape.177
  28.6 0.1 copy.90
  28.7 0.1 reshape_squeeze.7
  28.8 0.1 copy.93
  28.9 0.1 reshape_squeeze.8
  29.0 0.2 copy.92
  29.2 0.1 reshape.173
  29.3 0.1 rev.4
  29.4 0.2 copy.89
  29.5 0.1 reshape.171
  29.6 0.2 copy.100
  29.8 0.1 reshape.178
  29.9 0.1 pad.18.clone
  30.1 6.0 %collective-permute-done = f32[69,384]{1,0:T(8,128)S(1)} collective-permute-done((f32[69,384]{1,0:T(8,128)S(1)}, f32[69,384]{1,0:T(8,128)S(1)}, u32[]{:S(2)}, u32[]{:S(2)}) %collective-permute-start) | collective-permute-done | bytes 106016 | tf_op jit(solution)/shard_map/ppermute | solution.py:178
  36.4 0.1 pad_maximum_fusion.8
  36.5 0.1 copy.94
  36.7 0.7 broadcast_select_fusion
  37.4 5.3 %all-to-all-start = ((f32[4,16,128]{2,1,0:T(8,128)}), f32[4,16,128]{2,1,0:T(8,128)S(1)}, u32[]{:S(2)}, u32[]{:S(2)}) async-start(f32[4,16,128]{2,1,0:T(8,128)} %broadcast_select_fusion), calls=%async_computation | async-start | bytes 65536 | tf_op jit(solution)/shard_map/all_to_all | solution.py:208
  42.8 0.9 add_multiply_fusion.1
  43.7 2.2 %all-to-all-done = f32[4,16,128]{2,1,0:T(8,128)S(1)} async-done(((f32[4,16,128]{2,1,0:T(8,128)}), f32[4,16,128]{2,1,0:T(8,128)S(1)}, u32[]{:S(2)}, u32[]{:S(2)}) %all-to-all-start) | async-done | bytes 32800 | tf_op jit(solution)/shard_map/all_to_all | solution.py:208
  46.0 0.1 concatenate.91
  46.0 0.1 copy.95
  46.2 0.1 copy.102
  46.3 0.1 copy.101
  46.4 0.8 pad_maximum_fusion.3.full_ref
  47.2 2.0 %krylov.1 = (f32[4,16,384]{2,1,0:T(8,128)}, f32[8,128]{1,0:T(8,128)}) custom-call(f32[4,32,512]{2,1,0:T(8,128)} %pad_maximum_fusion.3.full_ref), custom_call_target="tpu_custom_call" | custom-call | tf_op jit(solution)/shard_map/krylov/pallas_call | solution.py:230
  49.2 0.7 slice_bitcast_fusion.5
  49.9 0.6 broadcast_in_dim.168
  50.4 4.0 %all-to-all-start.1 = ((f32[4,1,128]{2,1,0:T(1,128)}), f32[4,1,128]{2,1,0:T(1,128)S(1)}, u32[]{:S(2)}, u32[]{:S(2)}) async-start(f32[4,1,128]{2,1,0:T(1,128)} %broadcast_in_dim.168), calls=%async_computation.1 | async-start | bytes 4096 | tf_op jit(solution)/shard_map/all_to_all | solution.py:42
  54.4 0.1 broadcast_compare_fusion
  54.6 0.1 reshape.175
  54.7 0.2 copy.97
  54.9 0.2 copy.96
  55.1 2.3 %all-to-all-done.1 = f32[4,1,128]{2,1,0:T(1,128)S(1)} async-done(((f32[4,1,128]{2,1,0:T(1,128)}), f32[4,1,128]{2,1,0:T(1,128)S(1)}, u32[]{:S(2)}, u32[]{:S(2)}) %all-to-all-start.1) | async-done | bytes 2080 | tf_op jit(solution)/shard_map/all_to_all | solution.py:42
  57.4 0.6 broadcast_in_dim.169
  58.1 3.5 %all-to-all-start.2 = ((f32[12,8,128]{2,1,0:T(8,128)}), f32[12,8,128]{2,1,0:T(8,128)S(1)}, u32[]{:S(2)}, u32[]{:S(2)}) async-start(f32[12,8,128]{2,1,0:T(8,128)} %broadcast_in_dim.169), calls=%async_computation.2 | async-start | bytes 98304 | tf_op jit(solution)/shard_map/all_to_all | solution.py:42
  61.6 0.2 maximum_maximum_fusion
  61.8 9.4 %all-to-all-done.2 = f32[12,8,128]{2,1,0:T(8,128)S(1)} async-done(((f32[12,8,128]{2,1,0:T(8,128)}), f32[12,8,128]{2,1,0:T(8,128)S(1)}, u32[]{:S(2)}, u32[]{:S(2)}) %all-to-all-start.2) | async-done | bytes 49184 | tf_op jit(solution)/shard_map/all_to_all | solution.py:42
  71.2 0.6 broadcast_in_dim.170
  71.8 3.9 %all-to-all-start.3 = ((f32[16,8,128]{2,1,0:T(8,128)}), f32[16,8,128]{2,1,0:T(8,128)S(1)}, u32[]{:S(2)}, u32[]{:S(2)}) async-start(f32[16,8,128]{2,1,0:T(8,128)} %broadcast_in_dim.170), calls=%async_computation.3 | async-start | bytes 131072 | tf_op jit(solution)/shard_map/all_to_all | solution.py:42
  75.8 1.2 %add_multiply_fusion = f32[2,8,16,385]{3,1,2,0:T(8,128)S(1)} fusion(f32[2,8,16,387]{3,1,2,0:T(8,128)S(1)} %get-tuple-element.39, f32[2,8,16,387]{3,1,2,0:T(8,128)S(1)} %get-tuple-element.38, f32[8,16,385]{2,0,1:T(8,128)S(1)} %get-tuple-element.29, pred[8,16,385]{2,0,1:T(8,128)(4,1)S(1)} %get-tuple-element.28), kind=kLoop, calls=%fused_computation.39 | loop fusion | flops 6012160 | bytes 3006080 | tf_op jit(solution)/shard_map/mul | solution.py:38
  77.0 8.2 %all-to-all-done.3.sums_ref = f32[16,8,128]{2,1,0:T(8,128)S(1)} async-done(((f32[16,8,128]{2,1,0:T(8,128)}), f32[16,8,128]{2,1,0:T(8,128)S(1)}, u32[]{:S(2)}, u32[]{:S(2)}) %all-to-all-start.3) | async-done | bytes 65568 | tf_op jit(solution)/shard_map/all_to_all | solution.py:42
  85.3 0.1 reshape.182
  85.3 0.2 copy.106
  85.5 0.3 copy-done
  85.8 0.2 fusion.17
  86.1 0.7 copy.108
  86.8 0.7 copy.107
  87.5 1.7 %finish.1 = (f32[16,384]{1,0:T(8,128)}, f32[16,384]{1,0:T(8,128)}) custom-call(f32[4,16,384]{2,1,0:T(8,128)} %get-tuple-element.9.basis_ref, f32[16,8,128]{2,1,0:T(8,128)} %copy-done), custom_call_target="tpu_custom_call" | custom-call | tf_op jit(solution)/shard_map/finish/pallas_call | solution.py:248
  (68 shorter events, 1.1 us)
Async XLA Ops:
  0.6 0.8 copy-start.1
  2.2 1.6 %copy-start.2 = (f32[16,384]{1,0:T(8,128)S(1)}, f32[16,384]{1,0:T(8,128)}, u32[]{:S(2)}) copy-start(f32[16,384]{1,0:T(8,128)} %param.12) | copy-start | bytes 73732
  4.1 25.9 %collective-permute-start.1 = (f32[60,384]{1,0:T(8,128)S(1)}, f32[60,384]{1,0:T(8,128)S(1)}, u32[]{:S(2)}, u32[]{:S(2)}) collective-permute-start(f32[60,384]{1,0:T(8,128)S(1)} %concatenate.83), channel_id=1, source_target_pairs={{4,0},{8,4},{12,8},{16,12},{20,16},{24,20},{28,24},{32,28},{36,32}... | collective-permute-start | bytes 276488 | tf_op jit(solution)/shard_map/ppermute | solution.py:179
  24.8 11.2 %collective-permute-start = (f32[69,384]{1,0:T(8,128)S(1)}, f32[69,384]{1,0:T(8,128)S(1)}, u32[]{:S(2)}, u32[]{:S(2)}) collective-permute-start(f32[69,384]{1,0:T(8,128)S(1)} %concatenate.80), channel_id=1, source_target_pairs={{0,4},{4,8},{8,12},{12,16},{16,20},{20,24},{24,28},{28,32},{32,36}... | collective-permute-start | bytes 317960 | tf_op jit(solution)/shard_map/ppermute | solution.py:178
  26.8 0.7 copy-start.3
  37.4 8.5 %all-to-all-start = ((f32[4,16,128]{2,1,0:T(8,128)}), f32[4,16,128]{2,1,0:T(8,128)S(1)}, u32[]{:S(2)}, u32[]{:S(2)}) async-start(f32[4,16,128]{2,1,0:T(8,128)} %broadcast_select_fusion), calls=%async_computation | async-start | bytes 65536 | tf_op jit(solution)/shard_map/all_to_all | solution.py:208
  50.4 7.0 %all-to-all-start.1 = ((f32[4,1,128]{2,1,0:T(1,128)}), f32[4,1,128]{2,1,0:T(1,128)S(1)}, u32[]{:S(2)}, u32[]{:S(2)}) async-start(f32[4,1,128]{2,1,0:T(1,128)} %broadcast_in_dim.168), calls=%async_computation.1 | async-start | bytes 4096 | tf_op jit(solution)/shard_map/all_to_all | solution.py:42
  58.1 13.1 %all-to-all-start.2 = ((f32[12,8,128]{2,1,0:T(8,128)}), f32[12,8,128]{2,1,0:T(8,128)S(1)}, u32[]{:S(2)}, u32[]{:S(2)}) async-start(f32[12,8,128]{2,1,0:T(8,128)} %broadcast_in_dim.169), calls=%async_computation.2 | async-start | bytes 98304 | tf_op jit(solution)/shard_map/all_to_all | solution.py:42
  71.8 13.3 %all-to-all-start.3 = ((f32[16,8,128]{2,1,0:T(8,128)}), f32[16,8,128]{2,1,0:T(8,128)S(1)}, u32[]{:S(2)}, u32[]{:S(2)}) async-start(f32[16,8,128]{2,1,0:T(8,128)} %broadcast_in_dim.170), calls=%async_computation.3 | async-start | bytes 131072 | tf_op jit(solution)/shard_map/all_to_all | solution.py:42
  85.2 0.6 copy-start

commit v3 on v2

v3 whole, which is shorter than its diff:
```python
import jax
import jax.numpy as jnp
from jax import lax
from jax.experimental import pallas as pl
from jax.experimental.pallas import tpu as pltpu
from jax.sharding import Mesh, PartitionSpec as P

ITERS = 3
LON = ("y", "xh", "z")
LAT = ("xl", "core")
ALL = LON + LAT
SIZES = (8, 2, 12, 2, 2)
SHIFT = 17.0
SCALE = 16.0
PAIRS = [(i, j) for i in range(4) for j in range(i, 4)]


def weno_upwind(a, b, c, d, e):
    d0, d1, d2, d3 = b - a, c - b, d - c, e - d
    s0, s1, s2 = d1 - d0, d2 - d1, d3 - d2
    t0 = s0 + 2.0 * d1
    t1 = d1 + d2
    t2 = s2 - 2.0 * d2
    k = 13.0 / 12.0
    e0 = 1e-06 + k * s0 * s0 + 0.25 * t0 * t0
    e1 = 1e-06 + k * s1 * s1 + 0.25 * t1 * t1
    e2 = 1e-06 + k * s2 * s2 + 0.25 * t2 * t2
    w0, w1, w2 = e1 * e2, e0 * e2, e0 * e1
    w0, w1, w2 = 0.1 * w0 * w0, 0.6 * w1 * w1, 0.3 * w2 * w2
    top = w0 * (5.0 * d1 - 2.0 * d0) + w1 * (d1 + 2.0 * d2) + w2 * (4.0 * d2 - d3)
    return c + top / (6.0 * (w0 + w1 + w2))


def face_flux(padded, speed, count, axis):
    q = [lax.slice_in_dim(padded, o, o + count, axis=axis) for o in range(6)]
    pos = speed > 0.0
    a, b, c, d, e = (jnp.where(pos, q[i], q[5 - i]) for i in range(5))
    return speed * weno_upwind(a, b, c, d, e)


def coefficients(gram):
    def form(p, q):
        total = 0.0
        for i in range(4):
            for j in range(4):
                if p[i] is not None and q[j] is not None:
                    total = total + p[i] * q[j] * gram[min(i, j), max(i, j)]
        return total

    def add(p, s, q):
        return [
            (p[i] if q[i] is None else (s * q[i] if p[i] is None else p[i] + s * q[i]))
            for i in range(4)
        ]

    def image(p):
        out = [None] * 4

        def put(i, x):
            out[i] = x if out[i] is None else out[i] + x

        for i in range(3):
            if p[i] is None:
                continue
            put(i, SHIFT * p[i])
            if i == 0:
                put(1, SCALE * p[0])
            else:
                put(i + 1, 0.5 * SCALE * p[i])
                put(i - 1, 0.5 * SCALE * p[i])
        return out

    x = [None] * 4
    r = [jnp.ones_like(gram[0, 0]), None, None, None]
    p = list(r)
    norm = form(r, r)
    for it in range(ITERS):
        ap = image(p)
        step = norm / form(p, ap)
        x = add(x, step, p)
        r = add(r, -step, ap)
        if it + 1 < ITERS:
            new = form(r, r)
            p = add(r, new / norm, p)
            norm = new
    return x, r


def lat_index():
    return 2 * lax.axis_index("xl") + lax.axis_index("core")


def mirror16(x):
    lane = lax.broadcasted_iota(jnp.int32, x.shape, 1)
    for bit in (1, 2, 4, 8):
        x = jnp.where((lane & bit) != 0, pltpu.roll(x, bit, 1), pltpu.roll(x, 128 - bit, 1))
    return x


def pack_kernel(t, s, u, v, elev, flag, depth, fc, up, down, fields, edges, source, tile):
    nl, ni, nj = t.shape
    ocean = flag[...] == 1
    wet = depth[...]
    lane = lax.broadcasted_iota(jnp.int32, (ni, 128), 1)
    em = jnp.zeros((ni, nj), jnp.float32)
    nm = jnp.zeros((ni, nj), jnp.float32)
    zero = jnp.zeros((8, nj), jnp.float32)
    for l in range(nl):
        m = jnp.where(ocean & (wet > l), 1.0, 0.0)
        tt, ss, uu, vv = t[l] * m, s[l] * m, u[l] * m, v[l] * m
        em = em + uu
        nm = nm + vv
        up[8 * l : 8 * l + 3] = tt[ni - 3 :]
        up[8 * l + 3 : 8 * l + 6] = ss[ni - 3 :]
        up[8 * l + 6 : 8 * l + 7] = uu[ni - 1 :]
        up[8 * l + 7 : 8 * l + 8] = zero[:1]
        down[8 * l : 8 * l + 3] = tt[:3]
        down[8 * l + 3 : 8 * l + 6] = ss[:3]
        down[8 * l + 6 : 8 * l + 8] = zero[:2]
        x = jnp.where(lane < 8, tt[:, :128], tt[:, nj - 128 :])
        x = jnp.where((lane >= 8) & (lane < 16), pltpu.roll(ss[:, :128], 8, 1), x)
        x = jnp.where((lane >= 112) & (lane < 120), pltpu.roll(ss[:, nj - 128 :], 120, 1), x)
        x = jnp.where((lane >= 104) & (lane < 112), pltpu.roll(vv[:, nj - 128 :], 112, 1), x)
        tile[ni * l : ni * (l + 1)] = x
    em = em / nl
    nm = nm / nl
    part = elev[...] - em - nm
    coupler = 2.0 * jnp.sqrt((wet * flag[...]).astype(jnp.float32) / nl)
    for k, f in enumerate((part, em, nm, coupler)):
        fields[k] = f
    up[64:67] = part[ni - 3 :]
    up[67:71] = em[ni - 4 :]
    up[71:74] = nm[ni - 3 :]
    up[74:77] = coupler[ni - 3 :]
    up[77:80] = zero[:3]
    down[64:67] = part[:3]
    down[67:70] = em[:3]
    down[70:73] = nm[:3]
    down[73:76] = coupler[:3]
    down[76:80] = zero[:4]
    turned = tile[...].T
    edges[0:16] = turned[0:16]
    edges[16:40] = turned[104:128]
    block = lax.shift_right_logical(jnp.broadcast_to(fc[0:1, 0:1], (8, 128)), 4)
    row = jnp.zeros((8, 128), jnp.int32)
    nz = lax.axis_size("z")
    for k in range(1, lax.axis_size("y") * lax.axis_size("xh")):
        row = row + jnp.where(block >= nz * k, 1, 0)
    source[0] = block - nz * row
    source[1] = row


def widen_kernel(west, east, fields, edges, wide, slots):
    _, ni, nj = fields.shape
    lat = lat_index()
    blank = jnp.zeros((8, nj), jnp.float32)
    spans = ((64, 67, 64, 67), (67, 71, 67, 70), (71, 74, 70, 73), (74, 77, 73, 76))
    for k, (w0, w1, e0, e1) in enumerate(spans):
        wide[k, 0:8] = blank
        wide[k, 24:32] = blank
        wide[k, 8 - (w1 - w0) : 8] = west[w0:w1]
        wide[k, 8 : 8 + ni] = fields[k]
        wide[k, 24 : 24 + (e1 - e0)] = east[e0:e1]
    lane = lax.broadcasted_iota(jnp.int32, (4, 32, 128), 2)
    both = jnp.where(lane < 64, wide[:, :, 0:128], wide[:, :, nj - 128 : nj])
    turned = both.reshape(128, 128).T
    none = jnp.zeros((4, 128), jnp.float32)
    fold = jnp.concatenate(
        [edges[k : k + 1] for k in (39, 38, 37, 31, 30, 29)] + [none[:2]], axis=0
    )
    fold = mirror16(fold)
    north = jnp.concatenate(
        [edges[37:40], edges[29:32], edges[23:24], none[:1]], axis=0
    )
    south = jnp.concatenate([edges[0:3], edges[8:11], none[:2]], axis=0)
    for p in range(4):
        ahead = p > lat
        slots[p, 0:8] = jnp.where(ahead, north, south)
        slots[p, 8:12] = jnp.where(ahead, turned[124:128], turned[0:4])
        slots[p, 12:14] = fold[2 * p : 2 * p + 2]
        slots[p, 14:16] = none[:2]


def krylov_kernel(wide, got, basis_ref, message, tile):
    ni, nj = basis_ref.shape[1:]
    lat = lat_index()
    tile[...] = jnp.zeros((128, 128), jnp.float32)
    tile[0:4] = jnp.where(lat < 3, got[jnp.minimum(lat + 1, 3), 8:12], 0.0)
    tile[124:128] = jnp.where(lat > 0, got[jnp.maximum(lat - 1, 0), 8:12], 0.0)
    beyond = tile[...].T.reshape(4, 32, 128)
    part, em, nm, cpl = (jnp.concatenate([wide[k], beyond[k]], axis=1) for k in range(4))
    rows, lanes = part.shape
    b0 = part + pltpu.roll(em, 1, 0) + pltpu.roll(nm, 1, 1)

    def scaled(e):
        f = cpl * e
        lap = (
            4.0 * f
            - pltpu.roll(f, 1, 0)
            - pltpu.roll(f, rows - 1, 0)
            - pltpu.roll(f, 1, 1)
            - pltpu.roll(f, lanes - 1, 1)
        )
        return ((1.0 - SHIFT) * e + cpl * lap) * (1.0 / SCALE)

    b1 = scaled(b0)
    b2 = 2.0 * scaled(b1) - b0
    b3 = 2.0 * scaled(b2) - b1
    basis = [b[8 : 8 + ni, :nj] for b in (b0, b1, b2, b3)]
    for k in range(4):
        basis_ref[k] = basis[k]
    row = lax.broadcasted_iota(jnp.int32, (4, 128), 0)
    col = lax.broadcasted_iota(jnp.int32, (4, 128), 1)
    total = jnp.concatenate([got[3, 12:14], jnp.zeros((2, 128), jnp.float32)], axis=0)
    for n, (i, j) in enumerate(PAIRS):
        prod = basis[i] * basis[j]
        prod = prod[:8] + prod[8:]
        acc = prod[:, :128]
        for k in range(1, nj // 128):
            acc = acc + prod[:, 128 * k : 128 * (k + 1)]
        one = jnp.sum(jnp.sum(acc, axis=0, keepdims=True), axis=1, keepdims=True)
        total = jnp.where((row == 2) & (col == n), one, total)
    for k in range(message.shape[0]):
        message[k] = total


def relay_kernel(source, got, message):
    peers = got.shape[0]
    total = got[0]
    for k in range(1, peers):
        total = total + got[k]
    which = source[0, 0:2]
    pieces = []
    for p in range(3):
        piece = got[p, 0:2]
        for z in range(1, peers // 4):
            piece = jnp.where(which == z, got[4 * z + p, 0:2], piece)
        pieces.append(piece)
    text = jnp.concatenate(pieces + [total[2:4]], axis=0)
    for k in range(message.shape[0]):
        message[k] = text


def finish_kernel(basis_ref, source, got, surface_ref, residual_ref, fold_ref):
    total = got[0]
    fold = got[0]
    which = source[1]
    for k in range(1, got.shape[0]):
        total = total + got[k]
        fold = jnp.where(which == k, got[k], fold)
    fold_ref[...] = fold
    row = lax.broadcasted_iota(jnp.int32, (8, 128), 0)
    col = lax.broadcasted_iota(jnp.int32, (8, 128), 1)
    gram = {}
    for n, pair in enumerate(PAIRS):
        cell = jnp.where((row == 6) & (col == n), total, 0.0)
        gram[pair] = jnp.sum(jnp.sum(cell, axis=0, keepdims=True), axis=1, keepdims=True)
    xc, rc = coefficients(gram)
    basis = [basis_ref[k] for k in range(4)]
    surface_ref[...] = sum(c * f for c, f in zip(xc, basis) if c is not None)
    residual_ref[...] = sum(c * f for c, f in zip(rc, basis) if c is not None)


def f32(*shape):
    return jax.ShapeDtypeStruct(shape, jnp.float32)


def vmem(*shape):
    return pltpu.VMEM(shape, jnp.float32)


def make_on_device(sizes):
    ny, nxh, nz, nxl, ncore = sizes
    n_lon, n_lat = ny * nxh * nz, nxl * ncore

    def on_device(t, s, u, v, elev, flag, depth, fc):
        nl, ni, nj = t.shape
        lat = lax.axis_index(LAT)
        last = lat == n_lat - 1

        up, down, fields, edges, source = pl.pallas_call(
            pack_kernel,
            out_shape=(
                vmem(80, nj),
                vmem(80, nj),
                vmem(4, ni, nj),
                vmem(40, 128),
                pltpu.VMEM((2, 8, 128), jnp.int32),
            ),
            scratch_shapes=[vmem(128, 128)],
            name="pack",
        )(t, s, u, v, elev, flag, depth, fc.reshape(1, ni))
        west = lax.ppermute(up, LON, [(i, (i + 1) % n_lon) for i in range(n_lon)])
        east = lax.ppermute(down, LON, [((i + 1) % n_lon, i) for i in range(n_lon)])
        wide, slots = pl.pallas_call(
            widen_kernel,
            out_shape=(vmem(4, 32, nj), vmem(4, 16, 128)),
            name="widen",
        )(west, east, fields, edges)
        halo = lax.all_to_all(slots, LAT, 0, 0)
        basis, message = pl.pallas_call(
            krylov_kernel,
            out_shape=(vmem(4, ni, nj), vmem(nz * n_lat, 4, 128)),
            scratch_shapes=[vmem(128, 128)],
            name="krylov",
        )(wide, halo)
        got = lax.all_to_all(message, ("z",) + LAT, 0, 0)
        message = pl.pallas_call(
            relay_kernel, out_shape=vmem(ny * nxh, 8, 128), name="relay"
        )(source, got)
        got = lax.all_to_all(message, ("y", "xh"), 0, 0)
        surface, residual, fold = pl.pallas_call(
            finish_kernel, out_shape=(f32(ni, nj), f32(ni, nj), vmem(8, 128)), name="finish"
        )(basis, source, got)

        level = lax.broadcasted_iota(jnp.int32, t.shape, 0)
        mask = jnp.where((flag[None] == 1) & (level < depth[None]), 1.0, 0.0).astype(jnp.float32)
        q = jnp.stack([t * mask, s * mask])
        ue = u * mask
        vn = v * mask

        def sides(msg):
            tiles = msg[: 8 * nl].reshape(nl, 8, nj)
            return jnp.stack([tiles[:, 0:3], tiles[:, 3:6]]), tiles[:, 6:7]

        q_west, u_west = sides(west)
        q_east, _ = sides(east)
        north = jnp.where(
            last, 0.0, lax.dynamic_index_in_dim(halo, jnp.minimum(lat + 1, n_lat - 1), 0, False)
        )
        south = jnp.where(
            lat == 0, 0.0, lax.dynamic_index_in_dim(halo, jnp.maximum(lat - 1, 0), 0, False)
        )

        def columns(msg):
            return jnp.transpose(msg[:6].reshape(2, 3, nl, ni), (0, 2, 3, 1))

        q_north, q_south = columns(north), columns(south)
        v_south = south[6].reshape(nl, ni, 1)
        zonal = jnp.concatenate([q_west, q, q_east], axis=2)
        merid = jnp.concatenate([q_south, q, q_north], axis=3)
        speed_x = jnp.concatenate([u_west, ue], axis=1)
        place = lax.broadcasted_iota(jnp.int32, (1, 1, nj + 1), 2)
        speed_y = jnp.concatenate([v_south, vn], axis=2)
        speed_y = jnp.where(last & (place > nj - 3), 0.0, speed_y)
        flux_x = face_flux(zonal, speed_x[None], ni + 1, 2)
        flux_y = face_flux(merid, speed_y[None], nj + 1, 3)
        updated = q - (flux_x[:, :, 1:] - flux_x[:, :, :-1]) - (flux_y[..., 1:] - flux_y[..., :-1])
        own = jnp.stack([edges[35:40], edges[27:32]])
        speed = edges[None, 21:24]
        beyond = face_flux(
            jnp.concatenate([own, fold[:6].reshape(2, 3, 128)], axis=1),
            jnp.where(last, speed, 0.0),
            3,
            1,
        )
        change = jnp.concatenate([beyond[:, :1], beyond[:, 1:] - beyond[:, :-1]], axis=1)
        change = jnp.transpose(change.reshape(2, 3, nl, ni), (0, 2, 3, 1))
        updated = (updated - jnp.pad(change, ((0, 0), (0, 0), (0, 0), (nj - 3, 0)))) * mask
        return updated[0], updated[1], surface, residual

    return on_device


def solution(mesh, sizes=SIZES):
    fine = Mesh(mesh.devices.reshape(sizes), ALL)
    block, plane = P(None, LON, LAT), P(LON, LAT)
    return jax.shard_map(
        make_on_device(sizes),
        mesh=fine,
        in_specs=(block,) * 4 + (plane,) * 3 + (P(LON),),
        out_specs=(block, block, plane, plane),
        check_vma=False,
    )
```

time: 90.5 us -> 83.2 us (0.919)
  waiting for transfers between devices: 28.1 us -> 20.6 us
  Pallas kernels: 3.67 us -> 8.82 us
  other arithmetic: 7.92 us -> 3.87 us
  starting transfers between devices: 39.1 us -> 40.6 us
  local copies, waits for them, and re-layouts: 9.12 us -> 7.74 us
    ppermute x1, waiting for transfers between devices: 5.99 us -> 0.01 us  [on_device(): west = lax.ppermute(up, LON, [(i, (i + 1) % n_lon) for i in range(n_lon)])]
    pallas_call x2 -> x5, Pallas kernels: 3.67 us -> 8.82 us  [the longest x1 2.11 us: on_device(): pl.pallas_call(krylov_kernel, out_shape=(vmem(4, ni, nj), vmem(nz * n_lat...]
    unnamed x11 -> x37, local copies, waits for them, and re-layouts: 2.35 us -> 6.39 us
    ppermute x1, starting transfers between devices: 20.5 us -> 17.6 us  [on_device(): east = lax.ppermute(down, LON, [((i + 1) % n_lon, i) for i in range(n_lon)])]
    ppermute x1, starting transfers between devices: 1.91 us -> 4.82 us  [on_device(): west = lax.ppermute(up, LON, [(i, (i + 1) % n_lon) for i in range(n_lon)])]
    broadcast_in_dim x7 -> x0, local copies, waits for them, and re-layouts: 2.54 us -> none  [the longest x4 2.53 us: spread_to(): jnp.broadcast_to(value[None], (count,) + value.shape)]
    all_to_all x4 -> x3, waiting for transfers between devices: 22.1 us -> 20.6 us  [the longest x1 10.2 us: on_device(): got = lax.all_to_all(message, ('z',) + LAT, 0, 0)]
    all_to_all x4 -> x3, starting transfers between devices: 16.7 us -> 18.2 us  [the longest x1 8.47 us: on_device(): got = lax.all_to_all(message, ('y', 'xh'), 0, 0)]
  transfers between devices with their start and end apart: 6 -> 5, of which waited for: 5 -> 3; matrix products, arithmetic and copies ran while one was open for 6% -> 6% of each run, Pallas kernels for 0% -> 0%
where the time goes in v3:
time: 83.2 us; the launch traced here: 82.6 us
  starting transfers between devices  40.6 us (49%)
  waiting for transfers between devices  20.6 us (25%)
  Pallas kernels  8.82 us (11%)
  local copies, waits for them, and re-layouts  7.74 us (9%)
  other arithmetic  3.87 us (5%)
  between operations  1.05 us (1%)
    ppermute x1, starting transfers between devices, on_device(): east = lax.ppermute(down, LON, [((i + 1) % n_lon, i) for i in range(n_lon)])  17.6 us
    all_to_all x1, waiting for transfers between devices, on_device(): got = lax.all_to_all(message, ('z',) + LAT, 0, 0)  10.2 us
    all_to_all x1, starting transfers between devices, on_device(): got = lax.all_to_all(message, ('y', 'xh'), 0, 0)  8.47 us
    all_to_all x1, waiting for transfers between devices, on_device(): got = lax.all_to_all(message, ('y', 'xh'), 0, 0)  8.17 us
    unnamed x37, local copies, waits for them, and re-layouts  6.39 us
    all_to_all x1, starting transfers between devices, on_device(): halo = lax.all_to_all(slots, LAT, 0, 0)  4.86 us
    all_to_all x1, starting transfers between devices, on_device(): got = lax.all_to_all(message, ('z',) + LAT, 0, 0)  4.84 us
    ppermute x1, starting transfers between devices, on_device(): west = lax.ppermute(up, LON, [(i, (i + 1) % n_lon) for i in range(n_lon)])  4.82 us
  transfers between devices with their start and end apart: 5, of which 3 were waited for; matrix products, arithmetic and copies ran while one was open for 6% of the time, Pallas kernels for 0%

profile of v3, /device:TPU:1, one launch (start us, length us, event | category | flops | bytes accessed | tf_op | source)
XLA Modules:
  0.0 82.6 jit_solution(749066107151064315)
XLA Ops:
  0.6 0.0 copy-start.15
  0.6 0.0 copy-start.5
  0.7 0.0 copy-start.6
  0.7 0.0 copy-start.7
  0.7 0.0 copy-start.8
  0.7 1.5 %pack.1 = (f32[80,384]{1,0:T(8,128)S(1)}, f32[80,384]{1,0:T(8,128)S(1)}, f32[4,16,384]{2,1,0:T(8,128)S(1)}, f32[40,128]{1,0:T(8,128)S(1)}, s32[2,8,128]{2,1,0:T(8,128)S(1)}) custom-call(f32[8,16,384]{2,1,0:T(8,128)} %t.1, f32[8,16,384]{2,1,0:T(8,128)} %s.1, f32[8,16,384]{2,1,0:T(8,128)} %u.1, f32[8,16,384]{2,1,0:T(8,128)} %v.1, f32[16,384]{1,0:T(8,128)} %elev.1, ...), custom_call_target="tpu_custom_call" | custom-call | tf_op jit(solution)/shard_map/pack/pallas_call | solution.py:281
  2.2 0.0 copy-start.4
  2.2 0.6 copy-done.4
  2.8 0.0 copy-start.1
  2.8 0.0 copy-start.3
  2.8 4.8 %collective-permute-start = (f32[80,384]{1,0:T(8,128)S(1)}, f32[80,384]{1,0:T(8,128)S(1)}, u32[]{:S(2)}, u32[]{:S(2)}) collective-permute-start(f32[80,384]{1,0:T(8,128)S(1)} %get-tuple-element.16), channel_id=1, source_target_pairs={{0,4},{4,8},{8,12},{12,16},{16,20},{20,24},{24,28},{28,32},{32,36}... | collective-permute-start | bytes 368648 | tf_op jit(solution)/shard_map/ppermute | solution.py:293
  7.6 17.6 %collective-permute-start.1 = (f32[80,384]{1,0:T(8,128)S(1)}, f32[80,384]{1,0:T(8,128)S(1)}, u32[]{:S(2)}, u32[]{:S(2)}) collective-permute-start(f32[80,384]{1,0:T(8,128)S(1)} %get-tuple-element.17), channel_id=1, source_target_pairs={{4,0},{8,4},{12,8},{16,12},{20,16},{24,20},{28,24},{32,28},{36,32}... | collective-permute-start | bytes 368648 | tf_op jit(solution)/shard_map/ppermute | solution.py:294
  25.2 0.0 copy-done.15
  25.2 0.0 copy-start.14
  25.3 0.0 copy-done.5
  25.3 0.0 copy-done.6
  25.3 0.0 copy-done.7
  25.3 0.0 copy-done.8
  25.3 0.7 copy-done.14
  26.0 0.3 fusion.21
  26.3 0.0 copy-done.1
  26.3 0.0 copy-done.3
  26.4 0.0 collective-permute-done.west
  26.4 0.0 copy-start.9
  26.5 0.6 copy-done.9
  27.1 0.0 collective-permute-done.1.east
  27.1 0.0 copy-start.10
  27.2 0.6 copy-done.10
  27.8 1.9 %widen.1 = (f32[4,32,384]{2,1,0:T(8,128)S(1)}, f32[4,16,128]{2,1,0:T(8,128)}) custom-call(f32[80,384]{1,0:T(8,128)} %copy-done.9, f32[80,384]{1,0:T(8,128)} %copy-done.10, f32[4,16,384]{2,1,0:T(8,128)} %copy-done.1, f32[40,128]{1,0:T(8,128)} %copy-done.3), custom_call_target="tpu_custom_call" | custom-call | tf_op jit(solution)/shard_map/widen/pallas_call | solution.py:295
  29.7 0.0 copy-start
  29.7 4.9 %all-to-all-start = ((f32[4,16,128]{2,1,0:T(8,128)}), f32[4,16,128]{2,1,0:T(8,128)S(1)}, u32[]{:S(2)}, u32[]{:S(2)}) async-start(f32[4,16,128]{2,1,0:T(8,128)} %get-tuple-element.20), calls=%async_computation | async-start | bytes 65536 | tf_op jit(solution)/shard_map/all_to_all | solution.py:300
  34.5 0.0 copy-done
  34.5 0.1 maximum_maximum_fusion.1
  34.6 0.9 %add_multiply_fusion.1 = f32[2,8,17,384]{3,1,2,0:T(8,128)S(1)} fusion(f32[2,8,19,384]{3,1,2,0:T(8,128)S(1)} %get-tuple-element.59, f32[2,8,19,384]{3,1,2,0:T(8,128)S(1)} %get-tuple-element.58, f32[8,17,384]{2,0,1:T(8,128)S(1)} %pad_maximum_fusion.1, pred[8,17,384]{2,0,1:T(8,128)(4,1)S(1)} %broadcast_compare_fusion.1), kind=kLoop, calls=%fused_computation.40 | loop fusion | flops 6371328 | bytes 3185664 | tf_op jit(solution)/shard_map/mul | solution.py:38
  35.5 2.2 %all-to-all-done.got = f32[4,16,128]{2,1,0:T(8,128)S(1)} async-done(((f32[4,16,128]{2,1,0:T(8,128)}), f32[4,16,128]{2,1,0:T(8,128)S(1)}, u32[]{:S(2)}, u32[]{:S(2)}) %all-to-all-start) | async-done | bytes 32800 | tf_op jit(solution)/shard_map/all_to_all | solution.py:300
  37.7 0.0 copy-start.13
  37.7 0.6 copy-done.16
  38.3 0.0 copy-done.13
  38.3 2.1 %krylov.1 = (f32[4,16,384]{2,1,0:T(8,128)S(1)}, f32[48,4,128]{2,1,0:T(4,128)}) custom-call(f32[4,32,384]{2,1,0:T(8,128)} %copy-done, f32[4,16,128]{2,1,0:T(8,128)} %copy-done.13), custom_call_target="tpu_custom_call" | custom-call | tf_op jit(solution)/shard_map/krylov/pallas_call | solution.py:301
  40.4 0.6 copy-done.2
  41.1 4.8 %all-to-all-start.1 = ((f32[48,4,128]{2,1,0:T(4,128)}), f32[48,4,128]{2,1,0:T(4,128)S(1)}, u32[]{:S(2)}, u32[]{:S(2)}) async-start(f32[48,4,128]{2,1,0:T(4,128)} %get-tuple-element.24), calls=%async_computation.1 | async-start | bytes 196608 | tf_op jit(solution)/shard_map/all_to_all | solution.py:307
  45.9 0.0 slice-done
  45.9 0.1 reshape.109
  46.0 0.7 dynamic-slice_select_fusion.1
  46.7 0.1 reshape.110
  46.8 0.2 concatenate.56
  47.0 0.2 copy.148
  47.1 0.2 copy.147
  47.3 0.1 broadcast_compare_fusion
  47.5 0.2 copy.145
  47.7 0.2 maximum_maximum_fusion
  47.9 10.2 %all-to-all-done.1.got = f32[48,4,128]{2,1,0:T(4,128)S(1)} async-done(((f32[48,4,128]{2,1,0:T(4,128)}), f32[48,4,128]{2,1,0:T(4,128)S(1)}, u32[]{:S(2)}, u32[]{:S(2)}) %all-to-all-start.1) | async-done | bytes 98336 | tf_op jit(solution)/shard_map/all_to_all | solution.py:307
  58.1 0.6 copy-done.11
  58.7 1.6 %relay.1 = f32[16,8,128]{2,1,0:T(8,128)} custom-call(s32[2,8,128]{2,1,0:T(8,128)} %copy-done.4, f32[48,4,128]{2,1,0:T(4,128)} %copy-done.11), custom_call_target="tpu_custom_call" | custom-call | tf_op jit(solution)/shard_map/relay/pallas_call | solution.py:308
  60.3 8.5 %all-to-all-start.2 = ((f32[16,8,128]{2,1,0:T(8,128)}), f32[16,8,128]{2,1,0:T(8,128)S(1)}, u32[]{:S(2)}, u32[]{:S(2)}) async-start(f32[16,8,128]{2,1,0:T(8,128)} %relay.1), calls=%async_computation.2 | async-start | bytes 131072 | tf_op jit(solution)/shard_map/all_to_all | solution.py:311
  68.8 1.2 %add_multiply_fusion = f32[2,8,16,385]{3,1,2,0:T(8,128)S(1)} fusion(f32[2,8,16,387]{3,1,2,0:T(8,128)S(1)} %get-tuple-element.61, f32[2,8,16,387]{3,1,2,0:T(8,128)S(1)} %get-tuple-element.60, f32[8,16,385]{2,0,1:T(8,128)S(1)} %copy.145, pred[8,16,385]{2,0,1:T(8,128)(4,1)S(1)} %copy.146), kind=kLoop, calls=%fused_computation.28 | loop fusion | flops 6012160 | bytes 3006080 | tf_op jit(solution)/shard_map/mul | solution.py:38
  70.1 8.2 %all-to-all-done.2.got = f32[16,8,128]{2,1,0:T(8,128)S(1)} async-done(((f32[16,8,128]{2,1,0:T(8,128)}), f32[16,8,128]{2,1,0:T(8,128)S(1)}, u32[]{:S(2)}, u32[]{:S(2)}) %all-to-all-start.2) | async-done | bytes 65568 | tf_op jit(solution)/shard_map/all_to_all | solution.py:311
  78.2 0.6 copy-done.12
  78.9 1.7 %finish.1 = (f32[16,384]{1,0:T(8,128)}, f32[16,384]{1,0:T(8,128)}, f32[8,128]{1,0:T(8,128)S(1)}) custom-call(f32[4,16,384]{2,1,0:T(8,128)} %copy-done.2, s32[2,8,128]{2,1,0:T(8,128)} %copy-done.4, f32[16,8,128]{2,1,0:T(8,128)} %copy-done.12), custom_call_target="tpu_custom_call" | custom-call | tf_op jit(solution)/shard_map/finish/pallas_call | solution.py:312
  80.7 0.1 reshape.113
  80.7 0.2 copy.150
  80.9 0.2 fusion.16
  81.2 0.7 copy.152
  81.9 0.7 copy.151
  (30 shorter events, 0.4 us)
Async XLA Ops:
  0.6 24.6 %copy-start.15 = (s32[16,384]{1,0:T(8,128)S(1)}, s32[16,384]{1,0:T(8,128)}, u32[]{:S(2)}) copy-start(s32[16,384]{1,0:T(8,128)} %flag.1) | copy-start | bytes 73732
  0.6 24.6 %copy-start.5 = (f32[8,16,384]{2,1,0:T(8,128)S(1)}, f32[8,16,384]{2,1,0:T(8,128)}, u32[]{:S(2)}) copy-start(f32[8,16,384]{2,1,0:T(8,128)} %t.1) | copy-start | bytes 589828
  0.7 24.6 %copy-start.6 = (f32[8,16,384]{2,1,0:T(8,128)S(1)}, f32[8,16,384]{2,1,0:T(8,128)}, u32[]{:S(2)}) copy-start(f32[8,16,384]{2,1,0:T(8,128)} %s.1) | copy-start | bytes 589828
  0.7 24.6 %copy-start.7 = (f32[8,16,384]{2,1,0:T(8,128)S(1)}, f32[8,16,384]{2,1,0:T(8,128)}, u32[]{:S(2)}) copy-start(f32[8,16,384]{2,1,0:T(8,128)} %u.1) | copy-start | bytes 589828
  0.7 24.6 %copy-start.8 = (f32[8,16,384]{2,1,0:T(8,128)S(1)}, f32[8,16,384]{2,1,0:T(8,128)}, u32[]{:S(2)}) copy-start(f32[8,16,384]{2,1,0:T(8,128)} %v.1) | copy-start | bytes 589828
  2.2 0.6 copy-start.4
  2.8 23.5 %copy-start.1 = (f32[4,16,384]{2,1,0:T(8,128)}, f32[4,16,384]{2,1,0:T(8,128)S(1)}, u32[]{:S(2)}) copy-start(f32[4,16,384]{2,1,0:T(8,128)S(1)} %get-tuple-element.18.fields) | copy-start | bytes 294916
  2.8 23.5 %copy-start.3 = (f32[40,128]{1,0:T(8,128)}, f32[40,128]{1,0:T(8,128)S(1)}, u32[]{:S(2)}) copy-start(f32[40,128]{1,0:T(8,128)S(1)} %get-tuple-element.19.edges) | copy-start | bytes 61444
  2.8 23.6 %collective-permute-start = (f32[80,384]{1,0:T(8,128)S(1)}, f32[80,384]{1,0:T(8,128)S(1)}, u32[]{:S(2)}, u32[]{:S(2)}) collective-permute-start(f32[80,384]{1,0:T(8,128)S(1)} %get-tuple-element.16), channel_id=1, source_target_pairs={{0,4},{4,8},{8,12},{12,16},{16,20},{20,24},{24,28},{28,32},{32,36}... | collective-permute-start | bytes 368648 | tf_op jit(solution)/shard_map/ppermute | solution.py:293
  7.6 19.5 %collective-permute-start.1 = (f32[80,384]{1,0:T(8,128)S(1)}, f32[80,384]{1,0:T(8,128)S(1)}, u32[]{:S(2)}, u32[]{:S(2)}) collective-permute-start(f32[80,384]{1,0:T(8,128)S(1)} %get-tuple-element.17), channel_id=1, source_target_pairs={{4,0},{8,4},{12,8},{16,12},{20,16},{24,20},{28,24},{32,28},{36,32}... | collective-permute-start | bytes 368648 | tf_op jit(solution)/shard_map/ppermute | solution.py:294
  25.2 0.7 copy-start.14
  26.4 0.7 copy-start.9
  27.1 0.7 copy-start.10
  29.7 4.9 %copy-start = (f32[4,32,384]{2,1,0:T(8,128)}, f32[4,32,384]{2,1,0:T(8,128)S(1)}, u32[]{:S(2)}) copy-start(f32[4,32,384]{2,1,0:T(8,128)S(1)} %get-tuple-element.21.wide) | copy-start | bytes 589828
  29.7 8.0 %all-to-all-start = ((f32[4,16,128]{2,1,0:T(8,128)}), f32[4,16,128]{2,1,0:T(8,128)S(1)}, u32[]{:S(2)}, u32[]{:S(2)}) async-start(f32[4,16,128]{2,1,0:T(8,128)} %get-tuple-element.20), calls=%async_computation | async-start | bytes 65536 | tf_op jit(solution)/shard_map/all_to_all | solution.py:300
  37.7 0.6 copy-start.13
  37.7 0.6 copy-start.16
  40.4 0.6 copy-start.2
  40.4 5.5 %slice-start = ((f32[1,16,128]{2,1,0:T(8,128)}), f32[1,6,128]{2,1,0:T(8,128)S(1)}, s32[]{:S(2)}) async-start(f32[1,16,128]{2,1,0:T(8,128)} %copy-done.16), calls=%async_computation.3 | async-start | bytes 8192 | tf_op jit(solution)/shard_map/slice | solution.py:336
  41.1 17.0 %all-to-all-start.1 = ((f32[48,4,128]{2,1,0:T(4,128)}), f32[48,4,128]{2,1,0:T(4,128)S(1)}, u32[]{:S(2)}, u32[]{:S(2)}) async-start(f32[48,4,128]{2,1,0:T(4,128)} %get-tuple-element.24), calls=%async_computation.1 | async-start | bytes 196608 | tf_op jit(solution)/shard_map/all_to_all | solution.py:307
  58.1 0.6 copy-start.11
  60.3 17.9 %all-to-all-start.2 = ((f32[16,8,128]{2,1,0:T(8,128)}), f32[16,8,128]{2,1,0:T(8,128)S(1)}, u32[]{:S(2)}, u32[]{:S(2)}) async-start(f32[16,8,128]{2,1,0:T(8,128)} %relay.1), calls=%async_computation.2 | async-start | bytes 131072 | tf_op jit(solution)/shard_map/all_to_all | solution.py:311
  78.2 0.6 copy-start.12

commit v4 on v3

--- a/solution.py
+++ b/solution.py
@@ -241,24 +241,52 @@
         message[k] = text
 
 
-def finish_kernel(basis_ref, source, got, surface_ref, residual_ref, fold_ref):
+def finish_kernel(
+    basis_ref, source, got, edges, tail, wet, base_t, base_s,
+    surface_ref, residual_ref, out_t, out_s, tile, final, sems,
+):
+    del base_t, base_s
     total = got[0]
     fold = got[0]
     which = source[1]
     for k in range(1, got.shape[0]):
         total = total + got[k]
         fold = jnp.where(which == k, got[k], fold)
-    fold_ref[...] = fold
+    last = jnp.where(lat_index() == 3, 1.0, 0.0)
+    rows = [
+        jnp.concatenate([edges[35:40], fold[0:3]], axis=0),
+        jnp.concatenate([edges[27:32], fold[3:6]], axis=0),
+    ]
     row = lax.broadcasted_iota(jnp.int32, (8, 128), 0)
-    col = lax.broadcasted_iota(jnp.int32, (8, 128), 1)
+    speed = jnp.where(row < 3, pltpu.roll(edges[16:24], 3, 0) * last, 0.0)
+    pos = speed > 0.0
+    nj = surface_ref.shape[1]
+    copies = []
+    for k, out in enumerate((out_t, out_s)):
+        q = [rows[k]] + [pltpu.roll(rows[k], 8 - o, 0) for o in range(1, 6)]
+        face = speed * weno_upwind(*[jnp.where(pos, q[i], q[5 - i]) for i in range(5)])
+        change = face - jnp.where(row == 0, 0.0, pltpu.roll(face, 1, 0))
+        tile[...] = jnp.zeros((128, 128), jnp.float32)
+        tile[125:128] = change[0:3]
+        final[k] = (tail[k] - tile[...].T.reshape(tail.shape[1:])) * wet[...]
+        copy = pltpu.make_async_copy(final.at[k], out.at[:, :, nj - 128 : nj], sems.at[k])
+        copy.start()
+        copies.append(copy)
+    line = total[6:7]
+    col = lax.broadcasted_iota(jnp.int32, (1, 128), 1)
     gram = {}
     for n, pair in enumerate(PAIRS):
-        cell = jnp.where((row == 6) & (col == n), total, 0.0)
-        gram[pair] = jnp.sum(jnp.sum(cell, axis=0, keepdims=True), axis=1, keepdims=True)
+        gram[pair] = jnp.sum(jnp.where(col == n, line, 0.0), axis=1, keepdims=True)
     xc, rc = coefficients(gram)
     basis = [basis_ref[k] for k in range(4)]
     surface_ref[...] = sum(c * f for c, f in zip(xc, basis) if c is not None)
     residual_ref[...] = sum(c * f for c, f in zip(rc, basis) if c is not None)
+    for copy in copies:
+        copy.wait()
+
+
+def near(value):
+    return pltpu.with_memory_space_constraint(value, pltpu.VMEM)
 
 
 def f32(*shape):
@@ -296,23 +324,19 @@
             widen_kernel,
             out_shape=(vmem(4, 32, nj), vmem(4, 16, 128)),
             name="widen",
-        )(west, east, fields, edges)
+        )(near(west), near(east), near(fields), near(edges))
         halo = lax.all_to_all(slots, LAT, 0, 0)
         basis, message = pl.pallas_call(
             krylov_kernel,
             out_shape=(vmem(4, ni, nj), vmem(nz * n_lat, 4, 128)),
             scratch_shapes=[vmem(128, 128)],
             name="krylov",
-        )(wide, halo)
+        )(near(wide), near(halo))
         got = lax.all_to_all(message, ("z",) + LAT, 0, 0)
         message = pl.pallas_call(
             relay_kernel, out_shape=vmem(ny * nxh, 8, 128), name="relay"
-        )(source, got)
+        )(near(source), near(got))
         got = lax.all_to_all(message, ("y", "xh"), 0, 0)
-        surface, residual, fold = pl.pallas_call(
-            finish_kernel, out_shape=(f32(ni, nj), f32(ni, nj), vmem(8, 128)), name="finish"
-        )(basis, source, got)
-
         level = lax.broadcasted_iota(jnp.int32, t.shape, 0)
         mask = jnp.where((flag[None] == 1) & (level < depth[None]), 1.0, 0.0).astype(jnp.float32)
         q = jnp.stack([t * mask, s * mask])
@@ -346,18 +370,27 @@
         flux_x = face_flux(zonal, speed_x[None], ni + 1, 2)
         flux_y = face_flux(merid, speed_y[None], nj + 1, 3)
         updated = q - (flux_x[:, :, 1:] - flux_x[:, :, :-1]) - (flux_y[..., 1:] - flux_y[..., :-1])
-        own = jnp.stack([edges[35:40], edges[27:32]])
-        speed = edges[None, 21:24]
-        beyond = face_flux(
-            jnp.concatenate([own, fold[:6].reshape(2, 3, 128)], axis=1),
-            jnp.where(last, speed, 0.0),
-            3,
-            1,
+        updated = updated * mask
+        hbm, local = pl.BlockSpec(memory_space=pl.ANY), pl.BlockSpec(memory_space=pltpu.VMEM)
+        surface, residual, t_next, s_next = pl.pallas_call(
+            finish_kernel,
+            in_specs=[local] * 6 + [hbm] * 2,
+            out_specs=(local, local, hbm, hbm),
+            out_shape=(f32(ni, nj), f32(ni, nj), f32(nl, ni, nj), f32(nl, ni, nj)),
+            input_output_aliases={6: 2, 7: 3},
+            scratch_shapes=[vmem(128, 128), vmem(2, nl, ni, 128), pltpu.SemaphoreType.DMA((2,))],
+            name="finish",
+        )(
+            near(basis),
+            near(source),
+            near(got),
+            near(edges),
+            near(updated[..., nj - 128 :]),
+            near(mask[..., nj - 128 :]),
+            updated[0],
+            updated[1],
         )
-        change = jnp.concatenate([beyond[:, :1], beyond[:, 1:] - beyond[:, :-1]], axis=1)
-        change = jnp.transpose(change.reshape(2, 3, nl, ni), (0, 2, 3, 1))
-        updated = (updated - jnp.pad(change, ((0, 0), (0, 0), (0, 0), (nj - 3, 0)))) * mask
-        return updated[0], updated[1], surface, residual
+        return t_next, s_next, surface, residual
 
     return on_device
 

time: 83.2 us -> 75 us (0.901)
  local copies, waits for them, and re-layouts: 7.74 us -> 2.17 us
  Pallas kernels: 8.82 us -> 5.71 us
    unnamed x37 -> x14, local copies, waits for them, and re-layouts: 6.39 us -> 0.6 us
    pallas_call x1, Pallas kernels: 1.9 us -> 0.91 us  [on_device(): pl.pallas_call(widen_kernel, out_shape=(vmem(4, 32, nj), vmem(4, 16, 128)...]
    pallas_call x1, Pallas kernels: 2.11 us -> 1.18 us  [on_device(): pl.pallas_call(krylov_kernel, out_shape=(vmem(4, ni, nj), vmem(nz * n_lat...]
    pallas_call x1, Pallas kernels: 1.58 us -> 0.67 us  [on_device(): pl.pallas_call(relay_kernel, out_shape=vmem(ny * nxh, 8, 128), name='relay')]
    ppermute x1, waiting for transfers between devices: 0.01 us -> 0.89 us  [on_device(): west = lax.ppermute(up, LON, [(i, (i + 1) % n_lon) for i in range(n_lon)])]
    mul x3 -> x2, other arithmetic: 2.15 us -> 2.61 us  [face_flux(): return speed * weno_upwind(a, b, c, d, e)]
  transfers between devices with their start and end apart: 5 -> 5, of which waited for: 3 -> 5; matrix products, arithmetic and copies ran while one was open for 6% -> 7% of each run, Pallas kernels for 0% -> 0%
where the time goes in v4:
time: 75 us; the launch traced here: 74.6 us
  starting transfers between devices  40.9 us (55%)
  waiting for transfers between devices  21.3 us (28%)
  Pallas kernels  5.71 us (8%)
  other arithmetic  3.57 us (5%)
  local copies, waits for them, and re-layouts  2.17 us (3%)
  between operations  0.92 us (1%)
    ppermute x1, starting transfers between devices, on_device(): east = lax.ppermute(down, LON, [((i + 1) % n_lon, i) for i in range(n_lon)])  17.6 us
    all_to_all x1, waiting for transfers between devices, on_device(): got = lax.all_to_all(message, ('z',) + LAT, 0, 0)  9.53 us
    all_to_all x1, waiting for transfers between devices, on_device(): got = lax.all_to_all(message, ('y', 'xh'), 0, 0)  8.65 us
    all_to_all x1, starting transfers between devices, on_device(): got = lax.all_to_all(message, ('y', 'xh'), 0, 0)  8.47 us
    all_to_all x1, starting transfers between devices, on_device(): got = lax.all_to_all(message, ('z',) + LAT, 0, 0)  4.98 us
    ppermute x1, starting transfers between devices, on_device(): west = lax.ppermute(up, LON, [(i, (i + 1) % n_lon) for i in range(n_lon)])  4.96 us
    all_to_all x1, starting transfers between devices, on_device(): halo = lax.all_to_all(slots, LAT, 0, 0)  4.9 us
    mul x2, other arithmetic, face_flux(): return speed * weno_upwind(a, b, c, d, e)  2.61 us
  transfers between devices with their start and end apart: 5, of which 5 were waited for; matrix products, arithmetic and copies ran while one was open for 7% of the time, Pallas kernels for 0%

profile of v4, /device:TPU:1, one launch (start us, length us, event | category | flops | bytes accessed | tf_op | source)
XLA Modules:
  0.0 74.6 jit_solution(15271034116190645739)
XLA Ops:
  0.6 0.0 copy-start.5
  0.6 0.0 copy-start
  0.7 0.0 copy-start.1
  0.7 0.0 copy-start.2
  0.7 0.0 copy-start.3
  0.7 1.5 %pack.1 = (f32[80,384]{1,0:T(8,128)S(1)}, f32[80,384]{1,0:T(8,128)S(1)}, f32[4,16,384]{2,1,0:T(8,128)S(1)}, f32[40,128]{1,0:T(8,128)S(1)}, s32[2,8,128]{2,1,0:T(8,128)S(1)}) custom-call(f32[8,16,384]{2,1,0:T(8,128)} %t.1, f32[8,16,384]{2,1,0:T(8,128)} %s.1, f32[8,16,384]{2,1,0:T(8,128)} %u.1, f32[8,16,384]{2,1,0:T(8,128)} %v.1, f32[16,384]{1,0:T(8,128)} %elev.1, ...), custom_call_target="tpu_custom_call" | custom-call | tf_op jit(solution)/shard_map/pack/pallas_call | solution.py:309
  2.2 0.0 copy-start.4
  2.2 5.0 %collective-permute-start = (f32[80,384]{1,0:T(8,128)S(1)}, f32[80,384]{1,0:T(8,128)S(1)}, u32[]{:S(2)}, u32[]{:S(2)}) collective-permute-start(f32[80,384]{1,0:T(8,128)S(1)} %get-tuple-element.17), channel_id=1, source_target_pairs={{0,4},{4,8},{8,12},{12,16},{16,20},{20,24},{24,28},{28,32},{32,36}... | collective-permute-start | bytes 368648 | tf_op jit(solution)/shard_map/ppermute | solution.py:321
  7.2 17.6 %collective-permute-start.1 = (f32[80,384]{1,0:T(8,128)S(1)}, f32[80,384]{1,0:T(8,128)S(1)}, u32[]{:S(2)}, u32[]{:S(2)}) collective-permute-start(f32[80,384]{1,0:T(8,128)S(1)} %get-tuple-element.18), channel_id=1, source_target_pairs={{4,0},{8,4},{12,8},{16,12},{20,16},{24,20},{28,24},{32,28},{36,32}... | collective-permute-start | bytes 368648 | tf_op jit(solution)/shard_map/ppermute | solution.py:322
  24.8 0.0 copy-done.5
  24.8 0.0 copy-done
  24.8 0.0 copy-done.1
  24.8 0.0 copy-done.2
  24.8 0.0 copy-done.3
  24.8 0.0 copy-done.4
  24.9 0.1 fusion.20
  25.0 0.9 %collective-permute-done.west = f32[80,384]{1,0:T(8,128)S(1)} collective-permute-done((f32[80,384]{1,0:T(8,128)S(1)}, f32[80,384]{1,0:T(8,128)S(1)}, u32[]{:S(2)}, u32[]{:S(2)}) %collective-permute-start) | collective-permute-done | bytes 122912 | tf_op jit(solution)/shard_map/ppermute | solution.py:321
  25.9 0.1 broadcast_compare_fusion
  26.1 0.6 collective-permute-done.1.east
  26.6 0.9 %widen.1 = (f32[4,32,384]{2,1,0:T(8,128)S(1)}, f32[4,16,128]{2,1,0:T(8,128)}) custom-call(f32[80,384]{1,0:T(8,128)S(1)} %collective-permute-done.west, f32[80,384]{1,0:T(8,128)S(1)} %collective-permute-done.1.east, f32[4,16,384]{2,1,0:T(8,128)S(1)} %get-tuple-element.19.fields, f32[40,128]{1,0:T(8,128)S(1)} %get-tuple-element.20.edges), custom_call_target="tpu_custom_call" | custom-call | tf_op jit(solution)/shard_map/widen/pallas_call | solution.py:323
  27.5 4.9 %all-to-all-start = ((f32[4,16,128]{2,1,0:T(8,128)}), f32[4,16,128]{2,1,0:T(8,128)S(1)}, u32[]{:S(2)}, u32[]{:S(2)}) async-start(f32[4,16,128]{2,1,0:T(8,128)} %get-tuple-element.22), calls=%async_computation | async-start | bytes 65536 | tf_op jit(solution)/shard_map/all_to_all | solution.py:328
  32.5 0.1 maximum_maximum_fusion
  32.6 1.4 %add_multiply_fusion = f32[2,8,17,384]{3,2,1,0:T(8,128)S(1)} fusion(f32[2,8,19,384]{3,2,1,0:T(8,128)S(1)} %get-tuple-element.35, f32[2,8,19,384]{3,2,1,0:T(8,128)S(1)} %get-tuple-element.34, f32[8,17,384]{2,1,0:T(8,128)S(1)} %pad_maximum_fusion.1, pred[8,17,384]{2,1,0:T(8,128)(4,1)S(1)} %broadcast_compare_fusion), kind=kLoop, calls=%fused_computation.28 | loop fusion | flops 6371328 | bytes 3185664 | tf_op jit(solution)/shard_map/mul | solution.py:38
  33.9 1.7 %all-to-all-done.got = f32[4,16,128]{2,1,0:T(8,128)S(1)} async-done(((f32[4,16,128]{2,1,0:T(8,128)}), f32[4,16,128]{2,1,0:T(8,128)S(1)}, u32[]{:S(2)}, u32[]{:S(2)}) %all-to-all-start) | async-done | bytes 32800 | tf_op jit(solution)/shard_map/all_to_all | solution.py:328
  35.6 0.0 copy-start.6
  35.6 0.6 copy-done.6
  36.2 1.2 %krylov.1 = (f32[4,16,384]{2,1,0:T(8,128)S(1)}, f32[48,4,128]{2,1,0:T(4,128)}) custom-call(f32[4,32,384]{2,1,0:T(8,128)S(1)} %get-tuple-element.21.wide, f32[4,16,128]{2,1,0:T(8,128)S(1)} %all-to-all-done.got), custom_call_target="tpu_custom_call" | custom-call | tf_op jit(solution)/shard_map/krylov/pallas_call | solution.py:329
  37.4 0.0 slice-start
  37.4 5.0 %all-to-all-start.1 = ((f32[48,4,128]{2,1,0:T(4,128)}), f32[48,4,128]{2,1,0:T(4,128)S(1)}, u32[]{:S(2)}, u32[]{:S(2)}) async-start(f32[48,4,128]{2,1,0:T(4,128)} %get-tuple-element.25), calls=%async_computation.1 | async-start | bytes 196608 | tf_op jit(solution)/shard_map/all_to_all | solution.py:335
  42.4 0.0 slice-done
  42.4 0.1 reshape.99
  42.5 0.2 copy.19
  42.6 0.1 reshape.100
  42.7 0.2 copy.20
  42.9 0.2 concatenate.48
  43.1 0.2 maximum_maximum_fusion.2
  43.3 0.1 broadcast_compare_fusion.1
  43.5 1.2 %add_multiply_fusion.1 = f32[2,8,16,385]{3,2,1,0:T(8,128)S(1)} fusion(f32[2,8,16,387]{3,2,1,0:T(8,128)S(1)} %get-tuple-element.37, f32[2,8,16,387]{3,2,1,0:T(8,128)S(1)} %get-tuple-element.36, f32[8,16,385]{2,1,0:T(8,128)S(1)} %get-tuple-element.31, pred[8,16,385]{2,1,0:T(8,128)(4,1)S(1)} %get-tuple-element.30), kind=kLoop, calls=%fused_computation.40 | loop fusion | flops 6012160 | bytes 3006080 | tf_op jit(solution)/shard_map/mul | solution.py:38
  44.7 0.3 fusion.15
  45.0 9.5 %all-to-all-done.1.got = f32[48,4,128]{2,1,0:T(4,128)S(1)} async-done(((f32[48,4,128]{2,1,0:T(4,128)}), f32[48,4,128]{2,1,0:T(4,128)S(1)}, u32[]{:S(2)}, u32[]{:S(2)}) %all-to-all-start.1) | async-done | bytes 98336 | tf_op jit(solution)/shard_map/all_to_all | solution.py:335
  54.6 0.7 relay.1
  55.2 8.5 %all-to-all-start.2 = ((f32[16,8,128]{2,1,0:T(8,128)}), f32[16,8,128]{2,1,0:T(8,128)S(1)}, u32[]{:S(2)}, u32[]{:S(2)}) async-start(f32[16,8,128]{2,1,0:T(8,128)} %relay.1), calls=%async_computation.2 | async-start | bytes 131072 | tf_op jit(solution)/shard_map/all_to_all | solution.py:339
  63.7 0.8 %slice_bitcast_fusion = (f32[8,16,384]{2,1,0:T(8,128)}, f32[8,16,384]{2,1,0:T(8,128)}) fusion(f32[2,8,16,384]{3,2,1,0:T(8,128)S(1)} %fusion.15), kind=kLoop, calls=%fused_computation.55 | loop fusion | bytes 786432 | tf_op jit(solution)/shard_map/squeeze | solution.py:391
  64.5 8.7 %all-to-all-done.2.got = f32[16,8,128]{2,1,0:T(8,128)S(1)} async-done(((f32[16,8,128]{2,1,0:T(8,128)}), f32[16,8,128]{2,1,0:T(8,128)S(1)}, u32[]{:S(2)}, u32[]{:S(2)}) %all-to-all-start.2) | async-done | bytes 65568 | tf_op jit(solution)/shard_map/all_to_all | solution.py:339
  73.1 1.4 %finish.1 = (f32[16,384]{1,0:T(8,128)}, f32[16,384]{1,0:T(8,128)}, f32[8,16,384]{2,1,0:T(8,128)}, f32[8,16,384]{2,1,0:T(8,128)}) custom-call(f32[4,16,384]{2,1,0:T(8,128)S(1)} %get-tuple-element.23.basis_ref, s32[2,8,128]{2,1,0:T(8,128)S(1)} %get-tuple-element.24.source, ...), custom_call_target="tpu_custom_call", output_to_operand_aliasing={{2}: (6, {}), {3}: (7, {})} | custom-call | tf_op jit(solution)/shard_map/finish/pallas_call | solution.py:375
  (13 shorter events, 0.2 us)
Async XLA Ops:
  0.6 24.2 %copy-start.5 = (s32[16,384]{1,0:T(8,128)S(1)}, s32[16,384]{1,0:T(8,128)}, u32[]{:S(2)}) copy-start(s32[16,384]{1,0:T(8,128)} %flag.1) | copy-start | bytes 73732
  0.6 24.2 %copy-start = (f32[8,16,384]{2,1,0:T(8,128)S(1)}, f32[8,16,384]{2,1,0:T(8,128)}, u32[]{:S(2)}) copy-start(f32[8,16,384]{2,1,0:T(8,128)} %t.1) | copy-start | bytes 589828
  0.7 24.2 %copy-start.1 = (f32[8,16,384]{2,1,0:T(8,128)S(1)}, f32[8,16,384]{2,1,0:T(8,128)}, u32[]{:S(2)}) copy-start(f32[8,16,384]{2,1,0:T(8,128)} %s.1) | copy-start | bytes 589828
  0.7 24.2 %copy-start.2 = (f32[8,16,384]{2,1,0:T(8,128)S(1)}, f32[8,16,384]{2,1,0:T(8,128)}, u32[]{:S(2)}) copy-start(f32[8,16,384]{2,1,0:T(8,128)} %u.1) | copy-start | bytes 589828
  0.7 24.2 %copy-start.3 = (f32[8,16,384]{2,1,0:T(8,128)S(1)}, f32[8,16,384]{2,1,0:T(8,128)}, u32[]{:S(2)}) copy-start(f32[8,16,384]{2,1,0:T(8,128)} %v.1) | copy-start | bytes 589828
  2.2 22.6 %copy-start.4 = (s32[16,384]{1,0:T(8,128)S(1)}, s32[16,384]{1,0:T(8,128)}, u32[]{:S(2)}) copy-start(s32[16,384]{1,0:T(8,128)} %depth.1) | copy-start | bytes 73732
  2.2 23.7 %collective-permute-start = (f32[80,384]{1,0:T(8,128)S(1)}, f32[80,384]{1,0:T(8,128)S(1)}, u32[]{:S(2)}, u32[]{:S(2)}) collective-permute-start(f32[80,384]{1,0:T(8,128)S(1)} %get-tuple-element.17), channel_id=1, source_target_pairs={{0,4},{4,8},{8,12},{12,16},{16,20},{20,24},{24,28},{28,32},{32,36}... | collective-permute-start | bytes 368648 | tf_op jit(solution)/shard_map/ppermute | solution.py:321
  7.2 19.4 %collective-permute-start.1 = (f32[80,384]{1,0:T(8,128)S(1)}, f32[80,384]{1,0:T(8,128)S(1)}, u32[]{:S(2)}, u32[]{:S(2)}) collective-permute-start(f32[80,384]{1,0:T(8,128)S(1)} %get-tuple-element.18), channel_id=1, source_target_pairs={{4,0},{8,4},{12,8},{16,12},{20,16},{24,20},{28,24},{32,28},{36,32}... | collective-permute-start | bytes 368648 | tf_op jit(solution)/shard_map/ppermute | solution.py:322
  27.5 8.1 %all-to-all-start = ((f32[4,16,128]{2,1,0:T(8,128)}), f32[4,16,128]{2,1,0:T(8,128)S(1)}, u32[]{:S(2)}, u32[]{:S(2)}) async-start(f32[4,16,128]{2,1,0:T(8,128)} %get-tuple-element.22), calls=%async_computation | async-start | bytes 65536 | tf_op jit(solution)/shard_map/all_to_all | solution.py:328
  35.6 0.6 copy-start.6
  37.4 5.0 %slice-start = ((f32[1,16,128]{2,1,0:T(8,128)}), f32[1,6,128]{2,1,0:T(8,128)S(1)}, s32[]{:S(2)}) async-start(f32[1,16,128]{2,1,0:T(8,128)} %copy-done.6), calls=%async_computation.3 | async-start | bytes 8192 | tf_op jit(solution)/shard_map/slice | solution.py:360
  37.4 17.2 %all-to-all-start.1 = ((f32[48,4,128]{2,1,0:T(4,128)}), f32[48,4,128]{2,1,0:T(4,128)S(1)}, u32[]{:S(2)}, u32[]{:S(2)}) async-start(f32[48,4,128]{2,1,0:T(4,128)} %get-tuple-element.25), calls=%async_computation.1 | async-start | bytes 196608 | tf_op jit(solution)/shard_map/all_to_all | solution.py:335
  55.2 17.9 %all-to-all-start.2 = ((f32[16,8,128]{2,1,0:T(8,128)}), f32[16,8,128]{2,1,0:T(8,128)S(1)}, u32[]{:S(2)}, u32[]{:S(2)}) async-start(f32[16,8,128]{2,1,0:T(8,128)} %relay.1), calls=%async_computation.2 | async-start | bytes 131072 | tf_op jit(solution)/shard_map/all_to_all | solution.py:339

commit v5 on v4

--- a/solution.py
+++ b/solution.py
@@ -97,7 +97,13 @@
     return x
 
 
-def pack_kernel(t, s, u, v, elev, flag, depth, fc, up, down, fields, edges, source, tile):
+def lon_even():
+    return lax.rem(lax.axis_index("z"), 2) == 0
+
+
+def pack_kernel(
+    t, s, u, v, elev, flag, depth, fc, far, close, fields, edges, source, up, down, tile
+):
     nl, ni, nj = t.shape
     ocean = flag[...] == 1
     wet = depth[...]
@@ -138,6 +144,9 @@
     down[70:73] = nm[:3]
     down[73:76] = coupler[:3]
     down[76:80] = zero[:4]
+    even = lon_even()
+    far[...] = jnp.where(even, down[...], up[...])
+    close[...] = jnp.where(even, up[...], down[...])
     turned = tile[...].T
     edges[0:16] = turned[0:16]
     edges[16:40] = turned[104:128]
@@ -150,17 +159,18 @@
     source[1] = row
 
 
-def widen_kernel(west, east, fields, edges, wide, slots):
+def widen_kernel(far, close, fields, edges, wide, slots):
     _, ni, nj = fields.shape
     lat = lat_index()
+    even = lon_even()
     blank = jnp.zeros((8, nj), jnp.float32)
     spans = ((64, 67, 64, 67), (67, 71, 67, 70), (71, 74, 70, 73), (74, 77, 73, 76))
     for k, (w0, w1, e0, e1) in enumerate(spans):
         wide[k, 0:8] = blank
         wide[k, 24:32] = blank
-        wide[k, 8 - (w1 - w0) : 8] = west[w0:w1]
+        wide[k, 8 - (w1 - w0) : 8] = jnp.where(even, far[w0:w1], close[w0:w1])
         wide[k, 8 : 8 + ni] = fields[k]
-        wide[k, 24 : 24 + (e1 - e0)] = east[e0:e1]
+        wide[k, 24 : 24 + (e1 - e0)] = jnp.where(even, close[e0:e1], far[e0:e1])
     lane = lax.broadcasted_iota(jnp.int32, (4, 32, 128), 2)
     both = jnp.where(lane < 64, wide[:, :, 0:128], wide[:, :, nj - 128 : nj])
     turned = both.reshape(128, 128).T
@@ -177,16 +187,20 @@
         ahead = p > lat
         slots[p, 0:8] = jnp.where(ahead, north, south)
         slots[p, 8:12] = jnp.where(ahead, turned[124:128], turned[0:4])
-        slots[p, 12:14] = fold[2 * p : 2 * p + 2]
-        slots[p, 14:16] = none[:2]
-
-
-def krylov_kernel(wide, got, basis_ref, message, tile):
+        slots[p, 12:15] = fold[0:3] if p < 2 else fold[3:6]
+        slots[p, 15:16] = none[:1]
+
+
+def krylov_kernel(wide, got, basis_ref, message, rims, tile):
     ni, nj = basis_ref.shape[1:]
     lat = lat_index()
     tile[...] = jnp.zeros((128, 128), jnp.float32)
-    tile[0:4] = jnp.where(lat < 3, got[jnp.minimum(lat + 1, 3), 8:12], 0.0)
-    tile[124:128] = jnp.where(lat > 0, got[jnp.maximum(lat - 1, 0), 8:12], 0.0)
+    north = jnp.where(lat < 3, got[jnp.minimum(lat + 1, 3)], 0.0)
+    south = jnp.where(lat > 0, got[jnp.maximum(lat - 1, 0)], 0.0)
+    rims[0] = north[0:8]
+    rims[1] = south[0:8]
+    tile[0:4] = north[8:12]
+    tile[124:128] = south[8:12]
     beyond = tile[...].T.reshape(4, 32, 128)
     part, em, nm, cpl = (jnp.concatenate([wide[k], beyond[k]], axis=1) for k in range(4))
     rows, lanes = part.shape
@@ -211,7 +225,7 @@
         basis_ref[k] = basis[k]
     row = lax.broadcasted_iota(jnp.int32, (4, 128), 0)
     col = lax.broadcasted_iota(jnp.int32, (4, 128), 1)
-    total = jnp.concatenate([got[3, 12:14], jnp.zeros((2, 128), jnp.float32)], axis=0)
+    total = jnp.concatenate([got[3, 12:15], jnp.zeros((1, 128), jnp.float32)], axis=0)
     for n, (i, j) in enumerate(PAIRS):
         prod = basis[i] * basis[j]
         prod = prod[:8] + prod[8:]
@@ -219,7 +233,7 @@
         for k in range(1, nj // 128):
             acc = acc + prod[:, 128 * k : 128 * (k + 1)]
         one = jnp.sum(jnp.sum(acc, axis=0, keepdims=True), axis=1, keepdims=True)
-        total = jnp.where((row == 2) & (col == n), one, total)
+        total = jnp.where((row == 3) & (col == n), one, total)
     for k in range(message.shape[0]):
         message[k] = total
 
@@ -229,14 +243,12 @@
     total = got[0]
     for k in range(1, peers):
         total = total + got[k]
-    which = source[0, 0:2]
-    pieces = []
-    for p in range(3):
-        piece = got[p, 0:2]
-        for z in range(1, peers // 4):
-            piece = jnp.where(which == z, got[4 * z + p, 0:2], piece)
-        pieces.append(piece)
-    text = jnp.concatenate(pieces + [total[2:4]], axis=0)
+    which = source[0, 0:4]
+    piece = got[0]
+    for z in range(1, peers // 2):
+        piece = jnp.where(which == z, got[2 * z], piece)
+    row = lax.broadcasted_iota(jnp.int32, (4, 128), 0)
+    text = jnp.where(row < 3, piece, total)
     for k in range(message.shape[0]):
         message[k] = text
 
@@ -247,15 +259,16 @@
 ):
     del base_t, base_s
     total = got[0]
-    fold = got[0]
-    which = source[1]
     for k in range(1, got.shape[0]):
         total = total + got[k]
-        fold = jnp.where(which == k, got[k], fold)
+    fold = [got[0], got[1]]
+    which = source[1, 0:4]
+    for k in range(1, got.shape[0] // 2):
+        fold = [jnp.where(which == k, got[2 * k + i], fold[i]) for i in range(2)]
     last = jnp.where(lat_index() == 3, 1.0, 0.0)
     rows = [
-        jnp.concatenate([edges[35:40], fold[0:3]], axis=0),
-        jnp.concatenate([edges[27:32], fold[3:6]], axis=0),
+        jnp.concatenate([edges[35:40], fold[0][0:3]], axis=0),
+        jnp.concatenate([edges[27:32], fold[1][0:3]], axis=0),
     ]
     row = lax.broadcasted_iota(jnp.int32, (8, 128), 0)
     speed = jnp.where(row < 3, pltpu.roll(edges[16:24], 3, 0) * last, 0.0)
@@ -272,7 +285,7 @@
         copy = pltpu.make_async_copy(final.at[k], out.at[:, :, nj - 128 : nj], sems.at[k])
         copy.start()
         copies.append(copy)
-    line = total[6:7]
+    line = total[3:4]
     col = lax.broadcasted_iota(jnp.int32, (1, 128), 1)
     gram = {}
     for n, pair in enumerate(PAIRS):
@@ -306,7 +319,7 @@
         lat = lax.axis_index(LAT)
         last = lat == n_lat - 1
 
-        up, down, fields, edges, source = pl.pallas_call(
+        far, close, fields, edges, source = pl.pallas_call(
             pack_kernel,
             out_shape=(
                 vmem(80, nj),
@@ -315,28 +328,34 @@
                 vmem(40, 128),
                 pltpu.VMEM((2, 8, 128), jnp.int32),
             ),
-            scratch_shapes=[vmem(128, 128)],
+            scratch_shapes=[vmem(80, nj), vmem(80, nj), vmem(128, 128)],
             name="pack",
         )(t, s, u, v, elev, flag, depth, fc.reshape(1, ni))
-        west = lax.ppermute(up, LON, [(i, (i + 1) % n_lon) for i in range(n_lon)])
-        east = lax.ppermute(down, LON, [((i + 1) % n_lon, i) for i in range(n_lon)])
+        def swaps(first):
+            pairs = []
+            for i in range(first, n_lon, 2):
+                pairs += [(i, (i + 1) % n_lon), ((i + 1) % n_lon, i)]
+            return pairs
+
+        far = lax.ppermute(far, LON, swaps(1))
+        close = lax.ppermute(close, LON, swaps(0))
         wide, slots = pl.pallas_call(
             widen_kernel,
             out_shape=(vmem(4, 32, nj), vmem(4, 16, 128)),
             name="widen",
-        )(near(west), near(east), near(fields), near(edges))
+        )(near(far), near(close), near(fields), near(edges))
         halo = lax.all_to_all(slots, LAT, 0, 0)
-        basis, message = pl.pallas_call(
+        basis, message, rims = pl.pallas_call(
             krylov_kernel,
-            out_shape=(vmem(4, ni, nj), vmem(nz * n_lat, 4, 128)),
+            out_shape=(vmem(4, ni, nj), vmem(nz * ncore, 4, 128), vmem(2, 8, 128)),
             scratch_shapes=[vmem(128, 128)],
             name="krylov",
         )(near(wide), near(halo))
-        got = lax.all_to_all(message, ("z",) + LAT, 0, 0)
+        got = lax.all_to_all(message, ("z", "core"), 0, 0)
         message = pl.pallas_call(
-            relay_kernel, out_shape=vmem(ny * nxh, 8, 128), name="relay"
+            relay_kernel, out_shape=vmem(ny * nxh * nxl, 4, 128), name="relay"
         )(near(source), near(got))
-        got = lax.all_to_all(message, ("y", "xh"), 0, 0)
+        got = lax.all_to_all(message, ("y", "xh", "xl"), 0, 0)
         level = lax.broadcasted_iota(jnp.int32, t.shape, 0)
         mask = jnp.where((flag[None] == 1) & (level < depth[None]), 1.0, 0.0).astype(jnp.float32)
         q = jnp.stack([t * mask, s * mask])
@@ -347,14 +366,12 @@
             tiles = msg[: 8 * nl].reshape(nl, 8, nj)
             return jnp.stack([tiles[:, 0:3], tiles[:, 3:6]]), tiles[:, 6:7]
 
+        even = lon_even()
+        west = jnp.where(even, far, close)
+        east = jnp.where(even, close, far)
         q_west, u_west = sides(west)
         q_east, _ = sides(east)
-        north = jnp.where(
-            last, 0.0, lax.dynamic_index_in_dim(halo, jnp.minimum(lat + 1, n_lat - 1), 0, False)
-        )
-        south = jnp.where(
-            lat == 0, 0.0, lax.dynamic_index_in_dim(halo, jnp.maximum(lat - 1, 0), 0, False)
-        )
+        north, south = rims[0], rims[1]
 
         def columns(msg):
             return jnp.transpose(msg[:6].reshape(2, 3, nl, ni), (0, 2, 3, 1))

time: 75 us -> 70.7 us (0.943)
  starting transfers between devices: 40.9 us -> 37.1 us
    all_to_all x2, starting transfers between devices: 13.4 us -> 9.17 us  [the longest x1 4.86 us: on_device(): got = lax.all_to_all(message, ('y', 'xh', 'xl'), 0, 0)]
    ppermute x2, waiting for transfers between devices: 1.46 us -> 3.46 us  [the longest x1 2.59 us: on_device(): close = lax.ppermute(close, LON, swaps(0))]
    all_to_all x2, waiting for transfers between devices: 18.2 us -> 16.3 us  [the longest x1 8.23 us: on_device(): got = lax.all_to_all(message, ('z', 'core'), 0, 0)]
  transfers between devices with their start and end apart: 5 -> 5, of which waited for: 5 -> 5; matrix products, arithmetic and copies ran while one was open for 7% -> 6% of each run, Pallas kernels for 0% -> 0%
where the time goes in v5:
time: 70.7 us; the launch traced here: 70.2 us
  starting transfers between devices  37.1 us (52%)
  waiting for transfers between devices  21.5 us (30%)
  Pallas kernels  5.69 us (8%)
  other arithmetic  3.55 us (5%)
  local copies, waits for them, and re-layouts  1.58 us (2%)
  between operations  0.9 us (1%)
    ppermute x1, starting transfers between devices, on_device(): far = lax.ppermute(far, LON, swaps(1))  20.6 us
    all_to_all x1, waiting for transfers between devices, on_device(): got = lax.all_to_all(message, ('z', 'core'), 0, 0)  8.23 us
    all_to_all x1, waiting for transfers between devices, on_device(): got = lax.all_to_all(message, ('y', 'xh', 'xl'), 0, 0)  8.05 us
    all_to_all x1, starting transfers between devices, on_device(): halo = lax.all_to_all(slots, LAT, 0, 0)  5.34 us
    all_to_all x1, starting transfers between devices, on_device(): got = lax.all_to_all(message, ('y', 'xh', 'xl'), 0, 0)  4.86 us
    all_to_all x1, starting transfers between devices, on_device(): got = lax.all_to_all(message, ('z', 'core'), 0, 0)  4.31 us
    mul x2, other arithmetic, face_flux(): return speed * weno_upwind(a, b, c, d, e)  2.61 us
    ppermute x1, waiting for transfers between devices, on_device(): close = lax.ppermute(close, LON, swaps(0))  2.59 us
  transfers between devices with their start and end apart: 5, of which 5 were waited for; matrix products, arithmetic and copies ran while one was open for 6% of the time, Pallas kernels for 0%

profile of v5, /device:TPU:1, one launch (start us, length us, event | category | flops | bytes accessed | tf_op | source)
XLA Modules:
  0.0 70.2 jit_solution(9719074286677716282)
XLA Ops:
  0.6 0.0 copy-start.5
  0.6 0.0 copy-start
  0.7 0.0 copy-start.1
  0.7 0.0 copy-start.2
  0.7 0.0 copy-start.3
  0.7 1.5 %pack.1 = (f32[80,384]{1,0:T(8,128)S(1)}, f32[80,384]{1,0:T(8,128)S(1)}, f32[4,16,384]{2,1,0:T(8,128)S(1)}, f32[40,128]{1,0:T(8,128)S(1)}, s32[2,8,128]{2,1,0:T(8,128)S(1)}) custom-call(f32[8,16,384]{2,1,0:T(8,128)} %t.1, f32[8,16,384]{2,1,0:T(8,128)} %s.1, f32[8,16,384]{2,1,0:T(8,128)} %u.1, f32[8,16,384]{2,1,0:T(8,128)} %v.1, f32[16,384]{1,0:T(8,128)} %elev.1, ...), custom_call_target="tpu_custom_call" | custom-call | tf_op jit(solution)/shard_map/pack/pallas_call | solution.py:322
  2.2 0.0 copy-start.4
  2.2 20.6 %collective-permute-start = (f32[80,384]{1,0:T(8,128)S(1)}, f32[80,384]{1,0:T(8,128)S(1)}, u32[]{:S(2)}, u32[]{:S(2)}) collective-permute-start(f32[80,384]{1,0:T(8,128)S(1)} %get-tuple-element.18), channel_id=1, source_target_pairs={{4,8},{8,4},{12,16},{16,12},{20,24},{24,20},{28,32},{32,28},{36,40... | collective-permute-start | bytes 368648 | tf_op jit(solution)/shard_map/ppermute | solution.py:340
  22.9 1.9 %collective-permute-start.1 = (f32[80,384]{1,0:T(8,128)S(1)}, f32[80,384]{1,0:T(8,128)S(1)}, u32[]{:S(2)}, u32[]{:S(2)}) collective-permute-start(f32[80,384]{1,0:T(8,128)S(1)} %get-tuple-element.19), channel_id=1, source_target_pairs={{0,4},{4,0},{8,12},{12,8},{16,20},{20,16},{24,28},{28,24},{32,36},... | collective-permute-start | bytes 368648 | tf_op jit(solution)/shard_map/ppermute | solution.py:341
  24.8 0.0 copy-done.5
  24.8 0.0 copy-done
  24.8 0.0 copy-done.1
  24.8 0.0 copy-done.2
  24.9 0.0 copy-done.3
  24.9 0.0 copy-done.4
  24.9 0.1 fusion.20
  25.0 0.9 %collective-permute-done.far = f32[80,384]{1,0:T(8,128)S(1)} collective-permute-done((f32[80,384]{1,0:T(8,128)S(1)}, f32[80,384]{1,0:T(8,128)S(1)}, u32[]{:S(2)}, u32[]{:S(2)}) %collective-permute-start) | collective-permute-done | bytes 122912 | tf_op jit(solution)/shard_map/ppermute | solution.py:340
  25.9 2.6 %collective-permute-done.1.close = f32[80,384]{1,0:T(8,128)S(1)} collective-permute-done((f32[80,384]{1,0:T(8,128)S(1)}, f32[80,384]{1,0:T(8,128)S(1)}, u32[]{:S(2)}, u32[]{:S(2)}) %collective-permute-start.1) | collective-permute-done | bytes 122912 | tf_op jit(solution)/shard_map/ppermute | solution.py:341
  28.6 0.1 broadcast_compare_fusion
  28.7 0.9 %widen.1 = (f32[4,32,384]{2,1,0:T(8,128)S(1)}, f32[4,16,128]{2,1,0:T(8,128)}) custom-call(f32[80,384]{1,0:T(8,128)S(1)} %collective-permute-done.far, f32[80,384]{1,0:T(8,128)S(1)} %collective-permute-done.1.close, f32[4,16,384]{2,1,0:T(8,128)S(1)} %get-tuple-element.20.fields, f32[40,128]{1,0:T(8,128)S(1)} %get-tuple-element.21.edges), custom_call_target="tpu_custom_call" | custom-call | tf_op jit(solution)/shard_map/widen/pallas_call | solution.py:342
  29.6 5.3 %all-to-all-start = ((f32[4,16,128]{2,1,0:T(8,128)}), f32[4,16,128]{2,1,0:T(8,128)S(1)}, u32[]{:S(2)}, u32[]{:S(2)}) async-start(f32[4,16,128]{2,1,0:T(8,128)} %get-tuple-element.23), calls=%async_computation | async-start | bytes 65536 | tf_op jit(solution)/shard_map/all_to_all | solution.py:347
  34.9 0.1 maximum_maximum_fusion
  35.0 1.4 %add_multiply_fusion = f32[2,8,17,384]{3,2,1,0:T(8,128)S(1)} fusion(f32[2,8,19,384]{3,2,1,0:T(8,128)S(1)} %get-tuple-element.37, f32[2,8,19,384]{3,2,1,0:T(8,128)S(1)} %get-tuple-element.36, f32[8,17,384]{2,1,0:T(8,128)S(1)} %pad_maximum_fusion.1, pred[8,17,384]{2,1,0:T(8,128)(4,1)S(1)} %broadcast_compare_fusion), kind=kLoop, calls=%fused_computation.28 | loop fusion | flops 6371328 | bytes 3185664 | tf_op jit(solution)/shard_map/mul | solution.py:38
  36.4 1.7 %all-to-all-done.got = f32[4,16,128]{2,1,0:T(8,128)S(1)} async-done(((f32[4,16,128]{2,1,0:T(8,128)}), f32[4,16,128]{2,1,0:T(8,128)S(1)}, u32[]{:S(2)}, u32[]{:S(2)}) %all-to-all-start) | async-done | bytes 32800 | tf_op jit(solution)/shard_map/all_to_all | solution.py:347
  38.1 1.2 %krylov.1 = (f32[4,16,384]{2,1,0:T(8,128)S(1)}, f32[24,4,128]{2,1,0:T(4,128)}, f32[2,8,128]{2,1,0:T(8,128)S(1)}) custom-call(f32[4,32,384]{2,1,0:T(8,128)S(1)} %get-tuple-element.22.wide, f32[4,16,128]{2,1,0:T(8,128)S(1)} %all-to-all-done.got), custom_call_target="tpu_custom_call" | custom-call | tf_op jit(solution)/shard_map/krylov/pallas_call | solution.py:348
  39.3 0.1 reshape.94
  39.4 0.2 copy.20
  39.5 0.1 reshape.93
  39.6 0.2 copy.19
  39.8 0.2 concatenate.48
  40.0 4.3 %all-to-all-start.1 = ((f32[24,4,128]{2,1,0:T(4,128)}), f32[24,4,128]{2,1,0:T(4,128)S(1)}, u32[]{:S(2)}, u32[]{:S(2)}) async-start(f32[24,4,128]{2,1,0:T(4,128)} %get-tuple-element.26), calls=%async_computation.1 | async-start | bytes 98304 | tf_op jit(solution)/shard_map/all_to_all | solution.py:354
  44.3 0.2 maximum_maximum_fusion.2
  44.5 0.1 broadcast_compare_fusion.1
  44.7 1.2 %add_multiply_fusion.1 = f32[2,8,16,385]{3,2,1,0:T(8,128)S(1)} fusion(f32[2,8,16,387]{3,2,1,0:T(8,128)S(1)} %get-tuple-element.39, f32[2,8,16,387]{3,2,1,0:T(8,128)S(1)} %get-tuple-element.38, f32[8,16,385]{2,1,0:T(8,128)S(1)} %get-tuple-element.33, pred[8,16,385]{2,1,0:T(8,128)(4,1)S(1)} %get-tuple-element.32), kind=kLoop, calls=%fused_computation.40 | loop fusion | flops 6012160 | bytes 3006080 | tf_op jit(solution)/shard_map/mul | solution.py:38
  45.9 0.3 fusion.15
  46.2 8.2 %all-to-all-done.1.got = f32[24,4,128]{2,1,0:T(4,128)S(1)} async-done(((f32[24,4,128]{2,1,0:T(4,128)}), f32[24,4,128]{2,1,0:T(4,128)S(1)}, u32[]{:S(2)}, u32[]{:S(2)}) %all-to-all-start.1) | async-done | bytes 49184 | tf_op jit(solution)/shard_map/all_to_all | solution.py:354
  54.4 0.7 relay.1
  55.1 4.9 %all-to-all-start.2 = ((f32[32,4,128]{2,1,0:T(4,128)}), f32[32,4,128]{2,1,0:T(4,128)S(1)}, u32[]{:S(2)}, u32[]{:S(2)}) async-start(f32[32,4,128]{2,1,0:T(4,128)} %relay.1), calls=%async_computation.2 | async-start | bytes 131072 | tf_op jit(solution)/shard_map/all_to_all | solution.py:358
  60.0 0.8 %slice_bitcast_fusion = (f32[8,16,384]{2,1,0:T(8,128)}, f32[8,16,384]{2,1,0:T(8,128)}) fusion(f32[2,8,16,384]{3,2,1,0:T(8,128)S(1)} %fusion.15), kind=kLoop, calls=%fused_computation.55 | loop fusion | bytes 786432 | tf_op jit(solution)/shard_map/squeeze | solution.py:408
  60.7 8.0 %all-to-all-done.2.got = f32[32,4,128]{2,1,0:T(4,128)S(1)} async-done(((f32[32,4,128]{2,1,0:T(4,128)}), f32[32,4,128]{2,1,0:T(4,128)S(1)}, u32[]{:S(2)}, u32[]{:S(2)}) %all-to-all-start.2) | async-done | bytes 65568 | tf_op jit(solution)/shard_map/all_to_all | solution.py:358
  68.8 1.5 %finish.1 = (f32[16,384]{1,0:T(8,128)}, f32[16,384]{1,0:T(8,128)}, f32[8,16,384]{2,1,0:T(8,128)}, f32[8,16,384]{2,1,0:T(8,128)}) custom-call(f32[4,16,384]{2,1,0:T(8,128)S(1)} %get-tuple-element.24.basis_ref, s32[2,8,128]{2,1,0:T(8,128)S(1)} %get-tuple-element.25.source, ...), custom_call_target="tpu_custom_call", output_to_operand_aliasing={{2}: (6, {}), {3}: (7, {})} | custom-call | tf_op jit(solution)/shard_map/finish/pallas_call | solution.py:392
  (10 shorter events, 0.1 us)
Async XLA Ops:
  0.6 24.2 %copy-start.5 = (s32[16,384]{1,0:T(8,128)S(1)}, s32[16,384]{1,0:T(8,128)}, u32[]{:S(2)}) copy-start(s32[16,384]{1,0:T(8,128)} %flag.1) | copy-start | bytes 73732
  0.6 24.2 %copy-start = (f32[8,16,384]{2,1,0:T(8,128)S(1)}, f32[8,16,384]{2,1,0:T(8,128)}, u32[]{:S(2)}) copy-start(f32[8,16,384]{2,1,0:T(8,128)} %t.1) | copy-start | bytes 589828
  0.7 24.2 %copy-start.1 = (f32[8,16,384]{2,1,0:T(8,128)S(1)}, f32[8,16,384]{2,1,0:T(8,128)}, u32[]{:S(2)}) copy-start(f32[8,16,384]{2,1,0:T(8,128)} %s.1) | copy-start | bytes 589828
  0.7 24.2 %copy-start.2 = (f32[8,16,384]{2,1,0:T(8,128)S(1)}, f32[8,16,384]{2,1,0:T(8,128)}, u32[]{:S(2)}) copy-start(f32[8,16,384]{2,1,0:T(8,128)} %u.1) | copy-start | bytes 589828
  0.7 24.2 %copy-start.3 = (f32[8,16,384]{2,1,0:T(8,128)S(1)}, f32[8,16,384]{2,1,0:T(8,128)}, u32[]{:S(2)}) copy-start(f32[8,16,384]{2,1,0:T(8,128)} %v.1) | copy-start | bytes 589828
  2.2 22.6 %copy-start.4 = (s32[16,384]{1,0:T(8,128)S(1)}, s32[16,384]{1,0:T(8,128)}, u32[]{:S(2)}) copy-start(s32[16,384]{1,0:T(8,128)} %depth.1) | copy-start | bytes 73732
  2.2 23.7 %collective-permute-start = (f32[80,384]{1,0:T(8,128)S(1)}, f32[80,384]{1,0:T(8,128)S(1)}, u32[]{:S(2)}, u32[]{:S(2)}) collective-permute-start(f32[80,384]{1,0:T(8,128)S(1)} %get-tuple-element.18), channel_id=1, source_target_pairs={{4,8},{8,4},{12,16},{16,12},{20,24},{24,20},{28,32},{32,28},{36,40... | collective-permute-start | bytes 368648 | tf_op jit(solution)/shard_map/ppermute | solution.py:340
  22.9 5.6 %collective-permute-start.1 = (f32[80,384]{1,0:T(8,128)S(1)}, f32[80,384]{1,0:T(8,128)S(1)}, u32[]{:S(2)}, u32[]{:S(2)}) collective-permute-start(f32[80,384]{1,0:T(8,128)S(1)} %get-tuple-element.19), channel_id=1, source_target_pairs={{0,4},{4,0},{8,12},{12,8},{16,20},{20,16},{24,28},{28,24},{32,36},... | collective-permute-start | bytes 368648 | tf_op jit(solution)/shard_map/ppermute | solution.py:341
  29.6 8.5 %all-to-all-start = ((f32[4,16,128]{2,1,0:T(8,128)}), f32[4,16,128]{2,1,0:T(8,128)S(1)}, u32[]{:S(2)}, u32[]{:S(2)}) async-start(f32[4,16,128]{2,1,0:T(8,128)} %get-tuple-element.23), calls=%async_computation | async-start | bytes 65536 | tf_op jit(solution)/shard_map/all_to_all | solution.py:347
  40.0 14.5 %all-to-all-start.1 = ((f32[24,4,128]{2,1,0:T(4,128)}), f32[24,4,128]{2,1,0:T(4,128)S(1)}, u32[]{:S(2)}, u32[]{:S(2)}) async-start(f32[24,4,128]{2,1,0:T(4,128)} %get-tuple-element.26), calls=%async_computation.1 | async-start | bytes 98304 | tf_op jit(solution)/shard_map/all_to_all | solution.py:354
  55.1 13.7 %all-to-all-start.2 = ((f32[32,4,128]{2,1,0:T(4,128)}), f32[32,4,128]{2,1,0:T(4,128)S(1)}, u32[]{:S(2)}, u32[]{:S(2)}) async-start(f32[32,4,128]{2,1,0:T(4,128)} %relay.1), calls=%async_computation.2 | async-start | bytes 131072 | tf_op jit(solution)/shard_map/all_to_all | solution.py:358

commit v6 on v5

--- a/solution.py
+++ b/solution.py
@@ -102,7 +102,8 @@
 
 
 def pack_kernel(
-    t, s, u, v, elev, flag, depth, fc, far, close, fields, edges, source, up, down, tile
+    t, s, u, v, elev, flag, depth, fc,
+    far, close, far_q, close_q, fields, edges, source, up, down, tile
 ):
     nl, ni, nj = t.shape
     ocean = flag[...] == 1
@@ -145,8 +146,10 @@
     down[73:76] = coupler[:3]
     down[76:80] = zero[:4]
     even = lon_even()
-    far[...] = jnp.where(even, down[...], up[...])
-    close[...] = jnp.where(even, up[...], down[...])
+    far[...] = jnp.where(even, down[64:80], up[64:80])
+    close[...] = jnp.where(even, up[64:80], down[64:80])
+    far_q[...] = jnp.where(even, down[0:64], up[0:64])
+    close_q[...] = jnp.where(even, up[0:64], down[0:64])
     turned = tile[...].T
     edges[0:16] = turned[0:16]
     edges[16:40] = turned[104:128]
@@ -164,7 +167,7 @@
     lat = lat_index()
     even = lon_even()
     blank = jnp.zeros((8, nj), jnp.float32)
-    spans = ((64, 67, 64, 67), (67, 71, 67, 70), (71, 74, 70, 73), (74, 77, 73, 76))
+    spans = ((0, 3, 0, 3), (3, 7, 3, 6), (7, 10, 6, 9), (10, 13, 9, 12))
     for k, (w0, w1, e0, e1) in enumerate(spans):
         wide[k, 0:8] = blank
         wide[k, 24:32] = blank
@@ -319,11 +322,13 @@
         lat = lax.axis_index(LAT)
         last = lat == n_lat - 1
 
-        far, close, fields, edges, source = pl.pallas_call(
+        far, close, far_q, close_q, fields, edges, source = pl.pallas_call(
             pack_kernel,
             out_shape=(
-                vmem(80, nj),
-                vmem(80, nj),
+                vmem(16, nj),
+                vmem(16, nj),
+                vmem(64, nj),
+                vmem(64, nj),
                 vmem(4, ni, nj),
                 vmem(40, 128),
                 pltpu.VMEM((2, 8, 128), jnp.int32),
@@ -344,7 +349,10 @@
             out_shape=(vmem(4, 32, nj), vmem(4, 16, 128)),
             name="widen",
         )(near(far), near(close), near(fields), near(edges))
+        slots, far_q, close_q = lax.optimization_barrier((slots, far_q, close_q))
         halo = lax.all_to_all(slots, LAT, 0, 0)
+        far_q = lax.ppermute(far_q, LON, swaps(1))
+        close_q = lax.ppermute(close_q, LON, swaps(0))
         basis, message, rims = pl.pallas_call(
             krylov_kernel,
             out_shape=(vmem(4, ni, nj), vmem(nz * ncore, 4, 128), vmem(2, 8, 128)),
@@ -367,8 +375,8 @@
             return jnp.stack([tiles[:, 0:3], tiles[:, 3:6]]), tiles[:, 6:7]
 
         even = lon_even()
-        west = jnp.where(even, far, close)
-        east = jnp.where(even, close, far)
+        west = jnp.where(even, far_q, close_q)
+        east = jnp.where(even, close_q, far_q)
         q_west, u_west = sides(west)
         q_east, _ = sides(east)
         north, south = rims[0], rims[1]

time: 70.7 us -> 75.8 us (1.072)
  starting transfers between devices: 37.1 us -> 46.5 us
  waiting for transfers between devices: 21.5 us -> 17 us
    ppermute x0 -> x2, starting transfers between devices: none -> 7.36 us  [the longest x1 5.44 us: on_device(): far_q = lax.ppermute(far_q, LON, swaps(1))]
    all_to_all x1, starting transfers between devices: 4.86 us -> 7.36 us  [on_device(): got = lax.all_to_all(message, ('y', 'xh', 'xl'), 0, 0)]
    all_to_all x1, waiting for transfers between devices: 1.72 us -> 0.01 us  [on_device(): halo = lax.all_to_all(slots, LAT, 0, 0)]
    all_to_all x1, waiting for transfers between devices: 8.23 us -> 6.53 us  [on_device(): got = lax.all_to_all(message, ('z', 'core'), 0, 0)]
    ppermute x1, waiting for transfers between devices: 0.87 us -> 0.01 us  [on_device(): far = lax.ppermute(far, LON, swaps(1))]
  transfers between devices with their start and end apart: 5 -> 7, of which waited for: 5 -> 3; matrix products, arithmetic and copies ran while one was open for 6% -> 7% of each run, Pallas kernels for 0% -> 2%
where the time goes in v6:
time: 75.8 us; the launch traced here: 75.3 us
  starting transfers between devices  46.5 us (61%)
  waiting for transfers between devices  17 us (22%)
  Pallas kernels  5.69 us (8%)
  other arithmetic  3.57 us (5%)
  local copies, waits for them, and re-layouts  1.57 us (2%)
  between operations  0.93 us (1%)
    ppermute x1, starting transfers between devices, on_device(): far = lax.ppermute(far, LON, swaps(1))  20.6 us
    all_to_all x1, waiting for transfers between devices, on_device(): got = lax.all_to_all(message, ('y', 'xh', 'xl'), 0, 0)  8.05 us
    all_to_all x1, starting transfers between devices, on_device(): got = lax.all_to_all(message, ('y', 'xh', 'xl'), 0, 0)  7.36 us
    all_to_all x1, waiting for transfers between devices, on_device(): got = lax.all_to_all(message, ('z', 'core'), 0, 0)  6.53 us
    ppermute x1, starting transfers between devices, on_device(): far_q = lax.ppermute(far_q, LON, swaps(1))  5.44 us
    all_to_all x1, starting transfers between devices, on_device(): halo = lax.all_to_all(slots, LAT, 0, 0)  5.34 us
    all_to_all x1, starting transfers between devices, on_device(): got = lax.all_to_all(message, ('z', 'core'), 0, 0)  3.88 us
    mul x2, other arithmetic, face_flux(): return speed * weno_upwind(a, b, c, d, e)  2.61 us
  transfers between devices with their start and end apart: 7, of which 3 were waited for; matrix products, arithmetic and copies ran while one was open for 7% of the time, Pallas kernels for 2%

profile of v6, /device:TPU:1, one launch (start us, length us, event | category | flops | bytes accessed | tf_op | source)
XLA Modules:
  0.0 75.3 jit_solution(7355479904905785784)
XLA Ops:
  0.6 0.0 copy-start.5
  0.6 0.0 copy-start
  0.7 0.0 copy-start.1
  0.7 0.0 copy-start.2
  0.7 0.0 copy-start.3
  0.7 1.5 %pack.1 = (f32[16,384]{1,0:T(8,128)S(1)}, f32[16,384]{1,0:T(8,128)S(1)}, f32[64,384]{1,0:T(8,128)S(1)}, f32[64,384]{1,0:T(8,128)S(1)}, f32[4,16,384]{2,1,0:T(8,1...) custom-call(f32[8,16,384]{2,1,0:T(8,128)} %t.1, f32[8,16,384]{2,1,0:T(8,128)} %s.1, f32[8,16,384]{2,1,0:T(8,128)} %u.1, ...), custom_call_target="tpu_custom_call" | custom-call | tf_op jit(solution)/shard_map/pack/pallas_call | solution.py:325
  2.2 0.0 copy-start.4
  2.2 20.6 %collective-permute-start = (f32[16,384]{1,0:T(8,128)S(1)}, f32[16,384]{1,0:T(8,128)S(1)}, u32[]{:S(2)}, u32[]{:S(2)}) collective-permute-start(f32[16,384]{1,0:T(8,128)S(1)} %get-tuple-element.23), channel_id=1, source_target_pairs={{4,8},{8,4},{12,16},{16,12},{20,24},{24,20},{28,32},{32,28},{36,40... | collective-permute-start | bytes 73736 | tf_op jit(solution)/shard_map/ppermute | solution.py:345
  22.9 1.9 %collective-permute-start.1 = (f32[16,384]{1,0:T(8,128)S(1)}, f32[16,384]{1,0:T(8,128)S(1)}, u32[]{:S(2)}, u32[]{:S(2)}) collective-permute-start(f32[16,384]{1,0:T(8,128)S(1)} %get-tuple-element.24), channel_id=1, source_target_pairs={{0,4},{4,0},{8,12},{12,8},{16,20},{20,16},{24,28},{28,24},{32,36},... | collective-permute-start | bytes 73736 | tf_op jit(solution)/shard_map/ppermute | solution.py:346
  24.8 0.0 copy-done.5
  24.8 0.0 copy-done
  24.8 0.0 copy-done.1
  24.8 0.0 copy-done.2
  24.9 0.0 copy-done.3
  24.9 0.0 copy-done.4
  24.9 0.1 fusion.20
  25.0 0.0 collective-permute-done.far
  25.0 2.4 %collective-permute-done.1.close = f32[16,384]{1,0:T(8,128)S(1)} collective-permute-done((f32[16,384]{1,0:T(8,128)S(1)}, f32[16,384]{1,0:T(8,128)S(1)}, u32[]{:S(2)}, u32[]{:S(2)}) %collective-permute-start.1) | collective-permute-done | bytes 24608 | tf_op jit(solution)/shard_map/ppermute | solution.py:346
  27.4 0.9 %widen.1 = (f32[4,32,384]{2,1,0:T(8,128)S(1)}, f32[4,16,128]{2,1,0:T(8,128)}) custom-call(f32[16,384]{1,0:T(8,128)S(1)} %collective-permute-done.far, f32[16,384]{1,0:T(8,128)S(1)} %collective-permute-done.1.close, f32[4,16,384]{2,1,0:T(8,128)S(1)} %get-tuple-element.25.fields, f32[40,128]{1,0:T(8,128)S(1)} %get-tuple-element.26.edges), custom_call_target="tpu_custom_call" | custom-call | tf_op jit(solution)/shard_map/widen/pallas_call | solution.py:347
  28.3 5.3 %all-to-all-start = ((f32[4,16,128]{2,1,0:T(8,128)}), f32[4,16,128]{2,1,0:T(8,128)S(1)}, u32[]{:S(2)}, u32[]{:S(2)}) async-start(f32[4,16,128]{2,1,0:T(8,128)} %get-tuple-element.31), calls=%async_computation | async-start | bytes 65536 | tf_op jit(solution)/shard_map/all_to_all | solution.py:353
  33.7 5.4 %collective-permute-start.2 = (f32[64,384]{1,0:T(8,128)S(1)}, f32[64,384]{1,0:T(8,128)S(1)}, u32[]{:S(2)}, u32[]{:S(2)}) collective-permute-start(f32[64,384]{1,0:T(8,128)S(1)} %get-tuple-element.35), channel_id=1, source_target_pairs={{4,8},{8,4},{12,16},{16,12},{20,24},{24,20},{28,32},{32,28},{36,40... | collective-permute-start | bytes 294920 | tf_op jit(solution)/shard_map/ppermute | solution.py:354
  39.1 1.9 %collective-permute-start.3 = (f32[64,384]{1,0:T(8,128)S(1)}, f32[64,384]{1,0:T(8,128)S(1)}, u32[]{:S(2)}, u32[]{:S(2)}) collective-permute-start(f32[64,384]{1,0:T(8,128)S(1)} %get-tuple-element.36), channel_id=1, source_target_pairs={{0,4},{4,0},{8,12},{12,8},{16,20},{20,16},{24,28},{28,24},{32,36},... | collective-permute-start | bytes 294920 | tf_op jit(solution)/shard_map/ppermute | solution.py:355
  41.1 0.0 all-to-all-done.got
  41.1 1.2 %krylov.1 = (f32[4,16,384]{2,1,0:T(8,128)S(1)}, f32[24,4,128]{2,1,0:T(4,128)}, f32[2,8,128]{2,1,0:T(8,128)S(1)}) custom-call(f32[4,32,384]{2,1,0:T(8,128)S(1)} %get-tuple-element.27.wide, f32[4,16,128]{2,1,0:T(8,128)S(1)} %all-to-all-done.got), custom_call_target="tpu_custom_call" | custom-call | tf_op jit(solution)/shard_map/krylov/pallas_call | solution.py:356
  42.3 0.1 reshape.94
  42.3 0.2 copy.20
  42.5 0.1 reshape.93
  42.6 0.2 copy.19
  42.7 0.2 concatenate.48
  43.0 3.9 %all-to-all-start.1 = ((f32[24,4,128]{2,1,0:T(4,128)}), f32[24,4,128]{2,1,0:T(4,128)S(1)}, u32[]{:S(2)}, u32[]{:S(2)}) async-start(f32[24,4,128]{2,1,0:T(4,128)} %get-tuple-element.34), calls=%async_computation.1 | async-start | bytes 98304 | tf_op jit(solution)/shard_map/all_to_all | solution.py:362
  46.9 0.1 broadcast_compare_fusion.1
  47.0 0.2 maximum_maximum_fusion.2
  47.2 1.2 %add_multiply_fusion.1 = f32[2,8,16,385]{3,2,1,0:T(8,128)S(1)} fusion(f32[2,8,16,387]{3,2,1,0:T(8,128)S(1)} %get-tuple-element.49, f32[2,8,16,387]{3,2,1,0:T(8,128)S(1)} %get-tuple-element.48, f32[8,16,385]{2,1,0:T(8,128)S(1)} %get-tuple-element.43, pred[8,16,385]{2,1,0:T(8,128)(4,1)S(1)} %get-tuple-element.42), kind=kLoop, calls=%fused_computation.40 | loop fusion | flops 6012160 | bytes 3006080 | tf_op jit(solution)/shard_map/mul | solution.py:38
  48.5 0.0 collective-permute-done.2
  48.5 0.0 collective-permute-done.3
  48.6 0.1 broadcast_compare_fusion
  48.7 0.1 maximum_maximum_fusion
  48.8 1.4 %add_multiply_fusion = f32[2,8,17,384]{3,2,1,0:T(8,128)S(1)} fusion(f32[2,8,19,384]{3,2,1,0:T(8,128)S(1)} %get-tuple-element.47, f32[2,8,19,384]{3,2,1,0:T(8,128)S(1)} %get-tuple-element.46, f32[8,17,384]{2,1,0:T(8,128)S(1)} %pad_maximum_fusion.1, pred[8,17,384]{2,1,0:T(8,128)(4,1)S(1)} %broadcast_compare_fusion), kind=kLoop, calls=%fused_computation.28 | loop fusion | flops 6371328 | bytes 3185664 | tf_op jit(solution)/shard_map/mul | solution.py:38
  50.2 0.3 fusion.15
  50.5 6.5 %all-to-all-done.1.got = f32[24,4,128]{2,1,0:T(4,128)S(1)} async-done(((f32[24,4,128]{2,1,0:T(4,128)}), f32[24,4,128]{2,1,0:T(4,128)S(1)}, u32[]{:S(2)}, u32[]{:S(2)}) %all-to-all-start.1) | async-done | bytes 49184 | tf_op jit(solution)/shard_map/all_to_all | solution.py:362
  57.0 0.7 relay.1
  57.6 7.4 %all-to-all-start.2 = ((f32[32,4,128]{2,1,0:T(4,128)}), f32[32,4,128]{2,1,0:T(4,128)S(1)}, u32[]{:S(2)}, u32[]{:S(2)}) async-start(f32[32,4,128]{2,1,0:T(4,128)} %relay.1), calls=%async_computation.2 | async-start | bytes 131072 | tf_op jit(solution)/shard_map/all_to_all | solution.py:366
  65.0 0.8 %slice_bitcast_fusion = (f32[8,16,384]{2,1,0:T(8,128)}, f32[8,16,384]{2,1,0:T(8,128)}) fusion(f32[2,8,16,384]{3,2,1,0:T(8,128)S(1)} %fusion.15), kind=kLoop, calls=%fused_computation.55 | loop fusion | bytes 786432 | tf_op jit(solution)/shard_map/squeeze | solution.py:416
  65.8 8.0 %all-to-all-done.2.got = f32[32,4,128]{2,1,0:T(4,128)S(1)} async-done(((f32[32,4,128]{2,1,0:T(4,128)}), f32[32,4,128]{2,1,0:T(4,128)S(1)}, u32[]{:S(2)}, u32[]{:S(2)}) %all-to-all-start.2) | async-done | bytes 65568 | tf_op jit(solution)/shard_map/all_to_all | solution.py:366
  73.8 1.5 %finish.1 = (f32[16,384]{1,0:T(8,128)}, f32[16,384]{1,0:T(8,128)}, f32[8,16,384]{2,1,0:T(8,128)}, f32[8,16,384]{2,1,0:T(8,128)}) custom-call(f32[4,16,384]{2,1,0:T(8,128)S(1)} %get-tuple-element.32.basis_ref, s32[2,8,128]{2,1,0:T(8,128)S(1)} %get-tuple-element.33.source, ...), custom_call_target="tpu_custom_call", output_to_operand_aliasing={{2}: (6, {}), {3}: (7, {})} | custom-call | tf_op jit(solution)/shard_map/finish/pallas_call | solution.py:400
  (10 shorter events, 0.2 us)
Async XLA Ops:
  0.6 24.2 %copy-start.5 = (s32[16,384]{1,0:T(8,128)S(1)}, s32[16,384]{1,0:T(8,128)}, u32[]{:S(2)}) copy-start(s32[16,384]{1,0:T(8,128)} %flag.1) | copy-start | bytes 73732
  0.6 24.2 %copy-start = (f32[8,16,384]{2,1,0:T(8,128)S(1)}, f32[8,16,384]{2,1,0:T(8,128)}, u32[]{:S(2)}) copy-start(f32[8,16,384]{2,1,0:T(8,128)} %t.1) | copy-start | bytes 589828
  0.7 24.2 %copy-start.1 = (f32[8,16,384]{2,1,0:T(8,128)S(1)}, f32[8,16,384]{2,1,0:T(8,128)}, u32[]{:S(2)}) copy-start(f32[8,16,384]{2,1,0:T(8,128)} %s.1) | copy-start | bytes 589828
  0.7 24.2 %copy-start.2 = (f32[8,16,384]{2,1,0:T(8,128)S(1)}, f32[8,16,384]{2,1,0:T(8,128)}, u32[]{:S(2)}) copy-start(f32[8,16,384]{2,1,0:T(8,128)} %u.1) | copy-start | bytes 589828
  0.7 24.2 %copy-start.3 = (f32[8,16,384]{2,1,0:T(8,128)S(1)}, f32[8,16,384]{2,1,0:T(8,128)}, u32[]{:S(2)}) copy-start(f32[8,16,384]{2,1,0:T(8,128)} %v.1) | copy-start | bytes 589828
  2.2 22.6 %copy-start.4 = (s32[16,384]{1,0:T(8,128)S(1)}, s32[16,384]{1,0:T(8,128)}, u32[]{:S(2)}) copy-start(s32[16,384]{1,0:T(8,128)} %depth.1) | copy-start | bytes 73732
  2.2 22.8 %collective-permute-start = (f32[16,384]{1,0:T(8,128)S(1)}, f32[16,384]{1,0:T(8,128)S(1)}, u32[]{:S(2)}, u32[]{:S(2)}) collective-permute-start(f32[16,384]{1,0:T(8,128)S(1)} %get-tuple-element.23), channel_id=1, source_target_pairs={{4,8},{8,4},{12,16},{16,12},{20,24},{24,20},{28,32},{32,28},{36,40... | collective-permute-start | bytes 73736 | tf_op jit(solution)/shard_map/ppermute | solution.py:345
  22.9 4.6 %collective-permute-start.1 = (f32[16,384]{1,0:T(8,128)S(1)}, f32[16,384]{1,0:T(8,128)S(1)}, u32[]{:S(2)}, u32[]{:S(2)}) collective-permute-start(f32[16,384]{1,0:T(8,128)S(1)} %get-tuple-element.24), channel_id=1, source_target_pairs={{0,4},{4,0},{8,12},{12,8},{16,20},{20,16},{24,28},{28,24},{32,36},... | collective-permute-start | bytes 73736 | tf_op jit(solution)/shard_map/ppermute | solution.py:346
  28.3 12.7 %all-to-all-start = ((f32[4,16,128]{2,1,0:T(8,128)}), f32[4,16,128]{2,1,0:T(8,128)S(1)}, u32[]{:S(2)}, u32[]{:S(2)}) async-start(f32[4,16,128]{2,1,0:T(8,128)} %get-tuple-element.31), calls=%async_computation | async-start | bytes 65536 | tf_op jit(solution)/shard_map/all_to_all | solution.py:353
  33.7 14.8 %collective-permute-start.2 = (f32[64,384]{1,0:T(8,128)S(1)}, f32[64,384]{1,0:T(8,128)S(1)}, u32[]{:S(2)}, u32[]{:S(2)}) collective-permute-start(f32[64,384]{1,0:T(8,128)S(1)} %get-tuple-element.35), channel_id=1, source_target_pairs={{4,8},{8,4},{12,16},{16,12},{20,24},{24,20},{28,32},{32,28},{36,40... | collective-permute-start | bytes 294920 | tf_op jit(solution)/shard_map/ppermute | solution.py:354
  39.1 9.3 %collective-permute-start.3 = (f32[64,384]{1,0:T(8,128)S(1)}, f32[64,384]{1,0:T(8,128)S(1)}, u32[]{:S(2)}, u32[]{:S(2)}) collective-permute-start(f32[64,384]{1,0:T(8,128)S(1)} %get-tuple-element.36), channel_id=1, source_target_pairs={{0,4},{4,0},{8,12},{12,8},{16,20},{20,16},{24,28},{28,24},{32,36},... | collective-permute-start | bytes 294920 | tf_op jit(solution)/shard_map/ppermute | solution.py:355
  43.0 14.0 %all-to-all-start.1 = ((f32[24,4,128]{2,1,0:T(4,128)}), f32[24,4,128]{2,1,0:T(4,128)S(1)}, u32[]{:S(2)}, u32[]{:S(2)}) async-start(f32[24,4,128]{2,1,0:T(4,128)} %get-tuple-element.34), calls=%async_computation.1 | async-start | bytes 98304 | tf_op jit(solution)/shard_map/all_to_all | solution.py:362
  57.6 16.2 %all-to-all-start.2 = ((f32[32,4,128]{2,1,0:T(4,128)}), f32[32,4,128]{2,1,0:T(4,128)S(1)}, u32[]{:S(2)}, u32[]{:S(2)}) async-start(f32[32,4,128]{2,1,0:T(4,128)} %relay.1), calls=%async_computation.2 | async-start | bytes 131072 | tf_op jit(solution)/shard_map/all_to_all | solution.py:366

commit v7 on v5

--- a/solution.py
+++ b/solution.py
@@ -102,7 +102,7 @@
 
 
 def pack_kernel(
-    t, s, u, v, elev, flag, depth, fc, far, close, fields, edges, source, up, down, tile
+    t, s, u, v, elev, flag, depth, fc, far, close, fields, edges, source, slots, up, down, tile
 ):
     nl, ni, nj = t.shape
     ocean = flag[...] == 1
@@ -134,22 +134,28 @@
     coupler = 2.0 * jnp.sqrt((wet * flag[...]).astype(jnp.float32) / nl)
     for k, f in enumerate((part, em, nm, coupler)):
         fields[k] = f
-    up[64:67] = part[ni - 3 :]
-    up[67:71] = em[ni - 4 :]
-    up[71:74] = nm[ni - 3 :]
-    up[74:77] = coupler[ni - 3 :]
-    up[77:80] = zero[:3]
-    down[64:67] = part[:3]
-    down[67:70] = em[:3]
-    down[70:73] = nm[:3]
-    down[73:76] = coupler[:3]
-    down[76:80] = zero[:4]
     even = lon_even()
     far[...] = jnp.where(even, down[...], up[...])
     close[...] = jnp.where(even, up[...], down[...])
     turned = tile[...].T
     edges[0:16] = turned[0:16]
     edges[16:40] = turned[104:128]
+    for k, f in enumerate((part, em, nm, coupler)):
+        tile[ni * k : ni * (k + 1)] = jnp.where(lane < 64, f[:, :128], f[:, nj - 128 :])
+    columns = tile[...].T
+    lat = lat_index()
+    none = jnp.zeros((2, 128), jnp.float32)
+    t_end, s_end, v_end = turned[125:128], turned[117:120], turned[111:112]
+    fold = [jnp.concatenate([turned[k : k + 1] for k in (n, n - 1, n - 2)]) for n in (127, 119)]
+    fold = mirror16(jnp.concatenate(fold + [none], axis=0))
+    north = jnp.concatenate([t_end, s_end, v_end, none[:1]], axis=0)
+    south = jnp.concatenate([turned[0:3], turned[8:11], none], axis=0)
+    for p in range(4):
+        ahead = p > lat
+        slots[p, 0:8] = jnp.where(ahead, north, south)
+        slots[p, 8:12] = jnp.where(ahead, columns[124:128], columns[0:4])
+        slots[p, 12:15] = fold[0:3] if p < 2 else fold[3:6]
+        slots[p, 15:16] = none[:1]
     block = lax.shift_right_logical(jnp.broadcast_to(fc[0:1, 0:1], (8, 128)), 4)
     row = jnp.zeros((8, 128), jnp.int32)
     nz = lax.axis_size("z")
@@ -159,50 +165,56 @@
     source[1] = row
 
 
-def widen_kernel(far, close, fields, edges, wide, slots):
+def widen_kernel(got, fields, far_q, close_q, far, close, beyond, rims, tile, up, down):
     _, ni, nj = fields.shape
     lat = lat_index()
     even = lon_even()
-    blank = jnp.zeros((8, nj), jnp.float32)
-    spans = ((64, 67, 64, 67), (67, 71, 67, 70), (71, 74, 70, 73), (74, 77, 73, 76))
-    for k, (w0, w1, e0, e1) in enumerate(spans):
-        wide[k, 0:8] = blank
-        wide[k, 24:32] = blank
-        wide[k, 8 - (w1 - w0) : 8] = jnp.where(even, far[w0:w1], close[w0:w1])
-        wide[k, 8 : 8 + ni] = fields[k]
-        wide[k, 24 : 24 + (e1 - e0)] = jnp.where(even, close[e0:e1], far[e0:e1])
-    lane = lax.broadcasted_iota(jnp.int32, (4, 32, 128), 2)
-    both = jnp.where(lane < 64, wide[:, :, 0:128], wide[:, :, nj - 128 : nj])
-    turned = both.reshape(128, 128).T
-    none = jnp.zeros((4, 128), jnp.float32)
-    fold = jnp.concatenate(
-        [edges[k : k + 1] for k in (39, 38, 37, 31, 30, 29)] + [none[:2]], axis=0
-    )
-    fold = mirror16(fold)
-    north = jnp.concatenate(
-        [edges[37:40], edges[29:32], edges[23:24], none[:1]], axis=0
-    )
-    south = jnp.concatenate([edges[0:3], edges[8:11], none[:2]], axis=0)
-    for p in range(4):
-        ahead = p > lat
-        slots[p, 0:8] = jnp.where(ahead, north, south)
-        slots[p, 8:12] = jnp.where(ahead, turned[124:128], turned[0:4])
-        slots[p, 12:15] = fold[0:3] if p < 2 else fold[3:6]
-        slots[p, 15:16] = none[:1]
-
-
-def krylov_kernel(wide, got, basis_ref, message, rims, tile):
-    ni, nj = basis_ref.shape[1:]
-    lat = lat_index()
-    tile[...] = jnp.zeros((128, 128), jnp.float32)
     north = jnp.where(lat < 3, got[jnp.minimum(lat + 1, 3)], 0.0)
     south = jnp.where(lat > 0, got[jnp.maximum(lat - 1, 0)], 0.0)
     rims[0] = north[0:8]
     rims[1] = south[0:8]
+    tile[...] = jnp.zeros((128, 128), jnp.float32)
     tile[0:4] = north[8:12]
     tile[124:128] = south[8:12]
-    beyond = tile[...].T.reshape(4, 32, 128)
-    part, em, nm, cpl = (jnp.concatenate([wide[k], beyond[k]], axis=1) for k in range(4))
+    beyond[...] = tile[...].T[0 : 4 * ni].reshape(4, ni, 128)
+    far[0:64] = far_q[...]
+    close[0:64] = close_q[...]
+    at = 0
+    for k, n in enumerate((3, 4, 3, 3)):
+        up[at : at + n, 0:nj] = fields[k, ni - n : ni]
+        up[at : at + n, nj:] = beyond[k, ni - n : ni]
+        down[at : at + n, 0:nj] = fields[k, 0:n]
+        down[at : at + n, nj:] = beyond[k, 0:n]
+        at += n
+    up[13:16] = jnp.zeros((3, nj + 128), jnp.float32)
+    down[13:16] = jnp.zeros((3, nj + 128), jnp.float32)
+    for out, first, second in ((far, down, up), (close, up, down)):
+        rows = jnp.where(even, first[...], second[...])
+        out[64:80] = rows[:, 0:nj]
+        out[80:88, 0:128] = rows[0:8, nj:]
+        out[80:88, 128:256] = rows[8:16, nj:]
+        out[80:88, 256:384] = jnp.zeros((8, 128), jnp.float32)
+
+
+def krylov_kernel(got, fields, beyond, far, close, basis_ref, message, wide, west, east):
+    _, ni, nj = fields.shape
+    even = lon_even()
+    for out, first, second in ((west, far, close), (east, close, far)):
+        out[:, 0:nj] = jnp.where(even, first[64:80], second[64:80])
+        tail = jnp.where(even, first[80:88], second[80:88])
+        out[0:8, nj:] = tail[:, 0:128]
+        out[8:16, nj:] = tail[:, 128:256]
+    blank = jnp.zeros((8, nj + 128), jnp.float32)
+    at = 0
+    for k, n in enumerate((3, 4, 3, 3)):
+        wide[k, 0:8] = blank
+        wide[k, 24:32] = blank
+        wide[k, 8 - n : 8] = west[at : at + n]
+        wide[k, 24 : 24 + n] = east[at : at + n]
+        wide[k, 8:24, 0:nj] = fields[k]
+        wide[k, 8:24, nj:] = beyond[k]
+        at += n
+    part, em, nm, cpl = (wide[k] for k in range(4))
     rows, lanes = part.shape
     b0 = part + pltpu.roll(em, 1, 0) + pltpu.roll(nm, 1, 1)
 
@@ -319,18 +331,27 @@
         lat = lax.axis_index(LAT)
         last = lat == n_lat - 1
 
-        far, close, fields, edges, source = pl.pallas_call(
+        far, close, fields, edges, source, slots = pl.pallas_call(
             pack_kernel,
             out_shape=(
-                vmem(80, nj),
-                vmem(80, nj),
+                vmem(64, nj),
+                vmem(64, nj),
                 vmem(4, ni, nj),
                 vmem(40, 128),
                 pltpu.VMEM((2, 8, 128), jnp.int32),
+                vmem(4, 16, 128),
             ),
-            scratch_shapes=[vmem(80, nj), vmem(80, nj), vmem(128, 128)],
+            scratch_shapes=[vmem(64, nj), vmem(64, nj), vmem(128, 128)],
             name="pack",
         )(t, s, u, v, elev, flag, depth, fc.reshape(1, ni))
+        halo = lax.all_to_all(slots, LAT, 0, 0)
+        far, close, beyond, rims = pl.pallas_call(
+            widen_kernel,
+            out_shape=(vmem(88, nj), vmem(88, nj), vmem(4, ni, 128), vmem(2, 8, 128)),
+            scratch_shapes=[vmem(128, 128), vmem(16, nj + 128), vmem(16, nj + 128)],
+            name="widen",
+        )(near(halo), near(fields), near(far), near(close))
+
         def swaps(first):
             pairs = []
             for i in range(first, n_lon, 2):
@@ -339,18 +360,12 @@
 
         far = lax.ppermute(far, LON, swaps(1))
         close = lax.ppermute(close, LON, swaps(0))
-        wide, slots = pl.pallas_call(
-            widen_kernel,
-            out_shape=(vmem(4, 32, nj), vmem(4, 16, 128)),
-            name="widen",
-        )(near(far), near(close), near(fields), near(edges))
-        halo = lax.all_to_all(slots, LAT, 0, 0)
-        basis, message, rims = pl.pallas_call(
+        basis, message = pl.pallas_call(
             krylov_kernel,
-            out_shape=(vmem(4, ni, nj), vmem(nz * ncore, 4, 128), vmem(2, 8, 128)),
-            scratch_shapes=[vmem(128, 128)],
+            out_shape=(vmem(4, ni, nj), vmem(nz * ncore, 4, 128)),
+            scratch_shapes=[vmem(4, 32, nj + 128), vmem(16, nj + 128), vmem(16, nj + 128)],
             name="krylov",
-        )(near(wide), near(halo))
+        )(near(halo), near(fields), near(beyond), near(far), near(close))
         got = lax.all_to_all(message, ("z", "core"), 0, 0)
         message = pl.pallas_call(
             relay_kernel, out_shape=vmem(ny * nxh * nxl, 4, 128), name="relay"

time: 70.7 us -> 70.1 us (level)
  waiting for transfers between devices: 21.5 us -> 20.2 us
    ppermute x1, starting transfers between devices: 20.6 us -> 10.7 us  [on_device(): far = lax.ppermute(far, LON, swaps(1))]
    all_to_all x1, starting transfers between devices: 5.34 us -> 13.9 us  [on_device(): halo = lax.all_to_all(slots, LAT, 0, 0)]
    all_to_all x1, starting transfers between devices: 4.31 us -> 5.73 us  [on_device(): got = lax.all_to_all(message, ('z', 'core'), 0, 0)]
    ppermute x1, waiting for transfers between devices: 2.59 us -> 1.49 us  [on_device(): close = lax.ppermute(close, LON, swaps(0))]
    ppermute x1, waiting for transfers between devices: 0.87 us -> 0.01 us  [on_device(): far = lax.ppermute(far, LON, swaps(1))]
  transfers between devices with their start and end apart: 5 -> 5, of which waited for: 5 -> 4; matrix products, arithmetic and copies ran while one was open for 6% -> 7% of each run, Pallas kernels for 0% -> 0%
where the time goes in v7:
time: 70.1 us; the launch traced here: 69.6 us
  starting transfers between devices  37.1 us (53%)
  waiting for transfers between devices  20.2 us (29%)
  Pallas kernels  5.7 us (8%)
  other arithmetic  3.55 us (5%)
  local copies, waits for them, and re-layouts  2.25 us (3%)
  between operations  0.88 us (1%)
    all_to_all x1, starting transfers between devices, on_device(): halo = lax.all_to_all(slots, LAT, 0, 0)  13.9 us
    ppermute x1, starting transfers between devices, on_device(): far = lax.ppermute(far, LON, swaps(1))  10.7 us
    all_to_all x1, waiting for transfers between devices, on_device(): got = lax.all_to_all(message, ('z', 'core'), 0, 0)  8.34 us
    all_to_all x1, waiting for transfers between devices, on_device(): got = lax.all_to_all(message, ('y', 'xh', 'xl'), 0, 0)  8.05 us
    all_to_all x1, starting transfers between devices, on_device(): got = lax.all_to_all(message, ('z', 'core'), 0, 0)  5.73 us
    all_to_all x1, starting transfers between devices, on_device(): got = lax.all_to_all(message, ('y', 'xh', 'xl'), 0, 0)  4.89 us
    mul x2, other arithmetic, face_flux(): return speed * weno_upwind(a, b, c, d, e)  2.61 us
    pallas_call x1, Pallas kernels, on_device(): pl.pallas_call(pack_kernel, out_shape=(vmem(64, nj), vmem(64, nj), vmem(4...  2.41 us
  transfers between devices with their start and end apart: 5, of which 4 were waited for; matrix products, arithmetic and copies ran while one was open for 7% of the time, Pallas kernels for 0%

profile of v7, /device:TPU:1, one launch (start us, length us, event | category | flops | bytes accessed | tf_op | source)
XLA Modules:
  0.0 69.6 jit_solution(11401359479775167358)
XLA Ops:
  0.6 0.0 copy-start
  0.6 0.0 copy-start.1
  0.7 0.0 copy-start.2
  0.7 0.0 copy-start.3
  0.7 2.4 %pack.1 = (f32[64,384]{1,0:T(8,128)S(1)}, f32[64,384]{1,0:T(8,128)S(1)}, f32[4,16,384]{2,1,0:T(8,128)S(1)}, f32[40,128]{1,0:T(8,128)S(1)}, s32[2,8,128]{2,1,0:T(8,128)S(1)}, /*index=5*/f32[4,16,128]{2,1,0:T(8,128)}) custom-call(f32[8,16,384]{2,1,0:T(8,128)} %t.1, f32[8,16,384]{2,1,0:T(8,128)} %s.1, f32[8,16,384]{2,1,0:T(8,128)} %u.1, f32[8,16,384]{2,1,0:T(8,128)} %v.1, ...), custom_call_target="tpu_custom_call" | custom-call | tf_op jit(solution)/shard_map/pack/pallas_call | solution.py:334
  3.1 0.0 copy-start.5
  3.1 13.9 %all-to-all-start = ((f32[4,16,128]{2,1,0:T(8,128)}), f32[4,16,128]{2,1,0:T(8,128)S(1)}, u32[]{:S(2)}, u32[]{:S(2)}) async-start(f32[4,16,128]{2,1,0:T(8,128)} %get-tuple-element.20), calls=%async_computation | async-start | bytes 65536 | tf_op jit(solution)/shard_map/all_to_all | solution.py:347
  17.0 0.0 copy-done.5
  17.0 0.0 copy-start.4
  17.0 0.0 copy-done
  17.0 0.0 copy-done.1
  17.0 0.0 copy-done.2
  17.0 0.0 copy-done.3
  17.0 0.7 copy-done.4
  17.7 0.1 fusion.20
  17.8 2.3 %all-to-all-done.got = f32[4,16,128]{2,1,0:T(8,128)S(1)} async-done(((f32[4,16,128]{2,1,0:T(8,128)}), f32[4,16,128]{2,1,0:T(8,128)S(1)}, u32[]{:S(2)}, u32[]{:S(2)}) %all-to-all-start) | async-done | bytes 32800 | tf_op jit(solution)/shard_map/all_to_all | solution.py:347
  20.1 0.1 widen.1
  20.3 10.7 %collective-permute-start = (f32[88,384]{1,0:T(8,128)S(1)}, f32[88,384]{1,0:T(8,128)S(1)}, u32[]{:S(2)}, u32[]{:S(2)}) collective-permute-start(f32[88,384]{1,0:T(8,128)S(1)} %get-tuple-element.25), channel_id=1, source_target_pairs={{4,8},{8,4},{12,16},{16,12},{20,24},{24,20},{28,32},{32,28},{36,40... | collective-permute-start | bytes 405512 | tf_op jit(solution)/shard_map/ppermute | solution.py:361
  31.0 1.9 %collective-permute-start.1 = (f32[88,384]{1,0:T(8,128)S(1)}, f32[88,384]{1,0:T(8,128)S(1)}, u32[]{:S(2)}, u32[]{:S(2)}) collective-permute-start(f32[88,384]{1,0:T(8,128)S(1)} %get-tuple-element.26), channel_id=1, source_target_pairs={{0,4},{4,0},{8,12},{12,8},{16,20},{20,16},{24,28},{28,24},{32,36},... | collective-permute-start | bytes 405512 | tf_op jit(solution)/shard_map/ppermute | solution.py:362
  32.9 0.1 reshape.93
  33.0 0.2 copy.19
  33.1 0.1 reshape.94
  33.2 0.2 copy.20
  33.4 0.2 concatenate.48
  33.6 0.1 broadcast_compare_fusion.1
  33.8 0.2 maximum_maximum_fusion.2
  34.0 1.2 %add_multiply_fusion.1 = f32[2,8,16,385]{3,2,1,0:T(8,128)S(1)} fusion(f32[2,8,16,387]{3,2,1,0:T(8,128)S(1)} %get-tuple-element.43, f32[2,8,16,387]{3,2,1,0:T(8,128)S(1)} %get-tuple-element.42, f32[8,16,385]{2,1,0:T(8,128)S(1)} %get-tuple-element.37, pred[8,16,385]{2,1,0:T(8,128)(4,1)S(1)} %get-tuple-element.36), kind=kLoop, calls=%fused_computation.40 | loop fusion | flops 6012160 | bytes 3006080 | tf_op jit(solution)/shard_map/mul | solution.py:38
  35.2 0.0 collective-permute-done.far
  35.2 1.5 %collective-permute-done.1.close = f32[88,384]{1,0:T(8,128)S(1)} collective-permute-done((f32[88,384]{1,0:T(8,128)S(1)}, f32[88,384]{1,0:T(8,128)S(1)}, u32[]{:S(2)}, u32[]{:S(2)}) %collective-permute-start.1) | collective-permute-done | bytes 135200 | tf_op jit(solution)/shard_map/ppermute | solution.py:362
  36.8 0.1 broadcast_compare_fusion
  36.9 1.1 %krylov.1 = (f32[4,16,384]{2,1,0:T(8,128)S(1)}, f32[24,4,128]{2,1,0:T(4,128)}) custom-call(f32[4,16,128]{2,1,0:T(8,128)S(1)} %all-to-all-done.got, f32[4,16,384]{2,1,0:T(8,128)S(1)} %get-tuple-element.21.fields, f32[4,16,128]{2,1,0:T(8,128)S(1)} %get-tuple-element.24.beyond, f32[88,384]{1,0:T(8,128)S(1)} %collective-permute-done.far, ...), custom_call_target="tpu_custom_call" | custom-call | tf_op jit(solution)/shard_map/krylov/pallas_call | solution.py:363
  37.9 5.7 %all-to-all-start.1 = ((f32[24,4,128]{2,1,0:T(4,128)}), f32[24,4,128]{2,1,0:T(4,128)S(1)}, u32[]{:S(2)}, u32[]{:S(2)}) async-start(f32[24,4,128]{2,1,0:T(4,128)} %get-tuple-element.29), calls=%async_computation.1 | async-start | bytes 98304 | tf_op jit(solution)/shard_map/all_to_all | solution.py:369
  43.7 0.1 maximum_maximum_fusion
  43.8 1.4 %add_multiply_fusion = f32[2,8,17,384]{3,2,1,0:T(8,128)S(1)} fusion(f32[2,8,19,384]{3,2,1,0:T(8,128)S(1)} %get-tuple-element.41, f32[2,8,19,384]{3,2,1,0:T(8,128)S(1)} %get-tuple-element.40, f32[8,17,384]{2,1,0:T(8,128)S(1)} %pad_maximum_fusion.1, pred[8,17,384]{2,1,0:T(8,128)(4,1)S(1)} %broadcast_compare_fusion), kind=kLoop, calls=%fused_computation.28 | loop fusion | flops 6371328 | bytes 3185664 | tf_op jit(solution)/shard_map/mul | solution.py:38
  45.2 0.3 fusion.15
  45.5 8.3 %all-to-all-done.1.got = f32[24,4,128]{2,1,0:T(4,128)S(1)} async-done(((f32[24,4,128]{2,1,0:T(4,128)}), f32[24,4,128]{2,1,0:T(4,128)S(1)}, u32[]{:S(2)}, u32[]{:S(2)}) %all-to-all-start.1) | async-done | bytes 49184 | tf_op jit(solution)/shard_map/all_to_all | solution.py:369
  53.8 0.7 relay.1
  54.5 4.9 %all-to-all-start.2 = ((f32[32,4,128]{2,1,0:T(4,128)}), f32[32,4,128]{2,1,0:T(4,128)S(1)}, u32[]{:S(2)}, u32[]{:S(2)}) async-start(f32[32,4,128]{2,1,0:T(4,128)} %relay.1), calls=%async_computation.2 | async-start | bytes 131072 | tf_op jit(solution)/shard_map/all_to_all | solution.py:373
  59.4 0.8 %slice_bitcast_fusion = (f32[8,16,384]{2,1,0:T(8,128)}, f32[8,16,384]{2,1,0:T(8,128)}) fusion(f32[2,8,16,384]{3,2,1,0:T(8,128)S(1)} %fusion.15), kind=kLoop, calls=%fused_computation.55 | loop fusion | bytes 786432 | tf_op jit(solution)/shard_map/squeeze | solution.py:423
  60.1 8.0 %all-to-all-done.2.got = f32[32,4,128]{2,1,0:T(4,128)S(1)} async-done(((f32[32,4,128]{2,1,0:T(4,128)}), f32[32,4,128]{2,1,0:T(4,128)S(1)}, u32[]{:S(2)}, u32[]{:S(2)}) %all-to-all-start.2) | async-done | bytes 65568 | tf_op jit(solution)/shard_map/all_to_all | solution.py:373
  68.2 1.5 %finish.1 = (f32[16,384]{1,0:T(8,128)}, f32[16,384]{1,0:T(8,128)}, f32[8,16,384]{2,1,0:T(8,128)}, f32[8,16,384]{2,1,0:T(8,128)}) custom-call(f32[4,16,384]{2,1,0:T(8,128)S(1)} %get-tuple-element.27.basis_ref, s32[2,8,128]{2,1,0:T(8,128)S(1)} %get-tuple-element.28.source, ...), custom_call_target="tpu_custom_call", output_to_operand_aliasing={{2}: (6, {}), {3}: (7, {})} | custom-call | tf_op jit(solution)/shard_map/finish/pallas_call | solution.py:407
  (10 shorter events, 0.2 us)
Async XLA Ops:
  0.6 16.3 %copy-start = (f32[8,16,384]{2,1,0:T(8,128)S(1)}, f32[8,16,384]{2,1,0:T(8,128)}, u32[]{:S(2)}) copy-start(f32[8,16,384]{2,1,0:T(8,128)} %t.1) | copy-start | bytes 589828
  0.6 16.3 %copy-start.1 = (f32[8,16,384]{2,1,0:T(8,128)S(1)}, f32[8,16,384]{2,1,0:T(8,128)}, u32[]{:S(2)}) copy-start(f32[8,16,384]{2,1,0:T(8,128)} %s.1) | copy-start | bytes 589828
  0.7 16.3 %copy-start.2 = (f32[8,16,384]{2,1,0:T(8,128)S(1)}, f32[8,16,384]{2,1,0:T(8,128)}, u32[]{:S(2)}) copy-start(f32[8,16,384]{2,1,0:T(8,128)} %u.1) | copy-start | bytes 589828
  0.7 16.3 %copy-start.3 = (f32[8,16,384]{2,1,0:T(8,128)S(1)}, f32[8,16,384]{2,1,0:T(8,128)}, u32[]{:S(2)}) copy-start(f32[8,16,384]{2,1,0:T(8,128)} %v.1) | copy-start | bytes 589828
  3.1 13.9 %copy-start.5 = (s32[16,384]{1,0:T(8,128)S(1)}, s32[16,384]{1,0:T(8,128)}, u32[]{:S(2)}) copy-start(s32[16,384]{1,0:T(8,128)} %flag.1) | copy-start | bytes 73732
  3.1 17.1 %all-to-all-start = ((f32[4,16,128]{2,1,0:T(8,128)}), f32[4,16,128]{2,1,0:T(8,128)S(1)}, u32[]{:S(2)}, u32[]{:S(2)}) async-start(f32[4,16,128]{2,1,0:T(8,128)} %get-tuple-element.20), calls=%async_computation | async-start | bytes 65536 | tf_op jit(solution)/shard_map/all_to_all | solution.py:347
  17.0 0.7 %copy-start.4 = (s32[16,384]{1,0:T(8,128)S(1)}, s32[16,384]{1,0:T(8,128)}, u32[]{:S(2)}) copy-start(s32[16,384]{1,0:T(8,128)} %depth.1) | copy-start | bytes 73732
  20.3 14.9 %collective-permute-start = (f32[88,384]{1,0:T(8,128)S(1)}, f32[88,384]{1,0:T(8,128)S(1)}, u32[]{:S(2)}, u32[]{:S(2)}) collective-permute-start(f32[88,384]{1,0:T(8,128)S(1)} %get-tuple-element.25), channel_id=1, source_target_pairs={{4,8},{8,4},{12,16},{16,12},{20,24},{24,20},{28,32},{32,28},{36,40... | collective-permute-start | bytes 405512 | tf_op jit(solution)/shard_map/ppermute | solution.py:361
  31.0 5.8 %collective-permute-start.1 = (f32[88,384]{1,0:T(8,128)S(1)}, f32[88,384]{1,0:T(8,128)S(1)}, u32[]{:S(2)}, u32[]{:S(2)}) collective-permute-start(f32[88,384]{1,0:T(8,128)S(1)} %get-tuple-element.26), channel_id=1, source_target_pairs={{0,4},{4,0},{8,12},{12,8},{16,20},{20,16},{24,28},{28,24},{32,36},... | collective-permute-start | bytes 405512 | tf_op jit(solution)/shard_map/ppermute | solution.py:362
  37.9 15.9 %all-to-all-start.1 = ((f32[24,4,128]{2,1,0:T(4,128)}), f32[24,4,128]{2,1,0:T(4,128)S(1)}, u32[]{:S(2)}, u32[]{:S(2)}) async-start(f32[24,4,128]{2,1,0:T(4,128)} %get-tuple-element.29), calls=%async_computation.1 | async-start | bytes 98304 | tf_op jit(solution)/shard_map/all_to_all | solution.py:369
  54.5 13.7 %all-to-all-start.2 = ((f32[32,4,128]{2,1,0:T(4,128)}), f32[32,4,128]{2,1,0:T(4,128)S(1)}, u32[]{:S(2)}, u32[]{:S(2)}) async-start(f32[32,4,128]{2,1,0:T(4,128)} %relay.1), calls=%async_computation.2 | async-start | bytes 131072 | tf_op jit(solution)/shard_map/all_to_all | solution.py:373

commit v8 on v7

--- a/solution.py
+++ b/solution.py
@@ -102,7 +102,7 @@
 
 
 def pack_kernel(
-    t, s, u, v, elev, flag, depth, fc, far, close, fields, edges, source, slots, up, down, tile
+    t, s, u, v, elev, flag, depth, fc, far, close, fields, edges, source, slots_out, slots, tile, sem
 ):
     nl, ni, nj = t.shape
     ocean = flag[...] == 1
@@ -110,23 +110,17 @@
     lane = lax.broadcasted_iota(jnp.int32, (ni, 128), 1)
     em = jnp.zeros((ni, nj), jnp.float32)
     nm = jnp.zeros((ni, nj), jnp.float32)
-    zero = jnp.zeros((8, nj), jnp.float32)
+    tail = nj - 128
     for l in range(nl):
         m = jnp.where(ocean & (wet > l), 1.0, 0.0)
-        tt, ss, uu, vv = t[l] * m, s[l] * m, u[l] * m, v[l] * m
-        em = em + uu
+        em = em + u[l] * m
+        vv = v[l] * m
         nm = nm + vv
-        up[8 * l : 8 * l + 3] = tt[ni - 3 :]
-        up[8 * l + 3 : 8 * l + 6] = ss[ni - 3 :]
-        up[8 * l + 6 : 8 * l + 7] = uu[ni - 1 :]
-        up[8 * l + 7 : 8 * l + 8] = zero[:1]
-        down[8 * l : 8 * l + 3] = tt[:3]
-        down[8 * l + 3 : 8 * l + 6] = ss[:3]
-        down[8 * l + 6 : 8 * l + 8] = zero[:2]
-        x = jnp.where(lane < 8, tt[:, :128], tt[:, nj - 128 :])
-        x = jnp.where((lane >= 8) & (lane < 16), pltpu.roll(ss[:, :128], 8, 1), x)
-        x = jnp.where((lane >= 112) & (lane < 120), pltpu.roll(ss[:, nj - 128 :], 120, 1), x)
-        x = jnp.where((lane >= 104) & (lane < 112), pltpu.roll(vv[:, nj - 128 :], 112, 1), x)
+        first, last = m[:, :128], m[:, tail:]
+        x = jnp.where(lane < 8, t[l, :, :128] * first, t[l, :, tail:] * last)
+        x = jnp.where((lane >= 8) & (lane < 16), pltpu.roll(s[l, :, :128] * first, 8, 1), x)
+        x = jnp.where((lane >= 112) & (lane < 120), pltpu.roll(s[l, :, tail:] * last, 120, 1), x)
+        x = jnp.where((lane >= 104) & (lane < 112), pltpu.roll(vv[:, tail:], 112, 1), x)
         tile[ni * l : ni * (l + 1)] = x
     em = em / nl
     nm = nm / nl
@@ -134,15 +128,13 @@
     coupler = 2.0 * jnp.sqrt((wet * flag[...]).astype(jnp.float32) / nl)
     for k, f in enumerate((part, em, nm, coupler)):
         fields[k] = f
-    even = lon_even()
-    far[...] = jnp.where(even, down[...], up[...])
-    close[...] = jnp.where(even, up[...], down[...])
+        x = tile[ni * k : ni * (k + 1)]
+        x = jnp.where((lane >= 16) & (lane < 20), pltpu.roll(f[:, :128], 16, 1), x)
+        x = jnp.where((lane >= 100) & (lane < 104), pltpu.roll(f[:, tail:], 104, 1), x)
+        tile[ni * k : ni * (k + 1)] = x
     turned = tile[...].T
     edges[0:16] = turned[0:16]
     edges[16:40] = turned[104:128]
-    for k, f in enumerate((part, em, nm, coupler)):
-        tile[ni * k : ni * (k + 1)] = jnp.where(lane < 64, f[:, :128], f[:, nj - 128 :])
-    columns = tile[...].T
     lat = lat_index()
     none = jnp.zeros((2, 128), jnp.float32)
     t_end, s_end, v_end = turned[125:128], turned[117:120], turned[111:112]
@@ -153,9 +145,23 @@
     for p in range(4):
         ahead = p > lat
         slots[p, 0:8] = jnp.where(ahead, north, south)
-        slots[p, 8:12] = jnp.where(ahead, columns[124:128], columns[0:4])
+        slots[p, 8:12] = jnp.where(ahead, turned[100:104], turned[16:20])
         slots[p, 12:15] = fold[0:3] if p < 2 else fold[3:6]
         slots[p, 15:16] = none[:1]
+    copy = pltpu.make_async_copy(slots, slots_out, sem)
+    copy.start()
+
+    even = lon_even()
+    zero = jnp.zeros((2, nj), jnp.float32)
+    for l in range(nl):
+        m = jnp.where(ocean & (wet > l), 1.0, 0.0)
+        tt, ss = t[l] * m, s[l] * m
+        east_edge = jnp.concatenate(
+            [tt[ni - 3 :], ss[ni - 3 :], u[l, ni - 1 :] * m[ni - 1 :], zero[:1]], axis=0
+        )
+        west_edge = jnp.concatenate([tt[:3], ss[:3], zero], axis=0)
+        far[8 * l : 8 * l + 8] = jnp.where(even, west_edge, east_edge)
+        close[8 * l : 8 * l + 8] = jnp.where(even, east_edge, west_edge)
     block = lax.shift_right_logical(jnp.broadcast_to(fc[0:1, 0:1], (8, 128)), 4)
     row = jnp.zeros((8, 128), jnp.int32)
     nz = lax.axis_size("z")
@@ -163,9 +169,10 @@
         row = row + jnp.where(block >= nz * k, 1, 0)
     source[0] = block - nz * row
     source[1] = row
-
-
-def widen_kernel(got, fields, far_q, close_q, far, close, beyond, rims, tile, up, down):
+    copy.wait()
+
+
+def widen_kernel(got, fields, far_q, close_q, close, far, beyond, rims, tile, up, down):
     _, ni, nj = fields.shape
     lat = lat_index()
     even = lon_even()
@@ -196,7 +203,7 @@
         out[80:88, 256:384] = jnp.zeros((8, 128), jnp.float32)
 
 
-def krylov_kernel(got, fields, beyond, far, close, basis_ref, message, wide, west, east):
+def krylov_kernel(got, fields, beyond, close, far, basis_ref, message, wide, west, east):
     _, ni, nj = fields.shape
     even = lon_even()
     for out, first, second in ((west, far, close), (east, close, far)):
@@ -267,7 +274,7 @@
 
 def finish_kernel(
     basis_ref, source, got, edges, tail, wet, base_t, base_s,
-    surface_ref, residual_ref, out_t, out_s, tile, final, sems,
+    surface_out, residual_out, out_t, out_s, surface, residual, tile, final, sems,
 ):
     del base_t, base_s
     total = got[0]
@@ -285,18 +292,14 @@
     row = lax.broadcasted_iota(jnp.int32, (8, 128), 0)
     speed = jnp.where(row < 3, pltpu.roll(edges[16:24], 3, 0) * last, 0.0)
     pos = speed > 0.0
-    nj = surface_ref.shape[1]
-    copies = []
-    for k, out in enumerate((out_t, out_s)):
+    nj = surface.shape[1]
+    for k in range(2):
         q = [rows[k]] + [pltpu.roll(rows[k], 8 - o, 0) for o in range(1, 6)]
         face = speed * weno_upwind(*[jnp.where(pos, q[i], q[5 - i]) for i in range(5)])
         change = face - jnp.where(row == 0, 0.0, pltpu.roll(face, 1, 0))
-        tile[...] = jnp.zeros((128, 128), jnp.float32)
-        tile[125:128] = change[0:3]
-        final[k] = (tail[k] - tile[...].T.reshape(tail.shape[1:])) * wet[...]
-        copy = pltpu.make_async_copy(final.at[k], out.at[:, :, nj - 128 : nj], sems.at[k])
-        copy.start()
-        copies.append(copy)
+        tile[k] = jnp.zeros((128, 128), jnp.float32)
+        tile[k, 125:128] = change[0:3]
+        final[k] = (tail[k] - tile[k].T.reshape(tail.shape[1:])) * wet[...]
     line = total[3:4]
     col = lax.broadcasted_iota(jnp.int32, (1, 128), 1)
     gram = {}
@@ -304,8 +307,16 @@
         gram[pair] = jnp.sum(jnp.where(col == n, line, 0.0), axis=1, keepdims=True)
     xc, rc = coefficients(gram)
     basis = [basis_ref[k] for k in range(4)]
-    surface_ref[...] = sum(c * f for c, f in zip(xc, basis) if c is not None)
-    residual_ref[...] = sum(c * f for c, f in zip(rc, basis) if c is not None)
+    surface[...] = sum(c * f for c, f in zip(xc, basis) if c is not None)
+    residual[...] = sum(c * f for c, f in zip(rc, basis) if c is not None)
+    copies = [
+        pltpu.make_async_copy(final.at[0], out_t.at[:, :, nj - 128 : nj], sems.at[0]),
+        pltpu.make_async_copy(final.at[1], out_s.at[:, :, nj - 128 : nj], sems.at[1]),
+        pltpu.make_async_copy(surface, surface_out, sems.at[2]),
+        pltpu.make_async_copy(residual, residual_out, sems.at[3]),
+    ]
+    for copy in copies:
+        copy.start()
     for copy in copies:
         copy.wait()
 
@@ -330,6 +341,7 @@
         nl, ni, nj = t.shape
         lat = lax.axis_index(LAT)
         last = lat == n_lat - 1
+        hbm, local = pl.BlockSpec(memory_space=pl.ANY), pl.BlockSpec(memory_space=pltpu.VMEM)
 
         far, close, fields, edges, source, slots = pl.pallas_call(
             pack_kernel,
@@ -339,13 +351,15 @@
                 vmem(4, ni, nj),
                 vmem(40, 128),
                 pltpu.VMEM((2, 8, 128), jnp.int32),
-                vmem(4, 16, 128),
+                f32(4, 16, 128),
             ),
-            scratch_shapes=[vmem(64, nj), vmem(64, nj), vmem(128, 128)],
+            in_specs=[local] * 8,
+            out_specs=(local,) * 5 + (hbm,),
+            scratch_shapes=[vmem(4, 16, 128), vmem(128, 128), pltpu.SemaphoreType.DMA],
             name="pack",
         )(t, s, u, v, elev, flag, depth, fc.reshape(1, ni))
         halo = lax.all_to_all(slots, LAT, 0, 0)
-        far, close, beyond, rims = pl.pallas_call(
+        close, far, beyond, rims = pl.pallas_call(
             widen_kernel,
             out_shape=(vmem(88, nj), vmem(88, nj), vmem(4, ni, 128), vmem(2, 8, 128)),
             scratch_shapes=[vmem(128, 128), vmem(16, nj + 128), vmem(16, nj + 128)],
@@ -358,14 +372,14 @@
                 pairs += [(i, (i + 1) % n_lon), ((i + 1) % n_lon, i)]
             return pairs
 
+        close = lax.ppermute(close, LON, swaps(0))
         far = lax.ppermute(far, LON, swaps(1))
-        close = lax.ppermute(close, LON, swaps(0))
         basis, message = pl.pallas_call(
             krylov_kernel,
             out_shape=(vmem(4, ni, nj), vmem(nz * ncore, 4, 128)),
             scratch_shapes=[vmem(4, 32, nj + 128), vmem(16, nj + 128), vmem(16, nj + 128)],
             name="krylov",
-        )(near(halo), near(fields), near(beyond), near(far), near(close))
+        )(near(halo), near(fields), near(beyond), near(close), near(far))
         got = lax.all_to_all(message, ("z", "core"), 0, 0)
         message = pl.pallas_call(
             relay_kernel, out_shape=vmem(ny * nxh * nxl, 4, 128), name="relay"
@@ -403,14 +417,19 @@
         flux_y = face_flux(merid, speed_y[None], nj + 1, 3)
         updated = q - (flux_x[:, :, 1:] - flux_x[:, :, :-1]) - (flux_y[..., 1:] - flux_y[..., :-1])
         updated = updated * mask
-        hbm, local = pl.BlockSpec(memory_space=pl.ANY), pl.BlockSpec(memory_space=pltpu.VMEM)
         surface, residual, t_next, s_next = pl.pallas_call(
             finish_kernel,
             in_specs=[local] * 6 + [hbm] * 2,
-            out_specs=(local, local, hbm, hbm),
+            out_specs=(hbm,) * 4,
             out_shape=(f32(ni, nj), f32(ni, nj), f32(nl, ni, nj), f32(nl, ni, nj)),
             input_output_aliases={6: 2, 7: 3},
-            scratch_shapes=[vmem(128, 128), vmem(2, nl, ni, 128), pltpu.SemaphoreType.DMA((2,))],
+            scratch_shapes=[
+                vmem(ni, nj),
+                vmem(ni, nj),
+                vmem(2, 128, 128),
+                vmem(2, nl, ni, 128),
+                pltpu.SemaphoreType.DMA((4,)),
+            ],
             name="finish",
         )(
             near(basis),

time: 70.1 us -> 71.8 us (1.024)
  starting transfers between devices: 37.1 us -> 40.2 us
  waiting for transfers between devices: 20.2 us -> 19.2 us
    all_to_all x1, starting transfers between devices: 4.89 us -> 8.39 us  [on_device(): got = lax.all_to_all(message, ('y', 'xh', 'xl'), 0, 0)]
    ppermute x1, waiting for transfers between devices: 1.49 us -> 0.01 us  [on_device(): close = lax.ppermute(close, LON, swaps(0))]
where the time goes in v8:
time: 71.8 us; the launch traced here: 71.3 us
  starting transfers between devices  40.2 us (56%)
  waiting for transfers between devices  19.2 us (27%)
  Pallas kernels  5.16 us (7%)
  other arithmetic  3.56 us (5%)
  local copies, waits for them, and re-layouts  2.26 us (3%)
  between operations  0.9 us (1%)
    all_to_all x1, starting transfers between devices, on_device(): halo = lax.all_to_all(slots, LAT, 0, 0)  13.8 us
    ppermute x1, starting transfers between devices, on_device(): far = lax.ppermute(far, LON, swaps(1))  10.9 us
    all_to_all x1, starting transfers between devices, on_device(): got = lax.all_to_all(message, ('y', 'xh', 'xl'), 0, 0)  8.39 us
    all_to_all x1, waiting for transfers between devices, on_device(): got = lax.all_to_all(message, ('z', 'core'), 0, 0)  8.34 us
    all_to_all x1, waiting for transfers between devices, on_device(): got = lax.all_to_all(message, ('y', 'xh', 'xl'), 0, 0)  8.05 us
    all_to_all x1, starting transfers between devices, on_device(): got = lax.all_to_all(message, ('z', 'core'), 0, 0)  5.19 us
    mul x2, other arithmetic, face_flux(): return speed * weno_upwind(a, b, c, d, e)  2.6 us
    pallas_call x1, Pallas kernels, on_device(): pl.pallas_call(pack_kernel, out_shape=(vmem(64, nj), vmem(64, nj), vmem(4...  2.46 us
  transfers between devices with their start and end apart: 5, of which 4 were waited for; matrix products, arithmetic and copies ran while one was open for 7% of the time, Pallas kernels for 0%

profile of v8, /device:TPU:1, one launch (start us, length us, event | category | flops | bytes accessed | tf_op | source)
XLA Modules:
  0.0 71.3 jit_solution(13973144753413684816)
XLA Ops:
  0.6 0.0 copy-start
  0.6 0.0 copy-start.1
  0.7 0.0 copy-start.2
  0.7 0.0 copy-start.3
  0.7 2.5 %pack.1 = (f32[64,384]{1,0:T(8,128)S(1)}, f32[64,384]{1,0:T(8,128)S(1)}, f32[4,16,384]{2,1,0:T(8,128)S(1)}, f32[40,128]{1,0:T(8,128)S(1)}, s32[2,8,128]{2,1,0:T(8,128)S(1)}, /*index=5*/f32[4,16,128]{2,1,0:T(8,128)}) custom-call(f32[8,16,384]{2,1,0:T(8,128)} %t.1, f32[8,16,384]{2,1,0:T(8,128)} %s.1, f32[8,16,384]{2,1,0:T(8,128)} %u.1, f32[8,16,384]{2,1,0:T(8,128)} %v.1, ...), custom_call_target="tpu_custom_call" | custom-call | tf_op jit(solution)/shard_map/pack/pallas_call | solution.py:346
  3.1 0.0 copy-start.5
  3.1 13.8 %all-to-all-start = ((f32[4,16,128]{2,1,0:T(8,128)}), f32[4,16,128]{2,1,0:T(8,128)S(1)}, u32[]{:S(2)}, u32[]{:S(2)}) async-start(f32[4,16,128]{2,1,0:T(8,128)} %get-tuple-element.20), calls=%async_computation | async-start | bytes 65536 | tf_op jit(solution)/shard_map/all_to_all | solution.py:361
  16.9 0.0 copy-done.5
  16.9 0.0 copy-start.4
  16.9 0.0 copy-done
  16.9 0.0 copy-done.1
  16.9 0.0 copy-done.2
  17.0 0.0 copy-done.3
  17.0 0.7 copy-done.4
  17.7 0.1 fusion.20
  17.8 2.3 %all-to-all-done.got = f32[4,16,128]{2,1,0:T(8,128)S(1)} async-done(((f32[4,16,128]{2,1,0:T(8,128)}), f32[4,16,128]{2,1,0:T(8,128)S(1)}, u32[]{:S(2)}, u32[]{:S(2)}) %all-to-all-start) | async-done | bytes 32800 | tf_op jit(solution)/shard_map/all_to_all | solution.py:361
  20.1 0.1 widen.1
  20.3 1.9 %collective-permute-start = (f32[88,384]{1,0:T(8,128)S(1)}, f32[88,384]{1,0:T(8,128)S(1)}, u32[]{:S(2)}, u32[]{:S(2)}) collective-permute-start(f32[88,384]{1,0:T(8,128)S(1)} %get-tuple-element.25), channel_id=1, source_target_pairs={{0,4},{4,0},{8,12},{12,8},{16,20},{20,16},{24,28},{28,24},{32,36},... | collective-permute-start | bytes 405512 | tf_op jit(solution)/shard_map/ppermute | solution.py:375
  22.2 10.9 %collective-permute-start.1 = (f32[88,384]{1,0:T(8,128)S(1)}, f32[88,384]{1,0:T(8,128)S(1)}, u32[]{:S(2)}, u32[]{:S(2)}) collective-permute-start(f32[88,384]{1,0:T(8,128)S(1)} %get-tuple-element.26), channel_id=1, source_target_pairs={{4,8},{8,4},{12,16},{16,12},{20,24},{24,20},{28,32},{32,28},{36,40... | collective-permute-start | bytes 405512 | tf_op jit(solution)/shard_map/ppermute | solution.py:376
  33.1 0.1 reshape.93
  33.2 0.2 copy.19
  33.4 0.1 reshape.94
  33.4 0.2 copy.20
  33.6 0.2 concatenate.48
  33.8 0.1 broadcast_compare_fusion.1
  34.0 0.2 maximum_maximum_fusion.2
  34.2 1.2 %add_multiply_fusion.1 = f32[2,8,16,385]{3,2,1,0:T(8,128)S(1)} fusion(f32[2,8,16,387]{3,2,1,0:T(8,128)S(1)} %get-tuple-element.43, f32[2,8,16,387]{3,2,1,0:T(8,128)S(1)} %get-tuple-element.42, f32[8,16,385]{2,1,0:T(8,128)S(1)} %get-tuple-element.37, pred[8,16,385]{2,1,0:T(8,128)(4,1)S(1)} %get-tuple-element.36), kind=kLoop, calls=%fused_computation.40 | loop fusion | flops 6012160 | bytes 3006080 | tf_op jit(solution)/shard_map/mul | solution.py:38
  35.4 0.0 collective-permute-done.close
  35.4 0.5 collective-permute-done.1.far
  36.0 0.1 broadcast_compare_fusion
  36.1 1.1 %krylov.1 = (f32[4,16,384]{2,1,0:T(8,128)S(1)}, f32[24,4,128]{2,1,0:T(4,128)}) custom-call(f32[4,16,128]{2,1,0:T(8,128)S(1)} %all-to-all-done.got, f32[4,16,384]{2,1,0:T(8,128)S(1)} %get-tuple-element.21.fields, f32[4,16,128]{2,1,0:T(8,128)S(1)} %get-tuple-element.24.beyond, f32[88,384]{1,0:T(8,128)S(1)} %collective-permute-done.close, ...), custom_call_target="tpu_custom_call" | custom-call | tf_op jit(solution)/shard_map/krylov/pallas_call | solution.py:377
  37.2 5.2 %all-to-all-start.1 = ((f32[24,4,128]{2,1,0:T(4,128)}), f32[24,4,128]{2,1,0:T(4,128)S(1)}, u32[]{:S(2)}, u32[]{:S(2)}) async-start(f32[24,4,128]{2,1,0:T(4,128)} %get-tuple-element.29), calls=%async_computation.1 | async-start | bytes 98304 | tf_op jit(solution)/shard_map/all_to_all | solution.py:383
  42.4 0.1 maximum_maximum_fusion
  42.5 1.4 %add_multiply_fusion = f32[2,8,17,384]{3,2,1,0:T(8,128)S(1)} fusion(f32[2,8,19,384]{3,2,1,0:T(8,128)S(1)} %get-tuple-element.41, f32[2,8,19,384]{3,2,1,0:T(8,128)S(1)} %get-tuple-element.40, f32[8,17,384]{2,1,0:T(8,128)S(1)} %pad_maximum_fusion.1, pred[8,17,384]{2,1,0:T(8,128)(4,1)S(1)} %broadcast_compare_fusion), kind=kLoop, calls=%fused_computation.28 | loop fusion | flops 6371328 | bytes 3185664 | tf_op jit(solution)/shard_map/mul | solution.py:38
  43.9 0.3 fusion.15
  44.2 8.3 %all-to-all-done.1.got = f32[24,4,128]{2,1,0:T(4,128)S(1)} async-done(((f32[24,4,128]{2,1,0:T(4,128)}), f32[24,4,128]{2,1,0:T(4,128)S(1)}, u32[]{:S(2)}, u32[]{:S(2)}) %all-to-all-start.1) | async-done | bytes 49184 | tf_op jit(solution)/shard_map/all_to_all | solution.py:383
  52.5 0.7 relay.1
  53.2 8.4 %all-to-all-start.2 = ((f32[32,4,128]{2,1,0:T(4,128)}), f32[32,4,128]{2,1,0:T(4,128)S(1)}, u32[]{:S(2)}, u32[]{:S(2)}) async-start(f32[32,4,128]{2,1,0:T(4,128)} %relay.1), calls=%async_computation.2 | async-start | bytes 131072 | tf_op jit(solution)/shard_map/all_to_all | solution.py:387
  61.6 0.8 %slice_bitcast_fusion = (f32[8,16,384]{2,1,0:T(8,128)}, f32[8,16,384]{2,1,0:T(8,128)}) fusion(f32[2,8,16,384]{3,2,1,0:T(8,128)S(1)} %fusion.15), kind=kLoop, calls=%fused_computation.55 | loop fusion | bytes 786432 | tf_op jit(solution)/shard_map/squeeze | solution.py:442
  62.3 8.0 %all-to-all-done.2.got = f32[32,4,128]{2,1,0:T(4,128)S(1)} async-done(((f32[32,4,128]{2,1,0:T(4,128)}), f32[32,4,128]{2,1,0:T(4,128)S(1)}, u32[]{:S(2)}, u32[]{:S(2)}) %all-to-all-start.2) | async-done | bytes 65568 | tf_op jit(solution)/shard_map/all_to_all | solution.py:387
  70.4 0.9 %finish.1 = (f32[16,384]{1,0:T(8,128)}, f32[16,384]{1,0:T(8,128)}, f32[8,16,384]{2,1,0:T(8,128)}, f32[8,16,384]{2,1,0:T(8,128)}) custom-call(f32[4,16,384]{2,1,0:T(8,128)S(1)} %get-tuple-element.27.basis_ref, s32[2,8,128]{2,1,0:T(8,128)S(1)} %get-tuple-element.28.source, ...), custom_call_target="tpu_custom_call", output_to_operand_aliasing={{2}: (6, {}), {3}: (7, {})} | custom-call | tf_op jit(solution)/shard_map/finish/pallas_call | solution.py:420
  (10 shorter events, 0.2 us)
Async XLA Ops:
  0.6 16.3 %copy-start = (f32[8,16,384]{2,1,0:T(8,128)S(1)}, f32[8,16,384]{2,1,0:T(8,128)}, u32[]{:S(2)}) copy-start(f32[8,16,384]{2,1,0:T(8,128)} %t.1) | copy-start | bytes 589828
  0.6 16.3 %copy-start.1 = (f32[8,16,384]{2,1,0:T(8,128)S(1)}, f32[8,16,384]{2,1,0:T(8,128)}, u32[]{:S(2)}) copy-start(f32[8,16,384]{2,1,0:T(8,128)} %s.1) | copy-start | bytes 589828
  0.7 16.3 %copy-start.2 = (f32[8,16,384]{2,1,0:T(8,128)S(1)}, f32[8,16,384]{2,1,0:T(8,128)}, u32[]{:S(2)}) copy-start(f32[8,16,384]{2,1,0:T(8,128)} %u.1) | copy-start | bytes 589828
  0.7 16.3 %copy-start.3 = (f32[8,16,384]{2,1,0:T(8,128)S(1)}, f32[8,16,384]{2,1,0:T(8,128)}, u32[]{:S(2)}) copy-start(f32[8,16,384]{2,1,0:T(8,128)} %v.1) | copy-start | bytes 589828
  3.1 13.8 %copy-start.5 = (s32[16,384]{1,0:T(8,128)S(1)}, s32[16,384]{1,0:T(8,128)}, u32[]{:S(2)}) copy-start(s32[16,384]{1,0:T(8,128)} %flag.1) | copy-start | bytes 73732
  3.1 16.9 %all-to-all-start = ((f32[4,16,128]{2,1,0:T(8,128)}), f32[4,16,128]{2,1,0:T(8,128)S(1)}, u32[]{:S(2)}, u32[]{:S(2)}) async-start(f32[4,16,128]{2,1,0:T(8,128)} %get-tuple-element.20), calls=%async_computation | async-start | bytes 65536 | tf_op jit(solution)/shard_map/all_to_all | solution.py:361
  16.9 0.7 %copy-start.4 = (s32[16,384]{1,0:T(8,128)S(1)}, s32[16,384]{1,0:T(8,128)}, u32[]{:S(2)}) copy-start(s32[16,384]{1,0:T(8,128)} %depth.1) | copy-start | bytes 73732
  20.3 15.2 %collective-permute-start = (f32[88,384]{1,0:T(8,128)S(1)}, f32[88,384]{1,0:T(8,128)S(1)}, u32[]{:S(2)}, u32[]{:S(2)}) collective-permute-start(f32[88,384]{1,0:T(8,128)S(1)} %get-tuple-element.25), channel_id=1, source_target_pairs={{0,4},{4,0},{8,12},{12,8},{16,20},{20,16},{24,28},{28,24},{32,36},... | collective-permute-start | bytes 405512 | tf_op jit(solution)/shard_map/ppermute | solution.py:375
  22.2 13.8 %collective-permute-start.1 = (f32[88,384]{1,0:T(8,128)S(1)}, f32[88,384]{1,0:T(8,128)S(1)}, u32[]{:S(2)}, u32[]{:S(2)}) collective-permute-start(f32[88,384]{1,0:T(8,128)S(1)} %get-tuple-element.26), channel_id=1, source_target_pairs={{4,8},{8,4},{12,16},{16,12},{20,24},{24,20},{28,32},{32,28},{36,40... | collective-permute-start | bytes 405512 | tf_op jit(solution)/shard_map/ppermute | solution.py:376
  37.2 15.3 %all-to-all-start.1 = ((f32[24,4,128]{2,1,0:T(4,128)}), f32[24,4,128]{2,1,0:T(4,128)S(1)}, u32[]{:S(2)}, u32[]{:S(2)}) async-start(f32[24,4,128]{2,1,0:T(4,128)} %get-tuple-element.29), calls=%async_computation.1 | async-start | bytes 98304 | tf_op jit(solution)/shard_map/all_to_all | solution.py:383
  53.2 17.2 %all-to-all-start.2 = ((f32[32,4,128]{2,1,0:T(4,128)}), f32[32,4,128]{2,1,0:T(4,128)S(1)}, u32[]{:S(2)}, u32[]{:S(2)}) async-start(f32[32,4,128]{2,1,0:T(4,128)} %relay.1), calls=%async_computation.2 | async-start | bytes 131072 | tf_op jit(solution)/shard_map/all_to_all | solution.py:387

commit v9 on v8

--- a/solution.py
+++ b/solution.py
@@ -172,7 +172,7 @@
     copy.wait()
 
 
-def widen_kernel(got, fields, far_q, close_q, close, far, beyond, rims, tile, up, down):
+def widen_kernel(got, fields, far_q, close_q, far, close, beyond, rims, tile, up, down):
     _, ni, nj = fields.shape
     lat = lat_index()
     even = lon_even()
@@ -203,7 +203,7 @@
         out[80:88, 256:384] = jnp.zeros((8, 128), jnp.float32)
 
 
-def krylov_kernel(got, fields, beyond, close, far, basis_ref, message, wide, west, east):
+def krylov_kernel(got, fields, beyond, far, close, basis_ref, message, wide, west, east):
     _, ni, nj = fields.shape
     even = lon_even()
     for out, first, second in ((west, far, close), (east, close, far)):
@@ -359,7 +359,7 @@
             name="pack",
         )(t, s, u, v, elev, flag, depth, fc.reshape(1, ni))
         halo = lax.all_to_all(slots, LAT, 0, 0)
-        close, far, beyond, rims = pl.pallas_call(
+        far, close, beyond, rims = pl.pallas_call(
             widen_kernel,
             out_shape=(vmem(88, nj), vmem(88, nj), vmem(4, ni, 128), vmem(2, 8, 128)),
             scratch_shapes=[vmem(128, 128), vmem(16, nj + 128), vmem(16, nj + 128)],
@@ -379,7 +379,7 @@
             out_shape=(vmem(4, ni, nj), vmem(nz * ncore, 4, 128)),
             scratch_shapes=[vmem(4, 32, nj + 128), vmem(16, nj + 128), vmem(16, nj + 128)],
             name="krylov",
-        )(near(halo), near(fields), near(beyond), near(close), near(far))
+        )(near(halo), near(fields), near(beyond), near(far), near(close))
         got = lax.all_to_all(message, ("z", "core"), 0, 0)
         message = pl.pallas_call(
             relay_kernel, out_shape=vmem(ny * nxh * nxl, 4, 128), name="relay"

time: 71.8 us -> 69.5 us (0.968)
  starting transfers between devices: 40.2 us -> 37 us
  waiting for transfers between devices: 19.2 us -> 20.2 us
    all_to_all x1, starting transfers between devices: 8.39 us -> 4.89 us  [on_device(): got = lax.all_to_all(message, ('y', 'xh', 'xl'), 0, 0)]
    ppermute x1, waiting for transfers between devices: 0.01 us -> 1.49 us  [on_device(): close = lax.ppermute(close, LON, swaps(0))]
where the time goes in v9:
time: 69.5 us; the launch traced here: 69 us
  starting transfers between devices  37 us (53%)
  waiting for transfers between devices  20.2 us (29%)
  Pallas kernels  5.16 us (7%)
  other arithmetic  3.56 us (5%)
  local copies, waits for them, and re-layouts  2.26 us (3%)
  between operations  0.9 us (1%)
    all_to_all x1, starting transfers between devices, on_device(): halo = lax.all_to_all(slots, LAT, 0, 0)  13.8 us
    ppermute x1, starting transfers between devices, on_device(): far = lax.ppermute(far, LON, swaps(1))  10.7 us
    all_to_all x1, waiting for transfers between devices, on_device(): got = lax.all_to_all(message, ('z', 'core'), 0, 0)  8.34 us
    all_to_all x1, waiting for transfers between devices, on_device(): got = lax.all_to_all(message, ('y', 'xh', 'xl'), 0, 0)  8.05 us
    all_to_all x1, starting transfers between devices, on_device(): got = lax.all_to_all(message, ('z', 'core'), 0, 0)  5.73 us
    all_to_all x1, starting transfers between devices, on_device(): got = lax.all_to_all(message, ('y', 'xh', 'xl'), 0, 0)  4.89 us
    mul x2, other arithmetic, face_flux(): return speed * weno_upwind(a, b, c, d, e)  2.6 us
    pallas_call x1, Pallas kernels, on_device(): pl.pallas_call(pack_kernel, out_shape=(vmem(64, nj), vmem(64, nj), vmem(4...  2.46 us
  transfers between devices with their start and end apart: 5, of which 4 were waited for; matrix products, arithmetic and copies ran while one was open for 7% of the time, Pallas kernels for 0%

profile of v9, /device:TPU:1, one launch (start us, length us, event | category | flops | bytes accessed | tf_op | source)
XLA Modules:
  0.0 69.0 jit_solution(967299186332904346)
XLA Ops:
  0.6 0.0 copy-start
  0.6 0.0 copy-start.1
  0.7 0.0 copy-start.2
  0.7 0.0 copy-start.3
  0.7 2.5 %pack.1 = (f32[64,384]{1,0:T(8,128)S(1)}, f32[64,384]{1,0:T(8,128)S(1)}, f32[4,16,384]{2,1,0:T(8,128)S(1)}, f32[40,128]{1,0:T(8,128)S(1)}, s32[2,8,128]{2,1,0:T(8,128)S(1)}, /*index=5*/f32[4,16,128]{2,1,0:T(8,128)}) custom-call(f32[8,16,384]{2,1,0:T(8,128)} %t.1, f32[8,16,384]{2,1,0:T(8,128)} %s.1, f32[8,16,384]{2,1,0:T(8,128)} %u.1, f32[8,16,384]{2,1,0:T(8,128)} %v.1, ...), custom_call_target="tpu_custom_call" | custom-call | tf_op jit(solution)/shard_map/pack/pallas_call | solution.py:346
  3.1 0.0 copy-start.5
  3.1 13.8 %all-to-all-start = ((f32[4,16,128]{2,1,0:T(8,128)}), f32[4,16,128]{2,1,0:T(8,128)S(1)}, u32[]{:S(2)}, u32[]{:S(2)}) async-start(f32[4,16,128]{2,1,0:T(8,128)} %get-tuple-element.20), calls=%async_computation | async-start | bytes 65536 | tf_op jit(solution)/shard_map/all_to_all | solution.py:361
  16.9 0.0 copy-done.5
  16.9 0.0 copy-start.4
  16.9 0.0 copy-done
  16.9 0.0 copy-done.1
  16.9 0.0 copy-done.2
  17.0 0.0 copy-done.3
  17.0 0.7 copy-done.4
  17.7 0.1 fusion.20
  17.8 2.3 %all-to-all-done.got = f32[4,16,128]{2,1,0:T(8,128)S(1)} async-done(((f32[4,16,128]{2,1,0:T(8,128)}), f32[4,16,128]{2,1,0:T(8,128)S(1)}, u32[]{:S(2)}, u32[]{:S(2)}) %all-to-all-start) | async-done | bytes 32800 | tf_op jit(solution)/shard_map/all_to_all | solution.py:361
  20.1 0.1 widen.1
  20.3 10.7 %collective-permute-start = (f32[88,384]{1,0:T(8,128)S(1)}, f32[88,384]{1,0:T(8,128)S(1)}, u32[]{:S(2)}, u32[]{:S(2)}) collective-permute-start(f32[88,384]{1,0:T(8,128)S(1)} %get-tuple-element.25), channel_id=1, source_target_pairs={{4,8},{8,4},{12,16},{16,12},{20,24},{24,20},{28,32},{32,28},{36,40... | collective-permute-start | bytes 405512 | tf_op jit(solution)/shard_map/ppermute | solution.py:376
  30.9 1.9 %collective-permute-start.1 = (f32[88,384]{1,0:T(8,128)S(1)}, f32[88,384]{1,0:T(8,128)S(1)}, u32[]{:S(2)}, u32[]{:S(2)}) collective-permute-start(f32[88,384]{1,0:T(8,128)S(1)} %get-tuple-element.26), channel_id=1, source_target_pairs={{0,4},{4,0},{8,12},{12,8},{16,20},{20,16},{24,28},{28,24},{32,36},... | collective-permute-start | bytes 405512 | tf_op jit(solution)/shard_map/ppermute | solution.py:375
  32.8 0.1 reshape.93
  32.9 0.2 copy.19
  33.1 0.1 reshape.94
  33.2 0.2 copy.20
  33.3 0.2 concatenate.48
  33.5 0.1 broadcast_compare_fusion.1
  33.7 0.2 maximum_maximum_fusion.2
  33.9 1.2 %add_multiply_fusion.1 = f32[2,8,16,385]{3,2,1,0:T(8,128)S(1)} fusion(f32[2,8,16,387]{3,2,1,0:T(8,128)S(1)} %get-tuple-element.43, f32[2,8,16,387]{3,2,1,0:T(8,128)S(1)} %get-tuple-element.42, f32[8,16,385]{2,1,0:T(8,128)S(1)} %get-tuple-element.37, pred[8,16,385]{2,1,0:T(8,128)(4,1)S(1)} %get-tuple-element.36), kind=kLoop, calls=%fused_computation.40 | loop fusion | flops 6012160 | bytes 3006080 | tf_op jit(solution)/shard_map/mul | solution.py:38
  35.2 0.0 collective-permute-done.far
  35.2 1.5 %collective-permute-done.1.close = f32[88,384]{1,0:T(8,128)S(1)} collective-permute-done((f32[88,384]{1,0:T(8,128)S(1)}, f32[88,384]{1,0:T(8,128)S(1)}, u32[]{:S(2)}, u32[]{:S(2)}) %collective-permute-start.1) | collective-permute-done | bytes 135200 | tf_op jit(solution)/shard_map/ppermute | solution.py:375
  36.8 0.1 broadcast_compare_fusion
  36.8 1.1 %krylov.1 = (f32[4,16,384]{2,1,0:T(8,128)S(1)}, f32[24,4,128]{2,1,0:T(4,128)}) custom-call(f32[4,16,128]{2,1,0:T(8,128)S(1)} %all-to-all-done.got, f32[4,16,384]{2,1,0:T(8,128)S(1)} %get-tuple-element.21.fields, f32[4,16,128]{2,1,0:T(8,128)S(1)} %get-tuple-element.24.beyond, f32[88,384]{1,0:T(8,128)S(1)} %collective-permute-done.far, ...), custom_call_target="tpu_custom_call" | custom-call | tf_op jit(solution)/shard_map/krylov/pallas_call | solution.py:377
  37.9 5.7 %all-to-all-start.1 = ((f32[24,4,128]{2,1,0:T(4,128)}), f32[24,4,128]{2,1,0:T(4,128)S(1)}, u32[]{:S(2)}, u32[]{:S(2)}) async-start(f32[24,4,128]{2,1,0:T(4,128)} %get-tuple-element.29), calls=%async_computation.1 | async-start | bytes 98304 | tf_op jit(solution)/shard_map/all_to_all | solution.py:383
  43.7 0.1 maximum_maximum_fusion
  43.8 1.4 %add_multiply_fusion = f32[2,8,17,384]{3,2,1,0:T(8,128)S(1)} fusion(f32[2,8,19,384]{3,2,1,0:T(8,128)S(1)} %get-tuple-element.41, f32[2,8,19,384]{3,2,1,0:T(8,128)S(1)} %get-tuple-element.40, f32[8,17,384]{2,1,0:T(8,128)S(1)} %pad_maximum_fusion.1, pred[8,17,384]{2,1,0:T(8,128)(4,1)S(1)} %broadcast_compare_fusion), kind=kLoop, calls=%fused_computation.28 | loop fusion | flops 6371328 | bytes 3185664 | tf_op jit(solution)/shard_map/mul | solution.py:38
  45.1 0.3 fusion.15
  45.4 8.3 %all-to-all-done.1.got = f32[24,4,128]{2,1,0:T(4,128)S(1)} async-done(((f32[24,4,128]{2,1,0:T(4,128)}), f32[24,4,128]{2,1,0:T(4,128)S(1)}, u32[]{:S(2)}, u32[]{:S(2)}) %all-to-all-start.1) | async-done | bytes 49184 | tf_op jit(solution)/shard_map/all_to_all | solution.py:383
  53.8 0.7 relay.1
  54.4 4.9 %all-to-all-start.2 = ((f32[32,4,128]{2,1,0:T(4,128)}), f32[32,4,128]{2,1,0:T(4,128)S(1)}, u32[]{:S(2)}, u32[]{:S(2)}) async-start(f32[32,4,128]{2,1,0:T(4,128)} %relay.1), calls=%async_computation.2 | async-start | bytes 131072 | tf_op jit(solution)/shard_map/all_to_all | solution.py:387
  59.3 0.8 %slice_bitcast_fusion = (f32[8,16,384]{2,1,0:T(8,128)}, f32[8,16,384]{2,1,0:T(8,128)}) fusion(f32[2,8,16,384]{3,2,1,0:T(8,128)S(1)} %fusion.15), kind=kLoop, calls=%fused_computation.55 | loop fusion | bytes 786432 | tf_op jit(solution)/shard_map/squeeze | solution.py:442
  60.1 8.0 %all-to-all-done.2.got = f32[32,4,128]{2,1,0:T(4,128)S(1)} async-done(((f32[32,4,128]{2,1,0:T(4,128)}), f32[32,4,128]{2,1,0:T(4,128)S(1)}, u32[]{:S(2)}, u32[]{:S(2)}) %all-to-all-start.2) | async-done | bytes 65568 | tf_op jit(solution)/shard_map/all_to_all | solution.py:387
  68.1 0.9 %finish.1 = (f32[16,384]{1,0:T(8,128)}, f32[16,384]{1,0:T(8,128)}, f32[8,16,384]{2,1,0:T(8,128)}, f32[8,16,384]{2,1,0:T(8,128)}) custom-call(f32[4,16,384]{2,1,0:T(8,128)S(1)} %get-tuple-element.27.basis_ref, s32[2,8,128]{2,1,0:T(8,128)S(1)} %get-tuple-element.28.source, ...), custom_call_target="tpu_custom_call", output_to_operand_aliasing={{2}: (6, {}), {3}: (7, {})} | custom-call | tf_op jit(solution)/shard_map/finish/pallas_call | solution.py:420
  (10 shorter events, 0.2 us)
Async XLA Ops:
  0.6 16.3 %copy-start = (f32[8,16,384]{2,1,0:T(8,128)S(1)}, f32[8,16,384]{2,1,0:T(8,128)}, u32[]{:S(2)}) copy-start(f32[8,16,384]{2,1,0:T(8,128)} %t.1) | copy-start | bytes 589828
  0.6 16.3 %copy-start.1 = (f32[8,16,384]{2,1,0:T(8,128)S(1)}, f32[8,16,384]{2,1,0:T(8,128)}, u32[]{:S(2)}) copy-start(f32[8,16,384]{2,1,0:T(8,128)} %s.1) | copy-start | bytes 589828
  0.7 16.3 %copy-start.2 = (f32[8,16,384]{2,1,0:T(8,128)S(1)}, f32[8,16,384]{2,1,0:T(8,128)}, u32[]{:S(2)}) copy-start(f32[8,16,384]{2,1,0:T(8,128)} %u.1) | copy-start | bytes 589828
  0.7 16.3 %copy-start.3 = (f32[8,16,384]{2,1,0:T(8,128)S(1)}, f32[8,16,384]{2,1,0:T(8,128)}, u32[]{:S(2)}) copy-start(f32[8,16,384]{2,1,0:T(8,128)} %v.1) | copy-start | bytes 589828
  3.1 13.8 %copy-start.5 = (s32[16,384]{1,0:T(8,128)S(1)}, s32[16,384]{1,0:T(8,128)}, u32[]{:S(2)}) copy-start(s32[16,384]{1,0:T(8,128)} %flag.1) | copy-start | bytes 73732
  3.1 16.9 %all-to-all-start = ((f32[4,16,128]{2,1,0:T(8,128)}), f32[4,16,128]{2,1,0:T(8,128)S(1)}, u32[]{:S(2)}, u32[]{:S(2)}) async-start(f32[4,16,128]{2,1,0:T(8,128)} %get-tuple-element.20), calls=%async_computation | async-start | bytes 65536 | tf_op jit(solution)/shard_map/all_to_all | solution.py:361
  16.9 0.7 %copy-start.4 = (s32[16,384]{1,0:T(8,128)S(1)}, s32[16,384]{1,0:T(8,128)}, u32[]{:S(2)}) copy-start(s32[16,384]{1,0:T(8,128)} %depth.1) | copy-start | bytes 73732
  20.3 14.9 %collective-permute-start = (f32[88,384]{1,0:T(8,128)S(1)}, f32[88,384]{1,0:T(8,128)S(1)}, u32[]{:S(2)}, u32[]{:S(2)}) collective-permute-start(f32[88,384]{1,0:T(8,128)S(1)} %get-tuple-element.25), channel_id=1, source_target_pairs={{4,8},{8,4},{12,16},{16,12},{20,24},{24,20},{28,32},{32,28},{36,40... | collective-permute-start | bytes 405512 | tf_op jit(solution)/shard_map/ppermute | solution.py:376
  30.9 5.8 %collective-permute-start.1 = (f32[88,384]{1,0:T(8,128)S(1)}, f32[88,384]{1,0:T(8,128)S(1)}, u32[]{:S(2)}, u32[]{:S(2)}) collective-permute-start(f32[88,384]{1,0:T(8,128)S(1)} %get-tuple-element.26), channel_id=1, source_target_pairs={{0,4},{4,0},{8,12},{12,8},{16,20},{20,16},{24,28},{28,24},{32,36},... | collective-permute-start | bytes 405512 | tf_op jit(solution)/shard_map/ppermute | solution.py:375
  37.9 15.9 %all-to-all-start.1 = ((f32[24,4,128]{2,1,0:T(4,128)}), f32[24,4,128]{2,1,0:T(4,128)S(1)}, u32[]{:S(2)}, u32[]{:S(2)}) async-start(f32[24,4,128]{2,1,0:T(4,128)} %get-tuple-element.29), calls=%async_computation.1 | async-start | bytes 98304 | tf_op jit(solution)/shard_map/all_to_all | solution.py:383
  54.4 13.7 %all-to-all-start.2 = ((f32[32,4,128]{2,1,0:T(4,128)}), f32[32,4,128]{2,1,0:T(4,128)S(1)}, u32[]{:S(2)}, u32[]{:S(2)}) async-start(f32[32,4,128]{2,1,0:T(4,128)} %relay.1), calls=%async_computation.2 | async-start | bytes 131072 | tf_op jit(solution)/shard_map/all_to_all | solution.py:387

commit v10 on v9

--- a/solution.py
+++ b/solution.py
@@ -102,7 +102,8 @@
 
 
 def pack_kernel(
-    t, s, u, v, elev, flag, depth, fc, far, close, fields, edges, source, slots_out, slots, tile, sem
+    t, s, u, v, elev, flag, depth, fc,
+    far, close, fields, edges, source, fold_ref, chip_swap, core_swap, tile,
 ):
     nl, ni, nj = t.shape
     ocean = flag[...] == 1
@@ -142,14 +143,17 @@
     fold = mirror16(jnp.concatenate(fold + [none], axis=0))
     north = jnp.concatenate([t_end, s_end, v_end, none[:1]], axis=0)
     south = jnp.concatenate([turned[0:3], turned[8:11], none], axis=0)
-    for p in range(4):
-        ahead = p > lat
-        slots[p, 0:8] = jnp.where(ahead, north, south)
-        slots[p, 8:12] = jnp.where(ahead, turned[100:104], turned[16:20])
-        slots[p, 12:15] = fold[0:3] if p < 2 else fold[3:6]
-        slots[p, 15:16] = none[:1]
-    copy = pltpu.make_async_copy(slots, slots_out, sem)
-    copy.start()
+    fold_ref[...] = fold
+    ahead = lax.rem(lat, 2) == 0
+    core_swap[0:8] = jnp.where(ahead, north, south)
+    core_swap[8:12] = jnp.where(ahead, turned[100:104], turned[16:20])
+    core_swap[12:15] = fold[0:3]
+    core_swap[15:16] = none[:1]
+    ahead = lat == 1
+    chip_swap[0:8] = jnp.where(ahead, north, south)
+    chip_swap[8:12] = jnp.where(ahead, turned[100:104], turned[16:20])
+    chip_swap[12:14] = none
+    chip_swap[14:16] = none
 
     even = lon_even()
     zero = jnp.zeros((2, nj), jnp.float32)
@@ -163,21 +167,34 @@
         far[8 * l : 8 * l + 8] = jnp.where(even, west_edge, east_edge)
         close[8 * l : 8 * l + 8] = jnp.where(even, east_edge, west_edge)
     block = lax.shift_right_logical(jnp.broadcast_to(fc[0:1, 0:1], (8, 128)), 4)
-    row = jnp.zeros((8, 128), jnp.int32)
     nz = lax.axis_size("z")
-    for k in range(1, lax.axis_size("y") * lax.axis_size("xh")):
-        row = row + jnp.where(block >= nz * k, 1, 0)
-    source[0] = block - nz * row
-    source[1] = row
-    copy.wait()
-
-
-def widen_kernel(got, fields, far_q, close_q, far, close, beyond, rims, tile, up, down):
+    columns = lax.axis_size("y") * lax.axis_size("xh")
+    column = lax.axis_index("y") * lax.axis_size("xh") + lax.axis_index("xh")
+    place = lax.axis_index("z")
+
+    def column_of(x):
+        count = jnp.zeros((8, 128), jnp.int32)
+        for k in range(1, columns):
+            count = count + jnp.where(x >= nz * k, 1, 0)
+        return count
+
+    total = block + (nz * column + place)
+    total = jnp.where(total >= nz * columns, total - nz * columns, total)
+    ahead = total - nz * column_of(total) - place
+    ahead = jnp.where(ahead < 0, ahead + nz, ahead)
+    origin = total - (nz * column + ahead)
+    origin = jnp.where(origin < 0, origin + nz * columns, origin)
+    source[0] = column_of(origin)
+    source[1] = block - nz * column_of(block)
+
+
+def widen_kernel(chip_got, core_got, fields, far_q, close_q, far, close, beyond, rims, tile, up, down):
     _, ni, nj = fields.shape
     lat = lat_index()
     even = lon_even()
-    north = jnp.where(lat < 3, got[jnp.minimum(lat + 1, 3)], 0.0)
-    south = jnp.where(lat > 0, got[jnp.maximum(lat - 1, 0)], 0.0)
+    odd = lax.rem(lat, 2) == 1
+    north = jnp.where(lat < 3, jnp.where(odd, chip_got[...], core_got[...]), 0.0)
+    south = jnp.where(lat > 0, jnp.where(odd, core_got[...], chip_got[...]), 0.0)
     rims[0] = north[0:8]
     rims[1] = south[0:8]
     tile[...] = jnp.zeros((128, 128), jnp.float32)
@@ -203,7 +220,7 @@
         out[80:88, 256:384] = jnp.zeros((8, 128), jnp.float32)
 
 
-def krylov_kernel(got, fields, beyond, far, close, basis_ref, message, wide, west, east):
+def krylov_kernel(core_got, fold, fields, beyond, far, close, basis_ref, message, wide, west, east):
     _, ni, nj = fields.shape
     even = lon_even()
     for out, first, second in ((west, far, close), (east, close, far)):
@@ -244,7 +261,8 @@
         basis_ref[k] = basis[k]
     row = lax.broadcasted_iota(jnp.int32, (4, 128), 0)
     col = lax.broadcasted_iota(jnp.int32, (4, 128), 1)
-    total = jnp.concatenate([got[3, 12:15], jnp.zeros((1, 128), jnp.float32)], axis=0)
+    piece = jnp.where(lat_index() == 3, fold[3:6], core_got[12:15])
+    total = jnp.concatenate([piece, jnp.zeros((1, 128), jnp.float32)], axis=0)
     for n, (i, j) in enumerate(PAIRS):
         prod = basis[i] * basis[j]
         prod = prod[:8] + prod[8:]
@@ -263,9 +281,9 @@
     for k in range(1, peers):
         total = total + got[k]
     which = source[0, 0:4]
-    piece = got[0]
-    for z in range(1, peers // 2):
-        piece = jnp.where(which == z, got[2 * z], piece)
+    piece = got[1]
+    for k in range(1, peers // 2):
+        piece = jnp.where(which == k, got[2 * k + 1], piece)
     row = lax.broadcasted_iota(jnp.int32, (4, 128), 0)
     text = jnp.where(row < 3, piece, total)
     for k in range(message.shape[0]):
@@ -343,7 +361,7 @@
         last = lat == n_lat - 1
         hbm, local = pl.BlockSpec(memory_space=pl.ANY), pl.BlockSpec(memory_space=pltpu.VMEM)
 
-        far, close, fields, edges, source, slots = pl.pallas_call(
+        far, close, fields, edges, source, fold, chip_swap, core_swap = pl.pallas_call(
             pack_kernel,
             out_shape=(
                 vmem(64, nj),
@@ -351,20 +369,21 @@
                 vmem(4, ni, nj),
                 vmem(40, 128),
                 pltpu.VMEM((2, 8, 128), jnp.int32),
-                f32(4, 16, 128),
+                vmem(8, 128),
+                vmem(16, 128),
+                vmem(16, 128),
             ),
-            in_specs=[local] * 8,
-            out_specs=(local,) * 5 + (hbm,),
-            scratch_shapes=[vmem(4, 16, 128), vmem(128, 128), pltpu.SemaphoreType.DMA],
+            scratch_shapes=[vmem(128, 128)],
             name="pack",
         )(t, s, u, v, elev, flag, depth, fc.reshape(1, ni))
-        halo = lax.all_to_all(slots, LAT, 0, 0)
+        chip_got = lax.ppermute(chip_swap, LAT, [(1, 2), (2, 1)])
+        core_got = lax.ppermute(core_swap, LAT, [(0, 1), (1, 0), (2, 3), (3, 2)])
         far, close, beyond, rims = pl.pallas_call(
             widen_kernel,
             out_shape=(vmem(88, nj), vmem(88, nj), vmem(4, ni, 128), vmem(2, 8, 128)),
             scratch_shapes=[vmem(128, 128), vmem(16, nj + 128), vmem(16, nj + 128)],
             name="widen",
-        )(near(halo), near(fields), near(far), near(close))
+        )(near(chip_got), near(core_got), near(fields), near(far), near(close))
 
         def swaps(first):
             pairs = []
@@ -376,15 +395,15 @@
         far = lax.ppermute(far, LON, swaps(1))
         basis, message = pl.pallas_call(
             krylov_kernel,
-            out_shape=(vmem(4, ni, nj), vmem(nz * ncore, 4, 128)),
+            out_shape=(vmem(4, ni, nj), vmem(ny * nxh * nxl, 4, 128)),
             scratch_shapes=[vmem(4, 32, nj + 128), vmem(16, nj + 128), vmem(16, nj + 128)],
             name="krylov",
-        )(near(halo), near(fields), near(beyond), near(far), near(close))
+        )(near(core_got), near(fold), near(fields), near(beyond), near(far), near(close))
+        got = lax.all_to_all(message, ("y", "xh", "xl"), 0, 0)
+        message = pl.pallas_call(
+            relay_kernel, out_shape=vmem(nz * ncore, 4, 128), name="relay"
+        )(near(source), near(got))
         got = lax.all_to_all(message, ("z", "core"), 0, 0)
-        message = pl.pallas_call(
-            relay_kernel, out_shape=vmem(ny * nxh * nxl, 4, 128), name="relay"
-        )(near(source), near(got))
-        got = lax.all_to_all(message, ("y", "xh", "xl"), 0, 0)
         level = lax.broadcasted_iota(jnp.int32, t.shape, 0)
         mask = jnp.where((flag[None] == 1) & (level < depth[None]), 1.0, 0.0).astype(jnp.float32)
         q = jnp.stack([t * mask, s * mask])

time: 69.5 us -> 70 us (level)
  starting transfers between devices: 37 us -> 38.2 us
    ppermute x0 -> x2, starting transfers between devices: none -> 14.5 us  [the longest x1 12.6 us: on_device(): core_got = lax.ppermute(core_swap, LAT, [(0, 1), (1, 0), (2, 3), (3, 2)])]
    all_to_all x1 -> x0, starting transfers between devices: 13.8 us -> none  [on_device(): halo = lax.all_to_all(slots, LAT, 0, 0)]
    ppermute x0 -> x2, waiting for transfers between devices: none -> 2.82 us  [the longest x1 2.81 us: on_device(): chip_got = lax.ppermute(chip_swap, LAT, [(1, 2), (2, 1)])]
    all_to_all x1 -> x0, waiting for transfers between devices: 2.29 us -> none  [on_device(): halo = lax.all_to_all(slots, LAT, 0, 0)]
    all_to_all x1, starting transfers between devices: 5.73 us -> 6.87 us  [on_device(): got = lax.all_to_all(message, ('z', 'core'), 0, 0)]
    all_to_all x1, waiting for transfers between devices: 8.34 us -> 9.37 us  [on_device(): got = lax.all_to_all(message, ('z', 'core'), 0, 0)]
    all_to_all x1, waiting for transfers between devices: 8.05 us -> 7.09 us  [on_device(): got = lax.all_to_all(message, ('y', 'xh', 'xl'), 0, 0)]
  transfers between devices with their start and end apart: 5 -> 6, of which waited for: 4 -> 4; matrix products, arithmetic and copies ran while one was open for 7% -> 7% of each run, Pallas kernels for 0% -> 0%
where the time goes in v10:
time: 70 us; the launch traced here: 69.6 us
  starting transfers between devices  38.2 us (55%)
  waiting for transfers between devices  20.8 us (30%)
  Pallas kernels  4.54 us (6%)
  other arithmetic  3.53 us (5%)
  local copies, waits for them, and re-layouts  1.58 us (2%)
  between operations  0.94 us (1%)
    ppermute x1, starting transfers between devices, on_device(): core_got = lax.ppermute(core_swap, LAT, [(0, 1), (1, 0), (2, 3), (3, 2)])  12.6 us
    ppermute x1, starting transfers between devices, on_device(): far = lax.ppermute(far, LON, swaps(1))  10.7 us
    all_to_all x1, waiting for transfers between devices, on_device(): got = lax.all_to_all(message, ('z', 'core'), 0, 0)  9.37 us
    all_to_all x1, waiting for transfers between devices, on_device(): got = lax.all_to_all(message, ('y', 'xh', 'xl'), 0, 0)  7.09 us
    all_to_all x1, starting transfers between devices, on_device(): got = lax.all_to_all(message, ('z', 'core'), 0, 0)  6.87 us
    all_to_all x1, starting transfers between devices, on_device(): got = lax.all_to_all(message, ('y', 'xh', 'xl'), 0, 0)  4.3 us
    ppermute x1, waiting for transfers between devices, on_device(): chip_got = lax.ppermute(chip_swap, LAT, [(1, 2), (2, 1)])  2.81 us
    mul x2, other arithmetic, face_flux(): return speed * weno_upwind(a, b, c, d, e)  2.61 us
  transfers between devices with their start and end apart: 6, of which 4 were waited for; matrix products, arithmetic and copies ran while one was open for 7% of the time, Pallas kernels for 0%

profile of v10, /device:TPU:1, one launch (start us, length us, event | category | flops | bytes accessed | tf_op | source)
XLA Modules:
  0.0 69.6 jit_solution(12293208569836622576)
XLA Ops:
  0.6 0.0 copy-start.5
  0.6 0.0 copy-start
  0.7 0.0 copy-start.1
  0.7 0.0 copy-start.2
  0.7 0.0 copy-start.3
  0.7 1.8 %pack.1 = (f32[64,384]{1,0:T(8,128)S(1)}, f32[64,384]{1,0:T(8,128)S(1)}, f32[4,16,384]{2,1,0:T(8,128)S(1)}, f32[40,128]{1,0:T(8,128)S(1)}, s32[2,8,128]{2,1,0:T(...) custom-call(f32[8,16,384]{2,1,0:T(8,128)} %t.1, f32[8,16,384]{2,1,0:T(8,128)} %s.1, ...), custom_call_target="tpu_custom_call" | custom-call | tf_op jit(solution)/shard_map/pack/pallas_call | solution.py:364
  2.5 0.0 copy-start.4
  2.5 12.6 %collective-permute-start = (f32[16,128]{1,0:T(8,128)S(1)}, f32[16,128]{1,0:T(8,128)S(1)}, u32[]{:S(2)}, u32[]{:S(2)}) collective-permute-start(f32[16,128]{1,0:T(8,128)S(1)} %get-tuple-element.22), channel_id=1, source_target_pairs={{0,1},{1,0},{2,3},{3,2},{4,5},{5,4},{6,7},{7,6},{8,9},{9,8},{10,11... | collective-permute-start | bytes 24584 | tf_op jit(solution)/shard_map/ppermute | solution.py:380
  15.1 1.9 %collective-permute-start.1 = (f32[16,128]{1,0:T(8,128)S(1)}, f32[16,128]{1,0:T(8,128)S(1)}, u32[]{:S(2)}, u32[]{:S(2)}) collective-permute-start(f32[16,128]{1,0:T(8,128)S(1)} %get-tuple-element.25), channel_id=1, source_target_pairs={{1,2},{2,1},{5,6},{6,5},{9,10},{10,9},{13,14},{14,13},{17,18},{18,... | collective-permute-start | bytes 24584 | tf_op jit(solution)/shard_map/ppermute | solution.py:379
  17.0 0.0 copy-done.5
  17.0 0.0 copy-done
  17.0 0.0 copy-done.1
  17.1 0.0 copy-done.2
  17.1 0.0 copy-done.3
  17.1 0.0 copy-done.4
  17.1 0.1 fusion.20
  17.2 0.0 collective-permute-done.core_got
  17.2 2.8 %collective-permute-done.1.chip_got = f32[16,128]{1,0:T(8,128)S(1)} collective-permute-done((f32[16,128]{1,0:T(8,128)S(1)}, f32[16,128]{1,0:T(8,128)S(1)}, u32[]{:S(2)}, u32[]{:S(2)}) %collective-permute-start.1) | collective-permute-done | bytes 8224 | tf_op jit(solution)/shard_map/ppermute | solution.py:379
  20.0 0.1 widen.1
  20.2 10.7 %collective-permute-start.2 = (f32[88,384]{1,0:T(8,128)S(1)}, f32[88,384]{1,0:T(8,128)S(1)}, u32[]{:S(2)}, u32[]{:S(2)}) collective-permute-start(f32[88,384]{1,0:T(8,128)S(1)} %get-tuple-element.29), channel_id=1, source_target_pairs={{4,8},{8,4},{12,16},{16,12},{20,24},{24,20},{28,32},{32,28},{36,40... | collective-permute-start | bytes 405512 | tf_op jit(solution)/shard_map/ppermute | solution.py:395
  30.9 1.9 %collective-permute-start.3 = (f32[88,384]{1,0:T(8,128)S(1)}, f32[88,384]{1,0:T(8,128)S(1)}, u32[]{:S(2)}, u32[]{:S(2)}) collective-permute-start(f32[88,384]{1,0:T(8,128)S(1)} %get-tuple-element.30), channel_id=1, source_target_pairs={{0,4},{4,0},{8,12},{12,8},{16,20},{20,16},{24,28},{28,24},{32,36},... | collective-permute-start | bytes 405512 | tf_op jit(solution)/shard_map/ppermute | solution.py:394
  32.8 0.1 reshape.93
  32.9 0.2 copy.19
  33.1 0.1 reshape.94
  33.1 0.2 copy.20
  33.3 0.2 concatenate.48
  33.5 0.1 broadcast_compare_fusion.1
  33.7 0.2 maximum_maximum_fusion.2
  33.9 1.2 %add_multiply_fusion.1 = f32[2,8,16,385]{3,2,1,0:T(8,128)S(1)} fusion(f32[2,8,16,387]{3,2,1,0:T(8,128)S(1)} %get-tuple-element.47, f32[2,8,16,387]{3,2,1,0:T(8,128)S(1)} %get-tuple-element.46, f32[8,16,385]{2,1,0:T(8,128)S(1)} %get-tuple-element.41, pred[8,16,385]{2,1,0:T(8,128)(4,1)S(1)} %get-tuple-element.40), kind=kLoop, calls=%fused_computation.40 | loop fusion | flops 6012160 | bytes 3006080 | tf_op jit(solution)/shard_map/mul | solution.py:38
  35.1 0.0 collective-permute-done.2.far
  35.1 1.5 %collective-permute-done.3.close = f32[88,384]{1,0:T(8,128)S(1)} collective-permute-done((f32[88,384]{1,0:T(8,128)S(1)}, f32[88,384]{1,0:T(8,128)S(1)}, u32[]{:S(2)}, u32[]{:S(2)}) %collective-permute-start.3) | collective-permute-done | bytes 135200 | tf_op jit(solution)/shard_map/ppermute | solution.py:394
  36.7 0.1 broadcast_compare_fusion
  36.8 1.1 %krylov.1 = (f32[4,16,384]{2,1,0:T(8,128)S(1)}, f32[32,4,128]{2,1,0:T(4,128)}) custom-call(f32[16,128]{1,0:T(8,128)S(1)} %collective-permute-done.core_got, f32[8,128]{1,0:T(8,128)S(1)} %get-tuple-element.23.fold, f32[4,16,384]{2,1,0:T(8,128)S(1)} %get-tuple-element.24.fields, f32[4,16,128]{2,1,0:T(8,128)S(1)} %get-tuple-element.28.beyond, ...), custom_call_target="tpu_custom_call" | custom-call | tf_op jit(solution)/shard_map/krylov/pallas_call | solution.py:396
  37.9 4.3 %all-to-all-start = ((f32[32,4,128]{2,1,0:T(4,128)}), f32[32,4,128]{2,1,0:T(4,128)S(1)}, u32[]{:S(2)}, u32[]{:S(2)}) async-start(f32[32,4,128]{2,1,0:T(4,128)} %get-tuple-element.33), calls=%async_computation | async-start | bytes 131072 | tf_op jit(solution)/shard_map/all_to_all | solution.py:402
  42.2 0.1 maximum_maximum_fusion
  42.3 1.4 %add_multiply_fusion = f32[2,8,17,384]{3,2,1,0:T(8,128)S(1)} fusion(f32[2,8,19,384]{3,2,1,0:T(8,128)S(1)} %get-tuple-element.45, f32[2,8,19,384]{3,2,1,0:T(8,128)S(1)} %get-tuple-element.44, f32[8,17,384]{2,1,0:T(8,128)S(1)} %pad_maximum_fusion.1, pred[8,17,384]{2,1,0:T(8,128)(4,1)S(1)} %broadcast_compare_fusion), kind=kLoop, calls=%fused_computation.28 | loop fusion | flops 6371328 | bytes 3185664 | tf_op jit(solution)/shard_map/mul | solution.py:38
  43.7 0.3 fusion.15
  44.0 7.1 %all-to-all-done.got = f32[32,4,128]{2,1,0:T(4,128)S(1)} async-done(((f32[32,4,128]{2,1,0:T(4,128)}), f32[32,4,128]{2,1,0:T(4,128)S(1)}, u32[]{:S(2)}, u32[]{:S(2)}) %all-to-all-start) | async-done | bytes 65568 | tf_op jit(solution)/shard_map/all_to_all | solution.py:402
  51.1 0.7 relay.1
  51.7 6.9 %all-to-all-start.1 = ((f32[24,4,128]{2,1,0:T(4,128)}), f32[24,4,128]{2,1,0:T(4,128)S(1)}, u32[]{:S(2)}, u32[]{:S(2)}) async-start(f32[24,4,128]{2,1,0:T(4,128)} %relay.1), calls=%async_computation.1 | async-start | bytes 98304 | tf_op jit(solution)/shard_map/all_to_all | solution.py:406
  58.6 0.8 %slice_bitcast_fusion = (f32[8,16,384]{2,1,0:T(8,128)}, f32[8,16,384]{2,1,0:T(8,128)}) fusion(f32[2,8,16,384]{3,2,1,0:T(8,128)S(1)} %fusion.15), kind=kLoop, calls=%fused_computation.55 | loop fusion | bytes 786432 | tf_op jit(solution)/shard_map/squeeze | solution.py:461
  59.4 9.4 %all-to-all-done.1.got = f32[24,4,128]{2,1,0:T(4,128)S(1)} async-done(((f32[24,4,128]{2,1,0:T(4,128)}), f32[24,4,128]{2,1,0:T(4,128)S(1)}, u32[]{:S(2)}, u32[]{:S(2)}) %all-to-all-start.1) | async-done | bytes 49184 | tf_op jit(solution)/shard_map/all_to_all | solution.py:406
  68.7 0.9 %finish.1 = (f32[16,384]{1,0:T(8,128)}, f32[16,384]{1,0:T(8,128)}, f32[8,16,384]{2,1,0:T(8,128)}, f32[8,16,384]{2,1,0:T(8,128)}) custom-call(f32[4,16,384]{2,1,0:T(8,128)S(1)} %get-tuple-element.31.basis_ref, s32[2,8,128]{2,1,0:T(8,128)S(1)} %get-tuple-element.32.source, ...), custom_call_target="tpu_custom_call", output_to_operand_aliasing={{2}: (6, {}), {3}: (7, {})} | custom-call | tf_op jit(solution)/shard_map/finish/pallas_call | solution.py:439
  (10 shorter events, 0.1 us)
Async XLA Ops:
  0.6 16.4 %copy-start.5 = (s32[16,384]{1,0:T(8,128)S(1)}, s32[16,384]{1,0:T(8,128)}, u32[]{:S(2)}) copy-start(s32[16,384]{1,0:T(8,128)} %flag.1) | copy-start | bytes 73732
  0.6 16.4 %copy-start = (f32[8,16,384]{2,1,0:T(8,128)S(1)}, f32[8,16,384]{2,1,0:T(8,128)}, u32[]{:S(2)}) copy-start(f32[8,16,384]{2,1,0:T(8,128)} %t.1) | copy-start | bytes 589828
  0.7 16.4 %copy-start.1 = (f32[8,16,384]{2,1,0:T(8,128)S(1)}, f32[8,16,384]{2,1,0:T(8,128)}, u32[]{:S(2)}) copy-start(f32[8,16,384]{2,1,0:T(8,128)} %s.1) | copy-start | bytes 589828
  0.7 16.4 %copy-start.2 = (f32[8,16,384]{2,1,0:T(8,128)S(1)}, f32[8,16,384]{2,1,0:T(8,128)}, u32[]{:S(2)}) copy-start(f32[8,16,384]{2,1,0:T(8,128)} %u.1) | copy-start | bytes 589828
  0.7 16.4 %copy-start.3 = (f32[8,16,384]{2,1,0:T(8,128)S(1)}, f32[8,16,384]{2,1,0:T(8,128)}, u32[]{:S(2)}) copy-start(f32[8,16,384]{2,1,0:T(8,128)} %v.1) | copy-start | bytes 589828
  2.5 14.6 %copy-start.4 = (s32[16,384]{1,0:T(8,128)S(1)}, s32[16,384]{1,0:T(8,128)}, u32[]{:S(2)}) copy-start(s32[16,384]{1,0:T(8,128)} %depth.1) | copy-start | bytes 73732
  2.5 14.7 %collective-permute-start = (f32[16,128]{1,0:T(8,128)S(1)}, f32[16,128]{1,0:T(8,128)S(1)}, u32[]{:S(2)}, u32[]{:S(2)}) collective-permute-start(f32[16,128]{1,0:T(8,128)S(1)} %get-tuple-element.22), channel_id=1, source_target_pairs={{0,1},{1,0},{2,3},{3,2},{4,5},{5,4},{6,7},{7,6},{8,9},{9,8},{10,11... | collective-permute-start | bytes 24584 | tf_op jit(solution)/shard_map/ppermute | solution.py:380
  15.1 5.0 %collective-permute-start.1 = (f32[16,128]{1,0:T(8,128)S(1)}, f32[16,128]{1,0:T(8,128)S(1)}, u32[]{:S(2)}, u32[]{:S(2)}) collective-permute-start(f32[16,128]{1,0:T(8,128)S(1)} %get-tuple-element.25), channel_id=1, source_target_pairs={{1,2},{2,1},{5,6},{6,5},{9,10},{10,9},{13,14},{14,13},{17,18},{18,... | collective-permute-start | bytes 24584 | tf_op jit(solution)/shard_map/ppermute | solution.py:379
  20.2 14.9 %collective-permute-start.2 = (f32[88,384]{1,0:T(8,128)S(1)}, f32[88,384]{1,0:T(8,128)S(1)}, u32[]{:S(2)}, u32[]{:S(2)}) collective-permute-start(f32[88,384]{1,0:T(8,128)S(1)} %get-tuple-element.29), channel_id=1, source_target_pairs={{4,8},{8,4},{12,16},{16,12},{20,24},{24,20},{28,32},{32,28},{36,40... | collective-permute-start | bytes 405512 | tf_op jit(solution)/shard_map/ppermute | solution.py:395
  30.9 5.8 %collective-permute-start.3 = (f32[88,384]{1,0:T(8,128)S(1)}, f32[88,384]{1,0:T(8,128)S(1)}, u32[]{:S(2)}, u32[]{:S(2)}) collective-permute-start(f32[88,384]{1,0:T(8,128)S(1)} %get-tuple-element.30), channel_id=1, source_target_pairs={{0,4},{4,0},{8,12},{12,8},{16,20},{20,16},{24,28},{28,24},{32,36},... | collective-permute-start | bytes 405512 | tf_op jit(solution)/shard_map/ppermute | solution.py:394
  37.9 13.2 %all-to-all-start = ((f32[32,4,128]{2,1,0:T(4,128)}), f32[32,4,128]{2,1,0:T(4,128)S(1)}, u32[]{:S(2)}, u32[]{:S(2)}) async-start(f32[32,4,128]{2,1,0:T(4,128)} %get-tuple-element.33), calls=%async_computation | async-start | bytes 131072 | tf_op jit(solution)/shard_map/all_to_all | solution.py:402
  51.7 17.0 %all-to-all-start.1 = ((f32[24,4,128]{2,1,0:T(4,128)}), f32[24,4,128]{2,1,0:T(4,128)S(1)}, u32[]{:S(2)}, u32[]{:S(2)}) async-start(f32[24,4,128]{2,1,0:T(4,128)} %relay.1), calls=%async_computation.1 | async-start | bytes 98304 | tf_op jit(solution)/shard_map/all_to_all | solution.py:406

commit v11 on v10

--- a/solution.py
+++ b/solution.py
@@ -188,13 +188,17 @@
     source[1] = block - nz * column_of(block)
 
 
-def widen_kernel(chip_got, core_got, fields, far_q, close_q, far, close, beyond, rims, tile, up, down):
+def widen_kernel(
+    chip_got, core_got, fold, fields, far_q, close_q, far, close, beyond, rims, piece, tile, up, down
+):
     _, ni, nj = fields.shape
     lat = lat_index()
     even = lon_even()
     odd = lax.rem(lat, 2) == 1
     north = jnp.where(lat < 3, jnp.where(odd, chip_got[...], core_got[...]), 0.0)
     south = jnp.where(lat > 0, jnp.where(odd, core_got[...], chip_got[...]), 0.0)
+    piece[0:3] = jnp.where(lat == 3, fold[3:6], core_got[12:15])
+    piece[3:8] = jnp.zeros((5, 128), jnp.float32)
     rims[0] = north[0:8]
     rims[1] = south[0:8]
     tile[...] = jnp.zeros((128, 128), jnp.float32)
@@ -220,7 +224,7 @@
         out[80:88, 256:384] = jnp.zeros((8, 128), jnp.float32)
 
 
-def krylov_kernel(core_got, fold, fields, beyond, far, close, basis_ref, message, wide, west, east):
+def krylov_kernel(piece, fields, beyond, far, close, basis_ref, message, wide, west, east):
     _, ni, nj = fields.shape
     even = lon_even()
     for out, first, second in ((west, far, close), (east, close, far)):
@@ -261,8 +265,7 @@
         basis_ref[k] = basis[k]
     row = lax.broadcasted_iota(jnp.int32, (4, 128), 0)
     col = lax.broadcasted_iota(jnp.int32, (4, 128), 1)
-    piece = jnp.where(lat_index() == 3, fold[3:6], core_got[12:15])
-    total = jnp.concatenate([piece, jnp.zeros((1, 128), jnp.float32)], axis=0)
+    total = piece[0:4]
     for n, (i, j) in enumerate(PAIRS):
         prod = basis[i] * basis[j]
         prod = prod[:8] + prod[8:]
@@ -378,12 +381,12 @@
         )(t, s, u, v, elev, flag, depth, fc.reshape(1, ni))
         chip_got = lax.ppermute(chip_swap, LAT, [(1, 2), (2, 1)])
         core_got = lax.ppermute(core_swap, LAT, [(0, 1), (1, 0), (2, 3), (3, 2)])
-        far, close, beyond, rims = pl.pallas_call(
+        far, close, beyond, rims, piece = pl.pallas_call(
             widen_kernel,
-            out_shape=(vmem(88, nj), vmem(88, nj), vmem(4, ni, 128), vmem(2, 8, 128)),
+            out_shape=(vmem(88, nj), vmem(88, nj), vmem(4, ni, 128), vmem(2, 8, 128), vmem(8, 128)),
             scratch_shapes=[vmem(128, 128), vmem(16, nj + 128), vmem(16, nj + 128)],
             name="widen",
-        )(near(chip_got), near(core_got), near(fields), near(far), near(close))
+        )(near(chip_got), near(core_got), near(fold), near(fields), near(far), near(close))
 
         def swaps(first):
             pairs = []
@@ -398,7 +401,7 @@
             out_shape=(vmem(4, ni, nj), vmem(ny * nxh * nxl, 4, 128)),
             scratch_shapes=[vmem(4, 32, nj + 128), vmem(16, nj + 128), vmem(16, nj + 128)],
             name="krylov",
-        )(near(core_got), near(fold), near(fields), near(beyond), near(far), near(close))
+        )(near(piece), near(fields), near(beyond), near(far), near(close))
         got = lax.all_to_all(message, ("y", "xh", "xl"), 0, 0)
         message = pl.pallas_call(
             relay_kernel, out_shape=vmem(nz * ncore, 4, 128), name="relay"

time: 70 us -> 69.7 us (level)
  waiting for transfers between devices: 20.8 us -> 19.3 us
  starting transfers between devices: 38.2 us -> 39.4 us
    ppermute x1, starting transfers between devices: 12.6 us -> 8.58 us  [on_device(): core_got = lax.ppermute(core_swap, LAT, [(0, 1), (1, 0), (2, 3), (3, 2)])]
    ppermute x1, waiting for transfers between devices: 2.81 us -> 0.01 us  [on_device(): chip_got = lax.ppermute(chip_swap, LAT, [(1, 2), (2, 1)])]
    ppermute x1, starting transfers between devices: 1.92 us -> 4.64 us  [on_device(): chip_got = lax.ppermute(chip_swap, LAT, [(1, 2), (2, 1)])]
    ppermute x1, starting transfers between devices: 10.7 us -> 13.1 us  [on_device(): far = lax.ppermute(far, LON, swaps(1))]
    ppermute x1, waiting for transfers between devices: 1.49 us -> 2.33 us  [on_device(): close = lax.ppermute(close, LON, swaps(0))]
where the time goes in v11:
time: 69.7 us; the launch traced here: 69.3 us
  starting transfers between devices  39.4 us (57%)
  waiting for transfers between devices  19.3 us (28%)
  Pallas kernels  4.54 us (7%)
  other arithmetic  3.54 us (5%)
  local copies, waits for them, and re-layouts  1.58 us (2%)
  between operations  0.94 us (1%)
    ppermute x1, starting transfers between devices, on_device(): far = lax.ppermute(far, LON, swaps(1))  13.1 us
    all_to_all x1, waiting for transfers between devices, on_device(): got = lax.all_to_all(message, ('z', 'core'), 0, 0)  9.32 us
    ppermute x1, starting transfers between devices, on_device(): core_got = lax.ppermute(core_swap, LAT, [(0, 1), (1, 0), (2, 3), (3, 2)])  8.58 us
    all_to_all x1, waiting for transfers between devices, on_device(): got = lax.all_to_all(message, ('y', 'xh', 'xl'), 0, 0)  7.04 us
    all_to_all x1, starting transfers between devices, on_device(): got = lax.all_to_all(message, ('z', 'core'), 0, 0)  6.68 us
    ppermute x1, starting transfers between devices, on_device(): chip_got = lax.ppermute(chip_swap, LAT, [(1, 2), (2, 1)])  4.64 us
    all_to_all x1, starting transfers between devices, on_device(): got = lax.all_to_all(message, ('y', 'xh', 'xl'), 0, 0)  4.54 us
    mul x2, other arithmetic, face_flux(): return speed * weno_upwind(a, b, c, d, e)  2.61 us
  transfers between devices with their start and end apart: 6, of which 4 were waited for; matrix products, arithmetic and copies ran while one was open for 7% of the time, Pallas kernels for 0%

profile of v11, /device:TPU:1, one launch (start us, length us, event | category | flops | bytes accessed | tf_op | source)
XLA Modules:
  0.0 69.3 jit_solution(7792568420683648041)
XLA Ops:
  0.6 0.0 copy-start.5
  0.6 0.0 copy-start
  0.7 0.0 copy-start.1
  0.7 0.0 copy-start.2
  0.7 0.0 copy-start.3
  0.7 1.8 %pack.1 = (f32[64,384]{1,0:T(8,128)S(1)}, f32[64,384]{1,0:T(8,128)S(1)}, f32[4,16,384]{2,1,0:T(8,128)S(1)}, f32[40,128]{1,0:T(8,128)S(1)}, s32[2,8,128]{2,1,0:T(...) custom-call(f32[8,16,384]{2,1,0:T(8,128)} %t.1, f32[8,16,384]{2,1,0:T(8,128)} %s.1, ...), custom_call_target="tpu_custom_call" | custom-call | tf_op jit(solution)/shard_map/pack/pallas_call | solution.py:367
  2.5 0.0 copy-start.4
  2.5 4.6 %collective-permute-start = (f32[16,128]{1,0:T(8,128)S(1)}, f32[16,128]{1,0:T(8,128)S(1)}, u32[]{:S(2)}, u32[]{:S(2)}) collective-permute-start(f32[16,128]{1,0:T(8,128)S(1)} %get-tuple-element.23), channel_id=1, source_target_pairs={{1,2},{2,1},{5,6},{6,5},{9,10},{10,9},{13,14},{14,13},{17,18},{18,... | collective-permute-start | bytes 24584 | tf_op jit(solution)/shard_map/ppermute | solution.py:382
  7.2 8.6 %collective-permute-start.1 = (f32[16,128]{1,0:T(8,128)S(1)}, f32[16,128]{1,0:T(8,128)S(1)}, u32[]{:S(2)}, u32[]{:S(2)}) collective-permute-start(f32[16,128]{1,0:T(8,128)S(1)} %get-tuple-element.24), channel_id=1, source_target_pairs={{0,1},{1,0},{2,3},{3,2},{4,5},{5,4},{6,7},{7,6},{8,9},{9,8},{10,11... | collective-permute-start | bytes 24584 | tf_op jit(solution)/shard_map/ppermute | solution.py:383
  15.7 0.0 copy-done.5
  15.8 0.0 copy-done
  15.8 0.0 copy-done.1
  15.8 0.0 copy-done.2
  15.8 0.0 copy-done.3
  15.8 0.0 copy-done.4
  15.8 0.1 fusion.20
  16.0 0.0 collective-permute-done.chip_got
  16.0 0.6 collective-permute-done.1.core_got
  16.6 0.1 widen.1
  16.7 13.1 %collective-permute-start.2 = (f32[88,384]{1,0:T(8,128)S(1)}, f32[88,384]{1,0:T(8,128)S(1)}, u32[]{:S(2)}, u32[]{:S(2)}) collective-permute-start(f32[88,384]{1,0:T(8,128)S(1)} %get-tuple-element.31), channel_id=1, source_target_pairs={{4,8},{8,4},{12,16},{16,12},{20,24},{24,20},{28,32},{32,28},{36,40... | collective-permute-start | bytes 405512 | tf_op jit(solution)/shard_map/ppermute | solution.py:398
  29.8 1.9 %collective-permute-start.3 = (f32[88,384]{1,0:T(8,128)S(1)}, f32[88,384]{1,0:T(8,128)S(1)}, u32[]{:S(2)}, u32[]{:S(2)}) collective-permute-start(f32[88,384]{1,0:T(8,128)S(1)} %get-tuple-element.32), channel_id=1, source_target_pairs={{0,4},{4,0},{8,12},{12,8},{16,20},{20,16},{24,28},{28,24},{32,36},... | collective-permute-start | bytes 405512 | tf_op jit(solution)/shard_map/ppermute | solution.py:397
  31.7 0.1 reshape.93
  31.8 0.2 copy.19
  32.0 0.1 reshape.94
  32.0 0.2 copy.20
  32.2 0.2 concatenate.48
  32.4 0.1 broadcast_compare_fusion.1
  32.6 0.2 maximum_maximum_fusion.2
  32.8 1.3 %add_multiply_fusion.1 = f32[2,8,16,385]{3,2,1,0:T(8,128)S(1)} fusion(f32[2,8,16,387]{3,2,1,0:T(8,128)S(1)} %get-tuple-element.49, f32[2,8,16,387]{3,2,1,0:T(8,128)S(1)} %get-tuple-element.48, f32[8,16,385]{2,1,0:T(8,128)S(1)} %get-tuple-element.43, pred[8,16,385]{2,1,0:T(8,128)(4,1)S(1)} %get-tuple-element.42), kind=kLoop, calls=%fused_computation.40 | loop fusion | flops 6012160 | bytes 3006080 | tf_op jit(solution)/shard_map/mul | solution.py:38
  34.0 0.0 collective-permute-done.2.far
  34.0 2.3 %collective-permute-done.3.close = f32[88,384]{1,0:T(8,128)S(1)} collective-permute-done((f32[88,384]{1,0:T(8,128)S(1)}, f32[88,384]{1,0:T(8,128)S(1)}, u32[]{:S(2)}, u32[]{:S(2)}) %collective-permute-start.3) | collective-permute-done | bytes 135200 | tf_op jit(solution)/shard_map/ppermute | solution.py:397
  36.5 0.1 broadcast_compare_fusion
  36.5 1.1 %krylov.1 = (f32[4,16,384]{2,1,0:T(8,128)S(1)}, f32[32,4,128]{2,1,0:T(4,128)}) custom-call(f32[8,128]{1,0:T(8,128)S(1)} %get-tuple-element.29.piece, f32[4,16,384]{2,1,0:T(8,128)S(1)} %get-tuple-element.26.fields, f32[4,16,128]{2,1,0:T(8,128)S(1)} %get-tuple-element.30.beyond, f32[88,384]{1,0:T(8,128)S(1)} %collective-permute-done.2.far, ...), custom_call_target="tpu_custom_call" | custom-call | tf_op jit(solution)/shard_map/krylov/pallas_call | solution.py:399
  37.6 4.5 %all-to-all-start = ((f32[32,4,128]{2,1,0:T(4,128)}), f32[32,4,128]{2,1,0:T(4,128)S(1)}, u32[]{:S(2)}, u32[]{:S(2)}) async-start(f32[32,4,128]{2,1,0:T(4,128)} %get-tuple-element.35), calls=%async_computation | async-start | bytes 131072 | tf_op jit(solution)/shard_map/all_to_all | solution.py:405
  42.2 0.1 maximum_maximum_fusion
  42.3 1.4 %add_multiply_fusion = f32[2,8,17,384]{3,2,1,0:T(8,128)S(1)} fusion(f32[2,8,19,384]{3,2,1,0:T(8,128)S(1)} %get-tuple-element.47, f32[2,8,19,384]{3,2,1,0:T(8,128)S(1)} %get-tuple-element.46, f32[8,17,384]{2,1,0:T(8,128)S(1)} %pad_maximum_fusion.1, pred[8,17,384]{2,1,0:T(8,128)(4,1)S(1)} %broadcast_compare_fusion), kind=kLoop, calls=%fused_computation.28 | loop fusion | flops 6371328 | bytes 3185664 | tf_op jit(solution)/shard_map/mul | solution.py:38
  43.7 0.3 fusion.15
  44.0 7.0 %all-to-all-done.got = f32[32,4,128]{2,1,0:T(4,128)S(1)} async-done(((f32[32,4,128]{2,1,0:T(4,128)}), f32[32,4,128]{2,1,0:T(4,128)S(1)}, u32[]{:S(2)}, u32[]{:S(2)}) %all-to-all-start) | async-done | bytes 65568 | tf_op jit(solution)/shard_map/all_to_all | solution.py:405
  51.0 0.7 relay.1
  51.7 6.7 %all-to-all-start.1 = ((f32[24,4,128]{2,1,0:T(4,128)}), f32[24,4,128]{2,1,0:T(4,128)S(1)}, u32[]{:S(2)}, u32[]{:S(2)}) async-start(f32[24,4,128]{2,1,0:T(4,128)} %relay.1), calls=%async_computation.1 | async-start | bytes 98304 | tf_op jit(solution)/shard_map/all_to_all | solution.py:409
  58.3 0.8 %slice_bitcast_fusion = (f32[8,16,384]{2,1,0:T(8,128)}, f32[8,16,384]{2,1,0:T(8,128)}) fusion(f32[2,8,16,384]{3,2,1,0:T(8,128)S(1)} %fusion.15), kind=kLoop, calls=%fused_computation.55 | loop fusion | bytes 786432 | tf_op jit(solution)/shard_map/squeeze | solution.py:464
  59.1 9.3 %all-to-all-done.1.got = f32[24,4,128]{2,1,0:T(4,128)S(1)} async-done(((f32[24,4,128]{2,1,0:T(4,128)}), f32[24,4,128]{2,1,0:T(4,128)S(1)}, u32[]{:S(2)}, u32[]{:S(2)}) %all-to-all-start.1) | async-done | bytes 49184 | tf_op jit(solution)/shard_map/all_to_all | solution.py:409
  68.4 0.9 %finish.1 = (f32[16,384]{1,0:T(8,128)}, f32[16,384]{1,0:T(8,128)}, f32[8,16,384]{2,1,0:T(8,128)}, f32[8,16,384]{2,1,0:T(8,128)}) custom-call(f32[4,16,384]{2,1,0:T(8,128)S(1)} %get-tuple-element.33.basis_ref, s32[2,8,128]{2,1,0:T(8,128)S(1)} %get-tuple-element.34.source, ...), custom_call_target="tpu_custom_call", output_to_operand_aliasing={{2}: (6, {}), {3}: (7, {})} | custom-call | tf_op jit(solution)/shard_map/finish/pallas_call | solution.py:442
  (10 shorter events, 0.1 us)
Async XLA Ops:
  0.6 15.1 %copy-start.5 = (s32[16,384]{1,0:T(8,128)S(1)}, s32[16,384]{1,0:T(8,128)}, u32[]{:S(2)}) copy-start(s32[16,384]{1,0:T(8,128)} %flag.1) | copy-start | bytes 73732
  0.6 15.1 %copy-start = (f32[8,16,384]{2,1,0:T(8,128)S(1)}, f32[8,16,384]{2,1,0:T(8,128)}, u32[]{:S(2)}) copy-start(f32[8,16,384]{2,1,0:T(8,128)} %t.1) | copy-start | bytes 589828
  0.7 15.1 %copy-start.1 = (f32[8,16,384]{2,1,0:T(8,128)S(1)}, f32[8,16,384]{2,1,0:T(8,128)}, u32[]{:S(2)}) copy-start(f32[8,16,384]{2,1,0:T(8,128)} %s.1) | copy-start | bytes 589828
  0.7 15.1 %copy-start.2 = (f32[8,16,384]{2,1,0:T(8,128)S(1)}, f32[8,16,384]{2,1,0:T(8,128)}, u32[]{:S(2)}) copy-start(f32[8,16,384]{2,1,0:T(8,128)} %u.1) | copy-start | bytes 589828
  0.7 15.1 %copy-start.3 = (f32[8,16,384]{2,1,0:T(8,128)S(1)}, f32[8,16,384]{2,1,0:T(8,128)}, u32[]{:S(2)}) copy-start(f32[8,16,384]{2,1,0:T(8,128)} %v.1) | copy-start | bytes 589828
  2.5 13.3 %copy-start.4 = (s32[16,384]{1,0:T(8,128)S(1)}, s32[16,384]{1,0:T(8,128)}, u32[]{:S(2)}) copy-start(s32[16,384]{1,0:T(8,128)} %depth.1) | copy-start | bytes 73732
  2.5 13.5 %collective-permute-start = (f32[16,128]{1,0:T(8,128)S(1)}, f32[16,128]{1,0:T(8,128)S(1)}, u32[]{:S(2)}, u32[]{:S(2)}) collective-permute-start(f32[16,128]{1,0:T(8,128)S(1)} %get-tuple-element.23), channel_id=1, source_target_pairs={{1,2},{2,1},{5,6},{6,5},{9,10},{10,9},{13,14},{14,13},{17,18},{18,... | collective-permute-start | bytes 24584 | tf_op jit(solution)/shard_map/ppermute | solution.py:382
  7.2 9.4 %collective-permute-start.1 = (f32[16,128]{1,0:T(8,128)S(1)}, f32[16,128]{1,0:T(8,128)S(1)}, u32[]{:S(2)}, u32[]{:S(2)}) collective-permute-start(f32[16,128]{1,0:T(8,128)S(1)} %get-tuple-element.24), channel_id=1, source_target_pairs={{0,1},{1,0},{2,3},{3,2},{4,5},{5,4},{6,7},{7,6},{8,9},{9,8},{10,11... | collective-permute-start | bytes 24584 | tf_op jit(solution)/shard_map/ppermute | solution.py:383
  16.7 17.3 %collective-permute-start.2 = (f32[88,384]{1,0:T(8,128)S(1)}, f32[88,384]{1,0:T(8,128)S(1)}, u32[]{:S(2)}, u32[]{:S(2)}) collective-permute-start(f32[88,384]{1,0:T(8,128)S(1)} %get-tuple-element.31), channel_id=1, source_target_pairs={{4,8},{8,4},{12,16},{16,12},{20,24},{24,20},{28,32},{32,28},{36,40... | collective-permute-start | bytes 405512 | tf_op jit(solution)/shard_map/ppermute | solution.py:398
  29.8 6.6 %collective-permute-start.3 = (f32[88,384]{1,0:T(8,128)S(1)}, f32[88,384]{1,0:T(8,128)S(1)}, u32[]{:S(2)}, u32[]{:S(2)}) collective-permute-start(f32[88,384]{1,0:T(8,128)S(1)} %get-tuple-element.32), channel_id=1, source_target_pairs={{0,4},{4,0},{8,12},{12,8},{16,20},{20,16},{24,28},{28,24},{32,36},... | collective-permute-start | bytes 405512 | tf_op jit(solution)/shard_map/ppermute | solution.py:397
  37.6 13.4 %all-to-all-start = ((f32[32,4,128]{2,1,0:T(4,128)}), f32[32,4,128]{2,1,0:T(4,128)S(1)}, u32[]{:S(2)}, u32[]{:S(2)}) async-start(f32[32,4,128]{2,1,0:T(4,128)} %get-tuple-element.35), calls=%async_computation | async-start | bytes 131072 | tf_op jit(solution)/shard_map/all_to_all | solution.py:405
  51.7 16.8 %all-to-all-start.1 = ((f32[24,4,128]{2,1,0:T(4,128)}), f32[24,4,128]{2,1,0:T(4,128)S(1)}, u32[]{:S(2)}, u32[]{:S(2)}) async-start(f32[24,4,128]{2,1,0:T(4,128)} %relay.1), calls=%async_computation.1 | async-start | bytes 98304 | tf_op jit(solution)/shard_map/all_to_all | solution.py:409

commit v12 on v10

--- a/solution.py
+++ b/solution.py
@@ -103,7 +103,7 @@
 
 def pack_kernel(
     t, s, u, v, elev, flag, depth, fc,
-    far, close, fields, edges, source, fold_ref, chip_swap, core_swap, tile,
+    far, close, fields, edges, source, tile,
 ):
     nl, ni, nj = t.shape
     ocean = flag[...] == 1
@@ -129,32 +129,9 @@
     coupler = 2.0 * jnp.sqrt((wet * flag[...]).astype(jnp.float32) / nl)
     for k, f in enumerate((part, em, nm, coupler)):
         fields[k] = f
-        x = tile[ni * k : ni * (k + 1)]
-        x = jnp.where((lane >= 16) & (lane < 20), pltpu.roll(f[:, :128], 16, 1), x)
-        x = jnp.where((lane >= 100) & (lane < 104), pltpu.roll(f[:, tail:], 104, 1), x)
-        tile[ni * k : ni * (k + 1)] = x
     turned = tile[...].T
     edges[0:16] = turned[0:16]
     edges[16:40] = turned[104:128]
-    lat = lat_index()
-    none = jnp.zeros((2, 128), jnp.float32)
-    t_end, s_end, v_end = turned[125:128], turned[117:120], turned[111:112]
-    fold = [jnp.concatenate([turned[k : k + 1] for k in (n, n - 1, n - 2)]) for n in (127, 119)]
-    fold = mirror16(jnp.concatenate(fold + [none], axis=0))
-    north = jnp.concatenate([t_end, s_end, v_end, none[:1]], axis=0)
-    south = jnp.concatenate([turned[0:3], turned[8:11], none], axis=0)
-    fold_ref[...] = fold
-    ahead = lax.rem(lat, 2) == 0
-    core_swap[0:8] = jnp.where(ahead, north, south)
-    core_swap[8:12] = jnp.where(ahead, turned[100:104], turned[16:20])
-    core_swap[12:15] = fold[0:3]
-    core_swap[15:16] = none[:1]
-    ahead = lat == 1
-    chip_swap[0:8] = jnp.where(ahead, north, south)
-    chip_swap[8:12] = jnp.where(ahead, turned[100:104], turned[16:20])
-    chip_swap[12:14] = none
-    chip_swap[14:16] = none
-
     even = lon_even()
     zero = jnp.zeros((2, nj), jnp.float32)
     for l in range(nl):
@@ -166,6 +143,12 @@
         west_edge = jnp.concatenate([tt[:3], ss[:3], zero], axis=0)
         far[8 * l : 8 * l + 8] = jnp.where(even, west_edge, east_edge)
         close[8 * l : 8 * l + 8] = jnp.where(even, east_edge, west_edge)
+    east_edge = jnp.concatenate(
+        [part[ni - 3 :], em[ni - 4 :], nm[ni - 3 :], coupler[ni - 3 :], zero, zero[:1]], axis=0
+    )
+    west_edge = jnp.concatenate([part[:3], em[:3], nm[:3], coupler[:3], zero, zero], axis=0)
+    far[64:80] = jnp.where(even, west_edge, east_edge)
+    close[64:80] = jnp.where(even, east_edge, west_edge)
     block = lax.shift_right_logical(jnp.broadcast_to(fc[0:1, 0:1], (8, 128)), 4)
     nz = lax.axis_size("z")
     columns = lax.axis_size("y") * lax.axis_size("xh")
@@ -188,57 +171,51 @@
     source[1] = block - nz * column_of(block)
 
 
-def widen_kernel(chip_got, core_got, fields, far_q, close_q, far, close, beyond, rims, tile, up, down):
+def widen_kernel(far, close, fields, edges, wide, fold_ref, chip_swap, core_swap):
     _, ni, nj = fields.shape
     lat = lat_index()
     even = lon_even()
+    blank = jnp.zeros((8, nj), jnp.float32)
+    spans = ((64, 67, 64, 67), (67, 71, 67, 70), (71, 74, 70, 73), (74, 77, 73, 76))
+    for k, (w0, w1, e0, e1) in enumerate(spans):
+        wide[k, 0:8] = blank
+        wide[k, 24:32] = blank
+        wide[k, 8 - (w1 - w0) : 8] = jnp.where(even, far[w0:w1], close[w0:w1])
+        wide[k, 8 : 8 + ni] = fields[k]
+        wide[k, 24 : 24 + (e1 - e0)] = jnp.where(even, close[e0:e1], far[e0:e1])
+    lane = lax.broadcasted_iota(jnp.int32, (4, 32, 128), 2)
+    both = jnp.where(lane < 64, wide[:, :, 0:128], wide[:, :, nj - 128 : nj])
+    turned = both.reshape(128, 128).T
+    none = jnp.zeros((4, 128), jnp.float32)
+    fold = jnp.concatenate(
+        [edges[k : k + 1] for k in (39, 38, 37, 31, 30, 29)] + [none[:2]], axis=0
+    )
+    fold = mirror16(fold)
+    north = jnp.concatenate(
+        [edges[37:40], edges[29:32], edges[23:24], none[:1]], axis=0
+    )
+    south = jnp.concatenate([edges[0:3], edges[8:11], none[:2]], axis=0)
+    fold_ref[...] = fold
+    for out, ahead in ((chip_swap, lat == 1), (core_swap, lax.rem(lat, 2) == 0)):
+        out[0:8] = jnp.where(ahead, north, south)
+        out[8:12] = jnp.where(ahead, turned[124:128], turned[0:4])
+        out[12:15] = fold[0:3]
+        out[15:16] = none[:1]
+
+
+def krylov_kernel(wide, chip_got, core_got, fold, basis_ref, message, rims, tile):
+    ni, nj = basis_ref.shape[1:]
+    lat = lat_index()
+    tile[...] = jnp.zeros((128, 128), jnp.float32)
     odd = lax.rem(lat, 2) == 1
     north = jnp.where(lat < 3, jnp.where(odd, chip_got[...], core_got[...]), 0.0)
     south = jnp.where(lat > 0, jnp.where(odd, core_got[...], chip_got[...]), 0.0)
     rims[0] = north[0:8]
     rims[1] = south[0:8]
-    tile[...] = jnp.zeros((128, 128), jnp.float32)
     tile[0:4] = north[8:12]
     tile[124:128] = south[8:12]
-    beyond[...] = tile[...].T[0 : 4 * ni].reshape(4, ni, 128)
-    far[0:64] = far_q[...]
-    close[0:64] = close_q[...]
-    at = 0
-    for k, n in enumerate((3, 4, 3, 3)):
-        up[at : at + n, 0:nj] = fields[k, ni - n : ni]
-        up[at : at + n, nj:] = beyond[k, ni - n : ni]
-        down[at : at + n, 0:nj] = fields[k, 0:n]
-        down[at : at + n, nj:] = beyond[k, 0:n]
-        at += n
-    up[13:16] = jnp.zeros((3, nj + 128), jnp.float32)
-    down[13:16] = jnp.zeros((3, nj + 128), jnp.float32)
-    for out, first, second in ((far, down, up), (close, up, down)):
-        rows = jnp.where(even, first[...], second[...])
-        out[64:80] = rows[:, 0:nj]
-        out[80:88, 0:128] = rows[0:8, nj:]
-        out[80:88, 128:256] = rows[8:16, nj:]
-        out[80:88, 256:384] = jnp.zeros((8, 128), jnp.float32)
-
-
-def krylov_kernel(core_got, fold, fields, beyond, far, close, basis_ref, message, wide, west, east):
-    _, ni, nj = fields.shape
-    even = lon_even()
-    for out, first, second in ((west, far, close), (east, close, far)):
-        out[:, 0:nj] = jnp.where(even, first[64:80], second[64:80])
-        tail = jnp.where(even, first[80:88], second[80:88])
-        out[0:8, nj:] = tail[:, 0:128]
-        out[8:16, nj:] = tail[:, 128:256]
-    blank = jnp.zeros((8, nj + 128), jnp.float32)
-    at = 0
-    for k, n in enumerate((3, 4, 3, 3)):
-        wide[k, 0:8] = blank
-        wide[k, 24:32] = blank
-        wide[k, 8 - n : 8] = west[at : at + n]
-        wide[k, 24 : 24 + n] = east[at : at + n]
-        wide[k, 8:24, 0:nj] = fields[k]
-        wide[k, 8:24, nj:] = beyond[k]
-        at += n
-    part, em, nm, cpl = (wide[k] for k in range(4))
+    beyond = tile[...].T.reshape(4, 32, 128)
+    part, em, nm, cpl = (jnp.concatenate([wide[k], beyond[k]], axis=1) for k in range(4))
     rows, lanes = part.shape
     b0 = part + pltpu.roll(em, 1, 0) + pltpu.roll(nm, 1, 1)
 
@@ -261,7 +238,7 @@
         basis_ref[k] = basis[k]
     row = lax.broadcasted_iota(jnp.int32, (4, 128), 0)
     col = lax.broadcasted_iota(jnp.int32, (4, 128), 1)
-    piece = jnp.where(lat_index() == 3, fold[3:6], core_got[12:15])
+    piece = jnp.where(lat == 3, fold[3:6], core_got[12:15])
     total = jnp.concatenate([piece, jnp.zeros((1, 128), jnp.float32)], axis=0)
     for n, (i, j) in enumerate(PAIRS):
         prod = basis[i] * basis[j]
@@ -361,29 +338,18 @@
         last = lat == n_lat - 1
         hbm, local = pl.BlockSpec(memory_space=pl.ANY), pl.BlockSpec(memory_space=pltpu.VMEM)
 
-        far, close, fields, edges, source, fold, chip_swap, core_swap = pl.pallas_call(
+        far, close, fields, edges, source = pl.pallas_call(
             pack_kernel,
             out_shape=(
-                vmem(64, nj),
-                vmem(64, nj),
+                vmem(80, nj),
+                vmem(80, nj),
                 vmem(4, ni, nj),
                 vmem(40, 128),
                 pltpu.VMEM((2, 8, 128), jnp.int32),
-                vmem(8, 128),
-                vmem(16, 128),
-                vmem(16, 128),
             ),
             scratch_shapes=[vmem(128, 128)],
             name="pack",
         )(t, s, u, v, elev, flag, depth, fc.reshape(1, ni))
-        chip_got = lax.ppermute(chip_swap, LAT, [(1, 2), (2, 1)])
-        core_got = lax.ppermute(core_swap, LAT, [(0, 1), (1, 0), (2, 3), (3, 2)])
-        far, close, beyond, rims = pl.pallas_call(
-            widen_kernel,
-            out_shape=(vmem(88, nj), vmem(88, nj), vmem(4, ni, 128), vmem(2, 8, 128)),
-            scratch_shapes=[vmem(128, 128), vmem(16, nj + 128), vmem(16, nj + 128)],
-            name="widen",
-        )(near(chip_got), near(core_got), near(fields), near(far), near(close))
 
         def swaps(first):
             pairs = []
@@ -391,14 +357,21 @@
                 pairs += [(i, (i + 1) % n_lon), ((i + 1) % n_lon, i)]
             return pairs
 
+        far = lax.ppermute(far, LON, swaps(1))
         close = lax.ppermute(close, LON, swaps(0))
-        far = lax.ppermute(far, LON, swaps(1))
-        basis, message = pl.pallas_call(
+        wide, fold, chip_swap, core_swap = pl.pallas_call(
+            widen_kernel,
+            out_shape=(vmem(4, 32, nj), vmem(8, 128), vmem(16, 128), vmem(16, 128)),
+            name="widen",
+        )(near(far), near(close), near(fields), near(edges))
+        chip_got = lax.ppermute(chip_swap, LAT, [(1, 2), (2, 1)])
+        core_got = lax.ppermute(core_swap, LAT, [(0, 1), (1, 0), (2, 3), (3, 2)])
+        basis, message, rims = pl.pallas_call(
             krylov_kernel,
-            out_shape=(vmem(4, ni, nj), vmem(ny * nxh * nxl, 4, 128)),
-            scratch_shapes=[vmem(4, 32, nj + 128), vmem(16, nj + 128), vmem(16, nj + 128)],
+            out_shape=(vmem(4, ni, nj), vmem(ny * nxh * nxl, 4, 128), vmem(2, 8, 128)),
+            scratch_shapes=[vmem(128, 128)],
             name="krylov",
-        )(near(core_got), near(fold), near(fields), near(beyond), near(far), near(close))
+        )(near(wide), near(chip_got), near(core_got), near(fold))
         got = lax.all_to_all(message, ("y", "xh", "xl"), 0, 0)
         message = pl.pallas_call(
             relay_kernel, out_shape=vmem(nz * ncore, 4, 128), name="relay"

time: 70 us -> 70.6 us (level)
  starting transfers between devices: 38.2 us -> 39.9 us
  waiting for transfers between devices: 20.8 us -> 19.7 us
    ppermute x1, starting transfers between devices: 12.6 us -> 1.92 us  [on_device(): core_got = lax.ppermute(core_swap, LAT, [(0, 1), (1, 0), (2, 3), (3, 2)])]
    ppermute x1, starting transfers between devices: 10.7 us -> 20.6 us  [on_device(): far = lax.ppermute(far, LON, swaps(1))]
    ppermute x1, waiting for transfers between devices: 2.81 us -> 0.01 us  [on_device(): chip_got = lax.ppermute(chip_swap, LAT, [(1, 2), (2, 1)])]
    ppermute x1, starting transfers between devices: 1.92 us -> 4.23 us  [on_device(): chip_got = lax.ppermute(chip_swap, LAT, [(1, 2), (2, 1)])]
    all_to_all x1, starting transfers between devices: 4.3 us -> 5.77 us  [on_device(): got = lax.all_to_all(message, ('y', 'xh', 'xl'), 0, 0)]
    all_to_all x1, starting transfers between devices: 6.87 us -> 5.43 us  [on_device(): got = lax.all_to_all(message, ('z', 'core'), 0, 0)]
    ppermute x1, waiting for transfers between devices: 1.49 us -> 2.59 us  [on_device(): close = lax.ppermute(close, LON, swaps(0))]
    ppermute x1, waiting for transfers between devices: 0.01 us -> 0.87 us  [on_device(): far = lax.ppermute(far, LON, swaps(1))]
  transfers between devices with their start and end apart: 6 -> 6, of which waited for: 4 -> 4; matrix products, arithmetic and copies ran while one was open for 7% -> 6% of each run, Pallas kernels for 0% -> 0%
where the time goes in v12:
time: 70.6 us; the launch traced here: 70.2 us
  starting transfers between devices  39.9 us (57%)
  waiting for transfers between devices  19.7 us (28%)
  Pallas kernels  4.48 us (6%)
  other arithmetic  3.56 us (5%)
  local copies, waits for them, and re-layouts  1.58 us (2%)
  between operations  0.93 us (1%)
    ppermute x1, starting transfers between devices, on_device(): far = lax.ppermute(far, LON, swaps(1))  20.6 us
    all_to_all x1, waiting for transfers between devices, on_device(): got = lax.all_to_all(message, ('z', 'core'), 0, 0)  9.37 us
    all_to_all x1, waiting for transfers between devices, on_device(): got = lax.all_to_all(message, ('y', 'xh', 'xl'), 0, 0)  6.91 us
    all_to_all x1, starting transfers between devices, on_device(): got = lax.all_to_all(message, ('y', 'xh', 'xl'), 0, 0)  5.77 us
    all_to_all x1, starting transfers between devices, on_device(): got = lax.all_to_all(message, ('z', 'core'), 0, 0)  5.43 us
    ppermute x1, starting transfers between devices, on_device(): chip_got = lax.ppermute(chip_swap, LAT, [(1, 2), (2, 1)])  4.23 us
    mul x2, other arithmetic, face_flux(): return speed * weno_upwind(a, b, c, d, e)  2.61 us
    ppermute x1, waiting for transfers between devices, on_device(): close = lax.ppermute(close, LON, swaps(0))  2.59 us
  transfers between devices with their start and end apart: 6, of which 4 were waited for; matrix products, arithmetic and copies ran while one was open for 6% of the time, Pallas kernels for 0%

profile of v12, /device:TPU:1, one launch (start us, length us, event | category | flops | bytes accessed | tf_op | source)
XLA Modules:
  0.0 70.2 jit_solution(15814516888969758617)
XLA Ops:
  0.6 0.0 copy-start.5
  0.6 0.0 copy-start
  0.7 0.0 copy-start.1
  0.7 0.0 copy-start.2
  0.7 0.0 copy-start.3
  0.7 1.5 %pack.1 = (f32[80,384]{1,0:T(8,128)S(1)}, f32[80,384]{1,0:T(8,128)S(1)}, f32[4,16,384]{2,1,0:T(8,128)S(1)}, f32[40,128]{1,0:T(8,128)S(1)}, s32[2,8,128]{2,1,0:T(8,128)S(1)}) custom-call(f32[8,16,384]{2,1,0:T(8,128)} %t.1, f32[8,16,384]{2,1,0:T(8,128)} %s.1, f32[8,16,384]{2,1,0:T(8,128)} %u.1, f32[8,16,384]{2,1,0:T(8,128)} %v.1, f32[16,384]{1,0:T(8,128)} %elev.1, ...), custom_call_target="tpu_custom_call" | custom-call | tf_op jit(solution)/shard_map/pack/pallas_call | solution.py:341
  2.2 0.0 copy-start.4
  2.2 20.6 %collective-permute-start = (f32[80,384]{1,0:T(8,128)S(1)}, f32[80,384]{1,0:T(8,128)S(1)}, u32[]{:S(2)}, u32[]{:S(2)}) collective-permute-start(f32[80,384]{1,0:T(8,128)S(1)} %get-tuple-element.20), channel_id=1, source_target_pairs={{4,8},{8,4},{12,16},{16,12},{20,24},{24,20},{28,32},{32,28},{36,40... | collective-permute-start | bytes 368648 | tf_op jit(solution)/shard_map/ppermute | solution.py:360
  22.9 1.9 %collective-permute-start.1 = (f32[80,384]{1,0:T(8,128)S(1)}, f32[80,384]{1,0:T(8,128)S(1)}, u32[]{:S(2)}, u32[]{:S(2)}) collective-permute-start(f32[80,384]{1,0:T(8,128)S(1)} %get-tuple-element.21), channel_id=1, source_target_pairs={{0,4},{4,0},{8,12},{12,8},{16,20},{20,16},{24,28},{28,24},{32,36},... | collective-permute-start | bytes 368648 | tf_op jit(solution)/shard_map/ppermute | solution.py:361
  24.8 0.0 copy-done.5
  24.8 0.0 copy-done
  24.8 0.0 copy-done.1
  24.8 0.0 copy-done.2
  24.9 0.0 copy-done.3
  24.9 0.0 copy-done.4
  24.9 0.1 fusion.20
  25.0 0.9 %collective-permute-done.far = f32[80,384]{1,0:T(8,128)S(1)} collective-permute-done((f32[80,384]{1,0:T(8,128)S(1)}, f32[80,384]{1,0:T(8,128)S(1)}, u32[]{:S(2)}, u32[]{:S(2)}) %collective-permute-start) | collective-permute-done | bytes 122912 | tf_op jit(solution)/shard_map/ppermute | solution.py:360
  25.9 2.6 %collective-permute-done.1.close = f32[80,384]{1,0:T(8,128)S(1)} collective-permute-done((f32[80,384]{1,0:T(8,128)S(1)}, f32[80,384]{1,0:T(8,128)S(1)}, u32[]{:S(2)}, u32[]{:S(2)}) %collective-permute-start.1) | collective-permute-done | bytes 122912 | tf_op jit(solution)/shard_map/ppermute | solution.py:361
  28.6 0.1 broadcast_compare_fusion
  28.7 0.3 widen.1
  29.0 4.2 %collective-permute-start.2 = (f32[16,128]{1,0:T(8,128)S(1)}, f32[16,128]{1,0:T(8,128)S(1)}, u32[]{:S(2)}, u32[]{:S(2)}) collective-permute-start(f32[16,128]{1,0:T(8,128)S(1)} %get-tuple-element.25), channel_id=1, source_target_pairs={{1,2},{2,1},{5,6},{6,5},{9,10},{10,9},{13,14},{14,13},{17,18},{18,... | collective-permute-start | bytes 24584 | tf_op jit(solution)/shard_map/ppermute | solution.py:367
  33.2 1.9 %collective-permute-start.3 = (f32[16,128]{1,0:T(8,128)S(1)}, f32[16,128]{1,0:T(8,128)S(1)}, u32[]{:S(2)}, u32[]{:S(2)}) collective-permute-start(f32[16,128]{1,0:T(8,128)S(1)} %get-tuple-element.26), channel_id=1, source_target_pairs={{0,1},{1,0},{2,3},{3,2},{4,5},{5,4},{6,7},{7,6},{8,9},{9,8},{10,11... | collective-permute-start | bytes 24584 | tf_op jit(solution)/shard_map/ppermute | solution.py:368
  35.1 0.1 maximum_maximum_fusion
  35.2 1.4 %add_multiply_fusion = f32[2,8,17,384]{3,2,1,0:T(8,128)S(1)} fusion(f32[2,8,19,384]{3,2,1,0:T(8,128)S(1)} %get-tuple-element.41, f32[2,8,19,384]{3,2,1,0:T(8,128)S(1)} %get-tuple-element.40, f32[8,17,384]{2,1,0:T(8,128)S(1)} %pad_maximum_fusion.1, pred[8,17,384]{2,1,0:T(8,128)(4,1)S(1)} %broadcast_compare_fusion), kind=kLoop, calls=%fused_computation.28 | loop fusion | flops 6371328 | bytes 3185664 | tf_op jit(solution)/shard_map/mul | solution.py:38
  36.6 0.0 collective-permute-done.2.chip_got
  36.6 0.0 collective-permute-done.3.core_got
  36.6 1.2 %krylov.1 = (f32[4,16,384]{2,1,0:T(8,128)S(1)}, f32[32,4,128]{2,1,0:T(4,128)}, f32[2,8,128]{2,1,0:T(8,128)S(1)}) custom-call(f32[4,32,384]{2,1,0:T(8,128)S(1)} %get-tuple-element.24.wide, f32[16,128]{1,0:T(8,128)S(1)} %collective-permute-done.2.chip_got, f32[16,128]{1,0:T(8,128)S(1)} %collective-permute-done.3.core_got, f32[8,128]{1,0:T(8,128)S(1)} %get-tuple-element.27.fold), custom_call_target="tpu_custom_call" | custom-call | tf_op jit(solution)/shard_map/krylov/pallas_call | solution.py:369
  37.8 0.1 reshape.94
  37.9 0.2 copy.20
  38.0 0.1 reshape.93
  38.1 0.2 copy.19
  38.3 0.2 concatenate.48
  38.5 5.8 %all-to-all-start = ((f32[32,4,128]{2,1,0:T(4,128)}), f32[32,4,128]{2,1,0:T(4,128)S(1)}, u32[]{:S(2)}, u32[]{:S(2)}) async-start(f32[32,4,128]{2,1,0:T(4,128)} %get-tuple-element.30), calls=%async_computation | async-start | bytes 131072 | tf_op jit(solution)/shard_map/all_to_all | solution.py:375
  44.3 0.2 maximum_maximum_fusion.2
  44.5 0.1 broadcast_compare_fusion.1
  44.6 1.3 %add_multiply_fusion.1 = f32[2,8,16,385]{3,2,1,0:T(8,128)S(1)} fusion(f32[2,8,16,387]{3,2,1,0:T(8,128)S(1)} %get-tuple-element.43, f32[2,8,16,387]{3,2,1,0:T(8,128)S(1)} %get-tuple-element.42, f32[8,16,385]{2,1,0:T(8,128)S(1)} %get-tuple-element.37, pred[8,16,385]{2,1,0:T(8,128)(4,1)S(1)} %get-tuple-element.36), kind=kLoop, calls=%fused_computation.40 | loop fusion | flops 6012160 | bytes 3006080 | tf_op jit(solution)/shard_map/mul | solution.py:38
  45.9 0.3 fusion.15
  46.2 6.9 %all-to-all-done.got = f32[32,4,128]{2,1,0:T(4,128)S(1)} async-done(((f32[32,4,128]{2,1,0:T(4,128)}), f32[32,4,128]{2,1,0:T(4,128)S(1)}, u32[]{:S(2)}, u32[]{:S(2)}) %all-to-all-start) | async-done | bytes 65568 | tf_op jit(solution)/shard_map/all_to_all | solution.py:375
  53.1 0.7 relay.1
  53.8 5.4 %all-to-all-start.1 = ((f32[24,4,128]{2,1,0:T(4,128)}), f32[24,4,128]{2,1,0:T(4,128)S(1)}, u32[]{:S(2)}, u32[]{:S(2)}) async-start(f32[24,4,128]{2,1,0:T(4,128)} %relay.1), calls=%async_computation.1 | async-start | bytes 98304 | tf_op jit(solution)/shard_map/all_to_all | solution.py:379
  59.2 0.8 %slice_bitcast_fusion = (f32[8,16,384]{2,1,0:T(8,128)}, f32[8,16,384]{2,1,0:T(8,128)}) fusion(f32[2,8,16,384]{3,2,1,0:T(8,128)S(1)} %fusion.15), kind=kLoop, calls=%fused_computation.55 | loop fusion | bytes 786432 | tf_op jit(solution)/shard_map/squeeze | solution.py:434
  60.0 9.4 %all-to-all-done.1.got = f32[24,4,128]{2,1,0:T(4,128)S(1)} async-done(((f32[24,4,128]{2,1,0:T(4,128)}), f32[24,4,128]{2,1,0:T(4,128)S(1)}, u32[]{:S(2)}, u32[]{:S(2)}) %all-to-all-start.1) | async-done | bytes 49184 | tf_op jit(solution)/shard_map/all_to_all | solution.py:379
  69.3 0.9 %finish.1 = (f32[16,384]{1,0:T(8,128)}, f32[16,384]{1,0:T(8,128)}, f32[8,16,384]{2,1,0:T(8,128)}, f32[8,16,384]{2,1,0:T(8,128)}) custom-call(f32[4,16,384]{2,1,0:T(8,128)S(1)} %get-tuple-element.28.basis_ref, s32[2,8,128]{2,1,0:T(8,128)S(1)} %get-tuple-element.29.source, ...), custom_call_target="tpu_custom_call", output_to_operand_aliasing={{2}: (6, {}), {3}: (7, {})} | custom-call | tf_op jit(solution)/shard_map/finish/pallas_call | solution.py:412
  (10 shorter events, 0.2 us)
Async XLA Ops:
  0.6 24.2 %copy-start.5 = (s32[16,384]{1,0:T(8,128)S(1)}, s32[16,384]{1,0:T(8,128)}, u32[]{:S(2)}) copy-start(s32[16,384]{1,0:T(8,128)} %flag.1) | copy-start | bytes 73732
  0.6 24.2 %copy-start = (f32[8,16,384]{2,1,0:T(8,128)S(1)}, f32[8,16,384]{2,1,0:T(8,128)}, u32[]{:S(2)}) copy-start(f32[8,16,384]{2,1,0:T(8,128)} %t.1) | copy-start | bytes 589828
  0.7 24.2 %copy-start.1 = (f32[8,16,384]{2,1,0:T(8,128)S(1)}, f32[8,16,384]{2,1,0:T(8,128)}, u32[]{:S(2)}) copy-start(f32[8,16,384]{2,1,0:T(8,128)} %s.1) | copy-start | bytes 589828
  0.7 24.2 %copy-start.2 = (f32[8,16,384]{2,1,0:T(8,128)S(1)}, f32[8,16,384]{2,1,0:T(8,128)}, u32[]{:S(2)}) copy-start(f32[8,16,384]{2,1,0:T(8,128)} %u.1) | copy-start | bytes 589828
  0.7 24.2 %copy-start.3 = (f32[8,16,384]{2,1,0:T(8,128)S(1)}, f32[8,16,384]{2,1,0:T(8,128)}, u32[]{:S(2)}) copy-start(f32[8,16,384]{2,1,0:T(8,128)} %v.1) | copy-start | bytes 589828
  2.2 22.6 %copy-start.4 = (s32[16,384]{1,0:T(8,128)S(1)}, s32[16,384]{1,0:T(8,128)}, u32[]{:S(2)}) copy-start(s32[16,384]{1,0:T(8,128)} %depth.1) | copy-start | bytes 73732
  2.2 23.7 %collective-permute-start = (f32[80,384]{1,0:T(8,128)S(1)}, f32[80,384]{1,0:T(8,128)S(1)}, u32[]{:S(2)}, u32[]{:S(2)}) collective-permute-start(f32[80,384]{1,0:T(8,128)S(1)} %get-tuple-element.20), channel_id=1, source_target_pairs={{4,8},{8,4},{12,16},{16,12},{20,24},{24,20},{28,32},{32,28},{36,40... | collective-permute-start | bytes 368648 | tf_op jit(solution)/shard_map/ppermute | solution.py:360
  22.9 5.6 %collective-permute-start.1 = (f32[80,384]{1,0:T(8,128)S(1)}, f32[80,384]{1,0:T(8,128)S(1)}, u32[]{:S(2)}, u32[]{:S(2)}) collective-permute-start(f32[80,384]{1,0:T(8,128)S(1)} %get-tuple-element.21), channel_id=1, source_target_pairs={{0,4},{4,0},{8,12},{12,8},{16,20},{20,16},{24,28},{28,24},{32,36},... | collective-permute-start | bytes 368648 | tf_op jit(solution)/shard_map/ppermute | solution.py:361
  29.0 7.6 %collective-permute-start.2 = (f32[16,128]{1,0:T(8,128)S(1)}, f32[16,128]{1,0:T(8,128)S(1)}, u32[]{:S(2)}, u32[]{:S(2)}) collective-permute-start(f32[16,128]{1,0:T(8,128)S(1)} %get-tuple-element.25), channel_id=1, source_target_pairs={{1,2},{2,1},{5,6},{6,5},{9,10},{10,9},{13,14},{14,13},{17,18},{18,... | collective-permute-start | bytes 24584 | tf_op jit(solution)/shard_map/ppermute | solution.py:367
  33.2 3.4 %collective-permute-start.3 = (f32[16,128]{1,0:T(8,128)S(1)}, f32[16,128]{1,0:T(8,128)S(1)}, u32[]{:S(2)}, u32[]{:S(2)}) collective-permute-start(f32[16,128]{1,0:T(8,128)S(1)} %get-tuple-element.26), channel_id=1, source_target_pairs={{0,1},{1,0},{2,3},{3,2},{4,5},{5,4},{6,7},{7,6},{8,9},{9,8},{10,11... | collective-permute-start | bytes 24584 | tf_op jit(solution)/shard_map/ppermute | solution.py:368
  38.5 14.6 %all-to-all-start = ((f32[32,4,128]{2,1,0:T(4,128)}), f32[32,4,128]{2,1,0:T(4,128)S(1)}, u32[]{:S(2)}, u32[]{:S(2)}) async-start(f32[32,4,128]{2,1,0:T(4,128)} %get-tuple-element.30), calls=%async_computation | async-start | bytes 131072 | tf_op jit(solution)/shard_map/all_to_all | solution.py:375
  53.8 15.6 %all-to-all-start.1 = ((f32[24,4,128]{2,1,0:T(4,128)}), f32[24,4,128]{2,1,0:T(4,128)S(1)}, u32[]{:S(2)}, u32[]{:S(2)}) async-start(f32[24,4,128]{2,1,0:T(4,128)} %relay.1), calls=%async_computation.1 | async-start | bytes 98304 | tf_op jit(solution)/shard_map/all_to_all | solution.py:379

commit v13 on v11

--- a/solution.py
+++ b/solution.py
@@ -189,7 +189,7 @@
 
 
 def widen_kernel(
-    chip_got, core_got, fold, fields, far_q, close_q, far, close, beyond, rims, piece, tile, up, down
+    chip_got, core_got, fold, fields, far_q, close_q, far, close, plane, rims, piece, tile
 ):
     _, ni, nj = fields.shape
     lat = lat_index()
@@ -204,47 +204,44 @@
     tile[...] = jnp.zeros((128, 128), jnp.float32)
     tile[0:4] = north[8:12]
     tile[124:128] = south[8:12]
-    beyond[...] = tile[...].T[0 : 4 * ni].reshape(4, ni, 128)
+    beyond = tile[...].T[0 : 4 * ni].reshape(4, ni, 128)
+    part, em, nm, cpl = (jnp.concatenate([fields[k], beyond[k]], axis=1) for k in range(4))
+    row = lax.broadcasted_iota(jnp.int32, part.shape, 0)
+    side = part + pltpu.roll(nm, 1, 1) + jnp.where(row == 0, 0.0, pltpu.roll(em, 1, 0))
+    for k, f in enumerate((side, cpl, em)):
+        plane[k] = f
+    up = jnp.concatenate([side[ni - 3 :], cpl[ni - 3 :], em[ni - 1 :], em[ni - 1 :]], axis=0)
+    down = jnp.concatenate([side[0:3], cpl[0:3], cpl[0:2]], axis=0)
     far[0:64] = far_q[...]
     close[0:64] = close_q[...]
-    at = 0
-    for k, n in enumerate((3, 4, 3, 3)):
-        up[at : at + n, 0:nj] = fields[k, ni - n : ni]
-        up[at : at + n, nj:] = beyond[k, ni - n : ni]
-        down[at : at + n, 0:nj] = fields[k, 0:n]
-        down[at : at + n, nj:] = beyond[k, 0:n]
-        at += n
-    up[13:16] = jnp.zeros((3, nj + 128), jnp.float32)
-    down[13:16] = jnp.zeros((3, nj + 128), jnp.float32)
     for out, first, second in ((far, down, up), (close, up, down)):
-        rows = jnp.where(even, first[...], second[...])
-        out[64:80] = rows[:, 0:nj]
-        out[80:88, 0:128] = rows[0:8, nj:]
-        out[80:88, 128:256] = rows[8:16, nj:]
-        out[80:88, 256:384] = jnp.zeros((8, 128), jnp.float32)
-
-
-def krylov_kernel(piece, fields, beyond, far, close, basis_ref, message, wide, west, east):
-    _, ni, nj = fields.shape
+        rows = jnp.where(even, first, second)
+        for l in range(8):
+            out[8 * l + 7 : 8 * l + 8] = rows[l : l + 1, 0:nj]
+        out[64:72, 0:128] = rows[:, nj:]
+        out[64:72, 128:384] = jnp.zeros((8, 256), jnp.float32)
+
+
+def krylov_kernel(piece, plane, far, close, basis_ref, message, wide, west, east):
+    ni, nj = basis_ref.shape[1:]
     even = lon_even()
     for out, first, second in ((west, far, close), (east, close, far)):
-        out[:, 0:nj] = jnp.where(even, first[64:80], second[64:80])
-        tail = jnp.where(even, first[80:88], second[80:88])
-        out[0:8, nj:] = tail[:, 0:128]
-        out[8:16, nj:] = tail[:, 128:256]
+        for l in range(8):
+            at = 8 * l + 7
+            out[l : l + 1, 0:nj] = jnp.where(even, first[at : at + 1], second[at : at + 1])
+        out[:, nj:] = jnp.where(even, first[64:72, 0:128], second[64:72, 0:128])
     blank = jnp.zeros((8, nj + 128), jnp.float32)
-    at = 0
-    for k, n in enumerate((3, 4, 3, 3)):
+    for k in range(2):
         wide[k, 0:8] = blank
         wide[k, 24:32] = blank
-        wide[k, 8 - n : 8] = west[at : at + n]
-        wide[k, 24 : 24 + n] = east[at : at + n]
-        wide[k, 8:24, 0:nj] = fields[k]
-        wide[k, 8:24, nj:] = beyond[k]
-        at += n
-    part, em, nm, cpl = (wide[k] for k in range(4))
-    rows, lanes = part.shape
-    b0 = part + pltpu.roll(em, 1, 0) + pltpu.roll(nm, 1, 1)
+        wide[k, 8:24] = plane[k]
+        wide[k, 5:8] = west[3 * k : 3 * k + 3]
+        wide[k, 24:27] = east[3 * k : 3 * k + 3]
+    wide[0, 8:9] = plane[0, 0:1] + west[6:7]
+    wide[0, 24:25] = east[0:1] + plane[2, ni - 1 : ni]
+    b0 = wide[0]
+    cpl = wide[1]
+    rows, lanes = b0.shape
 
     def scaled(e):
         f = cpl * e
@@ -381,10 +378,16 @@
         )(t, s, u, v, elev, flag, depth, fc.reshape(1, ni))
         chip_got = lax.ppermute(chip_swap, LAT, [(1, 2), (2, 1)])
         core_got = lax.ppermute(core_swap, LAT, [(0, 1), (1, 0), (2, 3), (3, 2)])
-        far, close, beyond, rims, piece = pl.pallas_call(
+        far, close, plane, rims, piece = pl.pallas_call(
             widen_kernel,
-            out_shape=(vmem(88, nj), vmem(88, nj), vmem(4, ni, 128), vmem(2, 8, 128), vmem(8, 128)),
-            scratch_shapes=[vmem(128, 128), vmem(16, nj + 128), vmem(16, nj + 128)],
+            out_shape=(
+                vmem(72, nj),
+                vmem(72, nj),
+                vmem(3, ni, nj + 128),
+                vmem(2, 8, 128),
+                vmem(8, 128),
+            ),
+            scratch_shapes=[vmem(128, 128)],
             name="widen",
         )(near(chip_got), near(core_got), near(fold), near(fields), near(far), near(close))
 
@@ -399,9 +402,9 @@
         basis, message = pl.pallas_call(
             krylov_kernel,
             out_shape=(vmem(4, ni, nj), vmem(ny * nxh * nxl, 4, 128)),
-            scratch_shapes=[vmem(4, 32, nj + 128), vmem(16, nj + 128), vmem(16, nj + 128)],
+            scratch_shapes=[vmem(2, 32, nj + 128), vmem(8, nj + 128), vmem(8, nj + 128)],
             name="krylov",
-        )(near(piece), near(fields), near(beyond), near(far), near(close))
+        )(near(piece), near(plane), near(far), near(close))
         got = lax.all_to_all(message, ("y", "xh", "xl"), 0, 0)
         message = pl.pallas_call(
             relay_kernel, out_shape=vmem(nz * ncore, 4, 128), name="relay"

time: 69.7 us -> 69.2 us (level)
  no operation moved by 1% of the time
where the time goes in v13:
time: 69.2 us; the launch traced here: 68.8 us
  starting transfers between devices  39.4 us (57%)
  waiting for transfers between devices  18.7 us (27%)
  Pallas kernels  4.55 us (7%)
  other arithmetic  3.56 us (5%)
  local copies, waits for them, and re-layouts  1.58 us (2%)
  between operations  0.93 us (1%)
    ppermute x1, starting transfers between devices, on_device(): far = lax.ppermute(far, LON, swaps(1))  13.1 us
    all_to_all x1, waiting for transfers between devices, on_device(): got = lax.all_to_all(message, ('z', 'core'), 0, 0)  9.32 us
    ppermute x1, starting transfers between devices, on_device(): core_got = lax.ppermute(core_swap, LAT, [(0, 1), (1, 0), (2, 3), (3, 2)])  8.58 us
    all_to_all x1, waiting for transfers between devices, on_device(): got = lax.all_to_all(message, ('y', 'xh', 'xl'), 0, 0)  7.04 us
    all_to_all x1, starting transfers between devices, on_device(): got = lax.all_to_all(message, ('z', 'core'), 0, 0)  6.68 us
    ppermute x1, starting transfers between devices, on_device(): chip_got = lax.ppermute(chip_swap, LAT, [(1, 2), (2, 1)])  4.64 us
    all_to_all x1, starting transfers between devices, on_device(): got = lax.all_to_all(message, ('y', 'xh', 'xl'), 0, 0)  4.54 us
    mul x2, other arithmetic, face_flux(): return speed * weno_upwind(a, b, c, d, e)  2.61 us
  transfers between devices with their start and end apart: 6, of which 4 were waited for; matrix products, arithmetic and copies ran while one was open for 7% of the time, Pallas kernels for 0%

profile of v13, /device:TPU:1, one launch (start us, length us, event | category | flops | bytes accessed | tf_op | source)
XLA Modules:
  0.0 68.8 jit_solution(13360168732239070383)
XLA Ops:
  0.6 0.0 copy-start.5
  0.6 0.0 copy-start
  0.7 0.0 copy-start.1
  0.7 0.0 copy-start.2
  0.7 0.0 copy-start.3
  0.7 1.8 %pack.1 = (f32[64,384]{1,0:T(8,128)S(1)}, f32[64,384]{1,0:T(8,128)S(1)}, f32[4,16,384]{2,1,0:T(8,128)S(1)}, f32[40,128]{1,0:T(8,128)S(1)}, s32[2,8,128]{2,1,0:T(...) custom-call(f32[8,16,384]{2,1,0:T(8,128)} %t.1, f32[8,16,384]{2,1,0:T(8,128)} %s.1, ...), custom_call_target="tpu_custom_call" | custom-call | tf_op jit(solution)/shard_map/pack/pallas_call | solution.py:364
  2.5 0.0 copy-start.4
  2.5 4.6 %collective-permute-start = (f32[16,128]{1,0:T(8,128)S(1)}, f32[16,128]{1,0:T(8,128)S(1)}, u32[]{:S(2)}, u32[]{:S(2)}) collective-permute-start(f32[16,128]{1,0:T(8,128)S(1)} %get-tuple-element.23), channel_id=1, source_target_pairs={{1,2},{2,1},{5,6},{6,5},{9,10},{10,9},{13,14},{14,13},{17,18},{18,... | collective-permute-start | bytes 24584 | tf_op jit(solution)/shard_map/ppermute | solution.py:379
  7.2 8.6 %collective-permute-start.1 = (f32[16,128]{1,0:T(8,128)S(1)}, f32[16,128]{1,0:T(8,128)S(1)}, u32[]{:S(2)}, u32[]{:S(2)}) collective-permute-start(f32[16,128]{1,0:T(8,128)S(1)} %get-tuple-element.24), channel_id=1, source_target_pairs={{0,1},{1,0},{2,3},{3,2},{4,5},{5,4},{6,7},{7,6},{8,9},{9,8},{10,11... | collective-permute-start | bytes 24584 | tf_op jit(solution)/shard_map/ppermute | solution.py:380
  15.7 0.0 copy-done.5
  15.8 0.0 copy-done
  15.8 0.0 copy-done.1
  15.8 0.0 copy-done.2
  15.8 0.0 copy-done.3
  15.8 0.0 copy-done.4
  15.8 0.1 fusion.20
  16.0 0.0 collective-permute-done.chip_got
  16.0 0.6 collective-permute-done.1.core_got
  16.6 0.2 widen.1
  16.8 13.1 %collective-permute-start.2 = (f32[72,384]{1,0:T(8,128)S(1)}, f32[72,384]{1,0:T(8,128)S(1)}, u32[]{:S(2)}, u32[]{:S(2)}) collective-permute-start(f32[72,384]{1,0:T(8,128)S(1)} %get-tuple-element.31), channel_id=1, source_target_pairs={{4,8},{8,4},{12,16},{16,12},{20,24},{24,20},{28,32},{32,28},{36,40... | collective-permute-start | bytes 331784 | tf_op jit(solution)/shard_map/ppermute | solution.py:401
  29.8 1.9 %collective-permute-start.3 = (f32[72,384]{1,0:T(8,128)S(1)}, f32[72,384]{1,0:T(8,128)S(1)}, u32[]{:S(2)}, u32[]{:S(2)}) collective-permute-start(f32[72,384]{1,0:T(8,128)S(1)} %get-tuple-element.32), channel_id=1, source_target_pairs={{0,4},{4,0},{8,12},{12,8},{16,20},{20,16},{24,28},{28,24},{32,36},... | collective-permute-start | bytes 331784 | tf_op jit(solution)/shard_map/ppermute | solution.py:400
  31.8 0.1 reshape.93
  31.8 0.2 copy.19
  32.0 0.1 reshape.94
  32.1 0.2 copy.20
  32.2 0.2 concatenate.48
  32.5 0.1 broadcast_compare_fusion.1
  32.6 0.2 maximum_maximum_fusion.2
  32.8 1.2 %add_multiply_fusion.1 = f32[2,8,16,385]{3,2,1,0:T(8,128)S(1)} fusion(f32[2,8,16,387]{3,2,1,0:T(8,128)S(1)} %get-tuple-element.49, f32[2,8,16,387]{3,2,1,0:T(8,128)S(1)} %get-tuple-element.48, f32[8,16,385]{2,1,0:T(8,128)S(1)} %get-tuple-element.43, pred[8,16,385]{2,1,0:T(8,128)(4,1)S(1)} %get-tuple-element.42), kind=kLoop, calls=%fused_computation.40 | loop fusion | flops 6012160 | bytes 3006080 | tf_op jit(solution)/shard_map/mul | solution.py:38
  34.1 0.0 collective-permute-done.2.far
  34.1 1.8 %collective-permute-done.3.close = f32[72,384]{1,0:T(8,128)S(1)} collective-permute-done((f32[72,384]{1,0:T(8,128)S(1)}, f32[72,384]{1,0:T(8,128)S(1)}, u32[]{:S(2)}, u32[]{:S(2)}) %collective-permute-start.3) | collective-permute-done | bytes 110624 | tf_op jit(solution)/shard_map/ppermute | solution.py:400
  36.0 0.1 broadcast_compare_fusion
  36.1 1.0 %krylov.1 = (f32[4,16,384]{2,1,0:T(8,128)S(1)}, f32[32,4,128]{2,1,0:T(4,128)}) custom-call(f32[8,128]{1,0:T(8,128)S(1)} %get-tuple-element.29.piece, f32[3,16,512]{2,1,0:T(8,128)S(1)} %get-tuple-element.30.plane, f32[72,384]{1,0:T(8,128)S(1)} %collective-permute-done.2.far, f32[72,384]{1,0:T(8,128)S(1)} %collective-permute-done.3.close), custom_call_target="tpu_custom_call" | custom-call | tf_op jit(solution)/shard_map/krylov/pallas_call | solution.py:402
  37.1 4.5 %all-to-all-start = ((f32[32,4,128]{2,1,0:T(4,128)}), f32[32,4,128]{2,1,0:T(4,128)S(1)}, u32[]{:S(2)}, u32[]{:S(2)}) async-start(f32[32,4,128]{2,1,0:T(4,128)} %get-tuple-element.35), calls=%async_computation | async-start | bytes 131072 | tf_op jit(solution)/shard_map/all_to_all | solution.py:408
  41.7 0.1 maximum_maximum_fusion
  41.8 1.4 %add_multiply_fusion = f32[2,8,17,384]{3,2,1,0:T(8,128)S(1)} fusion(f32[2,8,19,384]{3,2,1,0:T(8,128)S(1)} %get-tuple-element.47, f32[2,8,19,384]{3,2,1,0:T(8,128)S(1)} %get-tuple-element.46, f32[8,17,384]{2,1,0:T(8,128)S(1)} %pad_maximum_fusion.1, pred[8,17,384]{2,1,0:T(8,128)(4,1)S(1)} %broadcast_compare_fusion), kind=kLoop, calls=%fused_computation.28 | loop fusion | flops 6371328 | bytes 3185664 | tf_op jit(solution)/shard_map/mul | solution.py:38
  43.1 0.3 fusion.15
  43.4 7.0 %all-to-all-done.got = f32[32,4,128]{2,1,0:T(4,128)S(1)} async-done(((f32[32,4,128]{2,1,0:T(4,128)}), f32[32,4,128]{2,1,0:T(4,128)S(1)}, u32[]{:S(2)}, u32[]{:S(2)}) %all-to-all-start) | async-done | bytes 65568 | tf_op jit(solution)/shard_map/all_to_all | solution.py:408
  50.5 0.7 relay.1
  51.1 6.7 %all-to-all-start.1 = ((f32[24,4,128]{2,1,0:T(4,128)}), f32[24,4,128]{2,1,0:T(4,128)S(1)}, u32[]{:S(2)}, u32[]{:S(2)}) async-start(f32[24,4,128]{2,1,0:T(4,128)} %relay.1), calls=%async_computation.1 | async-start | bytes 98304 | tf_op jit(solution)/shard_map/all_to_all | solution.py:412
  57.8 0.8 %slice_bitcast_fusion = (f32[8,16,384]{2,1,0:T(8,128)}, f32[8,16,384]{2,1,0:T(8,128)}) fusion(f32[2,8,16,384]{3,2,1,0:T(8,128)S(1)} %fusion.15), kind=kLoop, calls=%fused_computation.55 | loop fusion | bytes 786432 | tf_op jit(solution)/shard_map/squeeze | solution.py:467
  58.6 9.3 %all-to-all-done.1.got = f32[24,4,128]{2,1,0:T(4,128)S(1)} async-done(((f32[24,4,128]{2,1,0:T(4,128)}), f32[24,4,128]{2,1,0:T(4,128)S(1)}, u32[]{:S(2)}, u32[]{:S(2)}) %all-to-all-start.1) | async-done | bytes 49184 | tf_op jit(solution)/shard_map/all_to_all | solution.py:412
  67.9 0.9 %finish.1 = (f32[16,384]{1,0:T(8,128)}, f32[16,384]{1,0:T(8,128)}, f32[8,16,384]{2,1,0:T(8,128)}, f32[8,16,384]{2,1,0:T(8,128)}) custom-call(f32[4,16,384]{2,1,0:T(8,128)S(1)} %get-tuple-element.33.basis_ref, s32[2,8,128]{2,1,0:T(8,128)S(1)} %get-tuple-element.34.source, ...), custom_call_target="tpu_custom_call", output_to_operand_aliasing={{2}: (6, {}), {3}: (7, {})} | custom-call | tf_op jit(solution)/shard_map/finish/pallas_call | solution.py:445
  (10 shorter events, 0.2 us)
Async XLA Ops:
  0.6 15.1 %copy-start.5 = (s32[16,384]{1,0:T(8,128)S(1)}, s32[16,384]{1,0:T(8,128)}, u32[]{:S(2)}) copy-start(s32[16,384]{1,0:T(8,128)} %flag.1) | copy-start | bytes 73732
  0.6 15.1 %copy-start = (f32[8,16,384]{2,1,0:T(8,128)S(1)}, f32[8,16,384]{2,1,0:T(8,128)}, u32[]{:S(2)}) copy-start(f32[8,16,384]{2,1,0:T(8,128)} %t.1) | copy-start | bytes 589828
  0.7 15.1 %copy-start.1 = (f32[8,16,384]{2,1,0:T(8,128)S(1)}, f32[8,16,384]{2,1,0:T(8,128)}, u32[]{:S(2)}) copy-start(f32[8,16,384]{2,1,0:T(8,128)} %s.1) | copy-start | bytes 589828
  0.7 15.1 %copy-start.2 = (f32[8,16,384]{2,1,0:T(8,128)S(1)}, f32[8,16,384]{2,1,0:T(8,128)}, u32[]{:S(2)}) copy-start(f32[8,16,384]{2,1,0:T(8,128)} %u.1) | copy-start | bytes 589828
  0.7 15.1 %copy-start.3 = (f32[8,16,384]{2,1,0:T(8,128)S(1)}, f32[8,16,384]{2,1,0:T(8,128)}, u32[]{:S(2)}) copy-start(f32[8,16,384]{2,1,0:T(8,128)} %v.1) | copy-start | bytes 589828
  2.5 13.3 %copy-start.4 = (s32[16,384]{1,0:T(8,128)S(1)}, s32[16,384]{1,0:T(8,128)}, u32[]{:S(2)}) copy-start(s32[16,384]{1,0:T(8,128)} %depth.1) | copy-start | bytes 73732
  2.5 13.5 %collective-permute-start = (f32[16,128]{1,0:T(8,128)S(1)}, f32[16,128]{1,0:T(8,128)S(1)}, u32[]{:S(2)}, u32[]{:S(2)}) collective-permute-start(f32[16,128]{1,0:T(8,128)S(1)} %get-tuple-element.23), channel_id=1, source_target_pairs={{1,2},{2,1},{5,6},{6,5},{9,10},{10,9},{13,14},{14,13},{17,18},{18,... | collective-permute-start | bytes 24584 | tf_op jit(solution)/shard_map/ppermute | solution.py:379
  7.2 9.4 %collective-permute-start.1 = (f32[16,128]{1,0:T(8,128)S(1)}, f32[16,128]{1,0:T(8,128)S(1)}, u32[]{:S(2)}, u32[]{:S(2)}) collective-permute-start(f32[16,128]{1,0:T(8,128)S(1)} %get-tuple-element.24), channel_id=1, source_target_pairs={{0,1},{1,0},{2,3},{3,2},{4,5},{5,4},{6,7},{7,6},{8,9},{9,8},{10,11... | collective-permute-start | bytes 24584 | tf_op jit(solution)/shard_map/ppermute | solution.py:380
  16.8 17.3 %collective-permute-start.2 = (f32[72,384]{1,0:T(8,128)S(1)}, f32[72,384]{1,0:T(8,128)S(1)}, u32[]{:S(2)}, u32[]{:S(2)}) collective-permute-start(f32[72,384]{1,0:T(8,128)S(1)} %get-tuple-element.31), channel_id=1, source_target_pairs={{4,8},{8,4},{12,16},{16,12},{20,24},{24,20},{28,32},{32,28},{36,40... | collective-permute-start | bytes 331784 | tf_op jit(solution)/shard_map/ppermute | solution.py:401
  29.8 6.1 %collective-permute-start.3 = (f32[72,384]{1,0:T(8,128)S(1)}, f32[72,384]{1,0:T(8,128)S(1)}, u32[]{:S(2)}, u32[]{:S(2)}) collective-permute-start(f32[72,384]{1,0:T(8,128)S(1)} %get-tuple-element.32), channel_id=1, source_target_pairs={{0,4},{4,0},{8,12},{12,8},{16,20},{20,16},{24,28},{28,24},{32,36},... | collective-permute-start | bytes 331784 | tf_op jit(solution)/shard_map/ppermute | solution.py:400
  37.1 13.4 %all-to-all-start = ((f32[32,4,128]{2,1,0:T(4,128)}), f32[32,4,128]{2,1,0:T(4,128)S(1)}, u32[]{:S(2)}, u32[]{:S(2)}) async-start(f32[32,4,128]{2,1,0:T(4,128)} %get-tuple-element.35), calls=%async_computation | async-start | bytes 131072 | tf_op jit(solution)/shard_map/all_to_all | solution.py:408
  51.1 16.8 %all-to-all-start.1 = ((f32[24,4,128]{2,1,0:T(4,128)}), f32[24,4,128]{2,1,0:T(4,128)S(1)}, u32[]{:S(2)}, u32[]{:S(2)}) async-start(f32[24,4,128]{2,1,0:T(4,128)} %relay.1), calls=%async_computation.1 | async-start | bytes 98304 | tf_op jit(solution)/shard_map/all_to_all | solution.py:412

commit v14 on v13

--- a/solution.py
+++ b/solution.py
@@ -103,7 +103,7 @@
 
 def pack_kernel(
     t, s, u, v, elev, flag, depth, fc,
-    far, close, fields, edges, source, fold_ref, chip_swap, core_swap, tile,
+    fields, edges, source, fold_ref, chip_swap, core_swap, tile,
 ):
     nl, ni, nj = t.shape
     ocean = flag[...] == 1
@@ -155,6 +155,32 @@
     chip_swap[12:14] = none
     chip_swap[14:16] = none
 
+    block = lax.shift_right_logical(jnp.broadcast_to(fc[0:1, 0:1], (8, 128)), 4)
+    nz = lax.axis_size("z")
+    columns = lax.axis_size("y") * lax.axis_size("xh")
+    column = lax.axis_index("y") * lax.axis_size("xh") + lax.axis_index("xh")
+    place = lax.axis_index("z")
+
+    def column_of(x):
+        count = jnp.zeros((8, 128), jnp.int32)
+        for k in range(1, columns):
+            count = count + jnp.where(x >= nz * k, 1, 0)
+        return count
+
+    total = block + (nz * column + place)
+    total = jnp.where(total >= nz * columns, total - nz * columns, total)
+    ahead = total - nz * column_of(total) - place
+    ahead = jnp.where(ahead < 0, ahead + nz, ahead)
+    origin = total - (nz * column + ahead)
+    origin = jnp.where(origin < 0, origin + nz * columns, origin)
+    source[0] = column_of(origin)
+    source[1] = block - nz * column_of(block)
+
+
+def edge_kernel(t, s, u, flag, depth, far, close):
+    nl, ni, nj = t.shape
+    ocean = flag[...] == 1
+    wet = depth[...]
     even = lon_even()
     zero = jnp.zeros((2, nj), jnp.float32)
     for l in range(nl):
@@ -166,26 +192,6 @@
         west_edge = jnp.concatenate([tt[:3], ss[:3], zero], axis=0)
         far[8 * l : 8 * l + 8] = jnp.where(even, west_edge, east_edge)
         close[8 * l : 8 * l + 8] = jnp.where(even, east_edge, west_edge)
-    block = lax.shift_right_logical(jnp.broadcast_to(fc[0:1, 0:1], (8, 128)), 4)
-    nz = lax.axis_size("z")
-    columns = lax.axis_size("y") * lax.axis_size("xh")
-    column = lax.axis_index("y") * lax.axis_size("xh") + lax.axis_index("xh")
-    place = lax.axis_index("z")
-
-    def column_of(x):
-        count = jnp.zeros((8, 128), jnp.int32)
-        for k in range(1, columns):
-            count = count + jnp.where(x >= nz * k, 1, 0)
-        return count
-
-    total = block + (nz * column + place)
-    total = jnp.where(total >= nz * columns, total - nz * columns, total)
-    ahead = total - nz * column_of(total) - place
-    ahead = jnp.where(ahead < 0, ahead + nz, ahead)
-    origin = total - (nz * column + ahead)
-    origin = jnp.where(origin < 0, origin + nz * columns, origin)
-    source[0] = column_of(origin)
-    source[1] = block - nz * column_of(block)
 
 
 def widen_kernel(
@@ -361,11 +367,9 @@
         last = lat == n_lat - 1
         hbm, local = pl.BlockSpec(memory_space=pl.ANY), pl.BlockSpec(memory_space=pltpu.VMEM)
 
-        far, close, fields, edges, source, fold, chip_swap, core_swap = pl.pallas_call(
+        fields, edges, source, fold, chip_swap, core_swap = pl.pallas_call(
             pack_kernel,
             out_shape=(
-                vmem(64, nj),
-                vmem(64, nj),
                 vmem(4, ni, nj),
                 vmem(40, 128),
                 pltpu.VMEM((2, 8, 128), jnp.int32),
@@ -376,6 +380,9 @@
             scratch_shapes=[vmem(128, 128)],
             name="pack",
         )(t, s, u, v, elev, flag, depth, fc.reshape(1, ni))
+        far, close = pl.pallas_call(
+            edge_kernel, out_shape=(vmem(64, nj), vmem(64, nj)), name="edge"
+        )(near(t), near(s), near(u), near(flag), near(depth))
         chip_got = lax.ppermute(chip_swap, LAT, [(1, 2), (2, 1)])
         core_got = lax.ppermute(core_swap, LAT, [(0, 1), (1, 0), (2, 3), (3, 2)])
         far, close, plane, rims, piece = pl.pallas_call(

time: 69.2 us -> 69.2 us (level)
    pallas_call x1 -> x2, Pallas kernels: 1.83 us -> 1.9 us  [the longest x1 1.82 us: on_device(): pl.pallas_call(pack_kernel, out_shape=(vmem(4, ni, nj), vmem(40, 128), pl...]
where the time goes in v14:
time: 69.2 us; the launch traced here: 68.8 us
  starting transfers between devices  39.4 us (57%)
  waiting for transfers between devices  18.7 us (27%)
  Pallas kernels  4.63 us (7%)
  other arithmetic  3.54 us (5%)
  local copies, waits for them, and re-layouts  1.58 us (2%)
  between operations  0.94 us (1%)
    ppermute x1, starting transfers between devices, on_device(): far = lax.ppermute(far, LON, swaps(1))  13.1 us
    all_to_all x1, waiting for transfers between devices, on_device(): got = lax.all_to_all(message, ('z', 'core'), 0, 0)  9.32 us
    ppermute x1, starting transfers between devices, on_device(): core_got = lax.ppermute(core_swap, LAT, [(0, 1), (1, 0), (2, 3), (3, 2)])  8.58 us
    all_to_all x1, waiting for transfers between devices, on_device(): got = lax.all_to_all(message, ('y', 'xh', 'xl'), 0, 0)  7.05 us
    all_to_all x1, starting transfers between devices, on_device(): got = lax.all_to_all(message, ('z', 'core'), 0, 0)  6.68 us
    ppermute x1, starting transfers between devices, on_device(): chip_got = lax.ppermute(chip_swap, LAT, [(1, 2), (2, 1)])  4.64 us
    all_to_all x1, starting transfers between devices, on_device(): got = lax.all_to_all(message, ('y', 'xh', 'xl'), 0, 0)  4.54 us
    mul x2, other arithmetic, face_flux(): return speed * weno_upwind(a, b, c, d, e)  2.61 us
  transfers between devices with their start and end apart: 6, of which 4 were waited for; matrix products, arithmetic and copies ran while one was open for 7% of the time, Pallas kernels for 0%

profile of v14, /device:TPU:1, one launch (start us, length us, event | category | flops | bytes accessed | tf_op | source)
XLA Modules:
  0.0 68.8 jit_solution(13137263533543589765)
XLA Ops:
  0.6 0.0 copy-start.4
  0.6 0.0 copy-start
  0.7 0.0 copy-start.1
  0.7 0.0 copy-start.2
  0.7 0.0 copy-start.5
  0.7 1.8 %pack.1 = (f32[4,16,384]{2,1,0:T(8,128)S(1)}, f32[40,128]{1,0:T(8,128)S(1)}, s32[2,8,128]{2,1,0:T(8,128)S(1)}, f32[8,128]{1,0:T(8,128)S(1)}, f32[16,128]{1,0:T(8,128)S(1)}, /*index=5*/f32[16,128]{1,0:T(8,128)S(1)}) custom-call(f32[8,16,384]{2,1,0:T(8,128)} %t.3, f32[8,16,384]{2,1,0:T(8,128)} %s.3, f32[8,16,384]{2,1,0:T(8,128)} %u.3, f32[8,16,384]{2,1,0:T(8,128)} %v.1, ...), custom_call_target="tpu_custom_call" | custom-call | tf_op jit(solution)/shard_map/pack/pallas_call | solution.py:370
  2.5 0.0 copy-start.3
  2.5 4.6 %collective-permute-start = (f32[16,128]{1,0:T(8,128)S(1)}, f32[16,128]{1,0:T(8,128)S(1)}, u32[]{:S(2)}, u32[]{:S(2)}) collective-permute-start(f32[16,128]{1,0:T(8,128)S(1)} %get-tuple-element.23), channel_id=1, source_target_pairs={{1,2},{2,1},{5,6},{6,5},{9,10},{10,9},{13,14},{14,13},{17,18},{18,... | collective-permute-start | bytes 24584 | tf_op jit(solution)/shard_map/ppermute | solution.py:386
  7.2 8.6 %collective-permute-start.1 = (f32[16,128]{1,0:T(8,128)S(1)}, f32[16,128]{1,0:T(8,128)S(1)}, u32[]{:S(2)}, u32[]{:S(2)}) collective-permute-start(f32[16,128]{1,0:T(8,128)S(1)} %get-tuple-element.24), channel_id=1, source_target_pairs={{0,1},{1,0},{2,3},{3,2},{4,5},{5,4},{6,7},{7,6},{8,9},{9,8},{10,11... | collective-permute-start | bytes 24584 | tf_op jit(solution)/shard_map/ppermute | solution.py:387
  15.7 0.0 copy-done.4
  15.8 0.0 copy-done
  15.8 0.0 copy-done.1
  15.8 0.0 copy-done.2
  15.8 0.0 copy-done.5
  15.8 0.0 copy-done.3
  15.8 0.1 fusion.20
  15.9 0.1 edge.1
  16.1 0.0 collective-permute-done.chip_got
  16.1 0.5 collective-permute-done.1.core_got
  16.5 0.2 widen.1
  16.8 13.1 %collective-permute-start.2 = (f32[72,384]{1,0:T(8,128)S(1)}, f32[72,384]{1,0:T(8,128)S(1)}, u32[]{:S(2)}, u32[]{:S(2)}) collective-permute-start(f32[72,384]{1,0:T(8,128)S(1)} %get-tuple-element.31), channel_id=1, source_target_pairs={{4,8},{8,4},{12,16},{16,12},{20,24},{24,20},{28,32},{32,28},{36,40... | collective-permute-start | bytes 331784 | tf_op jit(solution)/shard_map/ppermute | solution.py:408
  29.8 1.9 %collective-permute-start.3 = (f32[72,384]{1,0:T(8,128)S(1)}, f32[72,384]{1,0:T(8,128)S(1)}, u32[]{:S(2)}, u32[]{:S(2)}) collective-permute-start(f32[72,384]{1,0:T(8,128)S(1)} %get-tuple-element.32), channel_id=1, source_target_pairs={{0,4},{4,0},{8,12},{12,8},{16,20},{20,16},{24,28},{28,24},{32,36},... | collective-permute-start | bytes 331784 | tf_op jit(solution)/shard_map/ppermute | solution.py:407
  31.7 0.1 reshape.93
  31.8 0.2 copy.19
  32.0 0.1 reshape.94
  32.1 0.2 copy.20
  32.2 0.2 concatenate.48
  32.4 0.1 broadcast_compare_fusion.1
  32.6 0.2 maximum_maximum_fusion.2
  32.8 1.2 %add_multiply_fusion.1 = f32[2,8,16,385]{3,2,1,0:T(8,128)S(1)} fusion(f32[2,8,16,387]{3,2,1,0:T(8,128)S(1)} %get-tuple-element.49, f32[2,8,16,387]{3,2,1,0:T(8,128)S(1)} %get-tuple-element.48, f32[8,16,385]{2,1,0:T(8,128)S(1)} %get-tuple-element.43, pred[8,16,385]{2,1,0:T(8,128)(4,1)S(1)} %get-tuple-element.42), kind=kLoop, calls=%fused_computation.40 | loop fusion | flops 6012160 | bytes 3006080 | tf_op jit(solution)/shard_map/mul | solution.py:38
  34.1 0.0 collective-permute-done.2.far
  34.1 1.8 %collective-permute-done.3.close = f32[72,384]{1,0:T(8,128)S(1)} collective-permute-done((f32[72,384]{1,0:T(8,128)S(1)}, f32[72,384]{1,0:T(8,128)S(1)}, u32[]{:S(2)}, u32[]{:S(2)}) %collective-permute-start.3) | collective-permute-done | bytes 110624 | tf_op jit(solution)/shard_map/ppermute | solution.py:407
  36.0 0.1 broadcast_compare_fusion
  36.1 1.0 %krylov.1 = (f32[4,16,384]{2,1,0:T(8,128)S(1)}, f32[32,4,128]{2,1,0:T(4,128)}) custom-call(f32[8,128]{1,0:T(8,128)S(1)} %get-tuple-element.29.piece, f32[3,16,512]{2,1,0:T(8,128)S(1)} %get-tuple-element.30.plane, f32[72,384]{1,0:T(8,128)S(1)} %collective-permute-done.2.far, f32[72,384]{1,0:T(8,128)S(1)} %collective-permute-done.3.close), custom_call_target="tpu_custom_call" | custom-call | tf_op jit(solution)/shard_map/krylov/pallas_call | solution.py:409
  37.1 4.5 %all-to-all-start = ((f32[32,4,128]{2,1,0:T(4,128)}), f32[32,4,128]{2,1,0:T(4,128)S(1)}, u32[]{:S(2)}, u32[]{:S(2)}) async-start(f32[32,4,128]{2,1,0:T(4,128)} %get-tuple-element.35), calls=%async_computation | async-start | bytes 131072 | tf_op jit(solution)/shard_map/all_to_all | solution.py:415
  41.7 0.1 maximum_maximum_fusion
  41.8 1.4 %add_multiply_fusion = f32[2,8,17,384]{3,2,1,0:T(8,128)S(1)} fusion(f32[2,8,19,384]{3,2,1,0:T(8,128)S(1)} %get-tuple-element.47, f32[2,8,19,384]{3,2,1,0:T(8,128)S(1)} %get-tuple-element.46, f32[8,17,384]{2,1,0:T(8,128)S(1)} %pad_maximum_fusion.1, pred[8,17,384]{2,1,0:T(8,128)(4,1)S(1)} %broadcast_compare_fusion), kind=kLoop, calls=%fused_computation.28 | loop fusion | flops 6371328 | bytes 3185664 | tf_op jit(solution)/shard_map/mul | solution.py:38
  43.1 0.3 fusion.15
  43.4 7.1 %all-to-all-done.got = f32[32,4,128]{2,1,0:T(4,128)S(1)} async-done(((f32[32,4,128]{2,1,0:T(4,128)}), f32[32,4,128]{2,1,0:T(4,128)S(1)}, u32[]{:S(2)}, u32[]{:S(2)}) %all-to-all-start) | async-done | bytes 65568 | tf_op jit(solution)/shard_map/all_to_all | solution.py:415
  50.5 0.7 relay.1
  51.1 6.7 %all-to-all-start.1 = ((f32[24,4,128]{2,1,0:T(4,128)}), f32[24,4,128]{2,1,0:T(4,128)S(1)}, u32[]{:S(2)}, u32[]{:S(2)}) async-start(f32[24,4,128]{2,1,0:T(4,128)} %relay.1), calls=%async_computation.1 | async-start | bytes 98304 | tf_op jit(solution)/shard_map/all_to_all | solution.py:419
  57.8 0.8 %slice_bitcast_fusion = (f32[8,16,384]{2,1,0:T(8,128)}, f32[8,16,384]{2,1,0:T(8,128)}) fusion(f32[2,8,16,384]{3,2,1,0:T(8,128)S(1)} %fusion.15), kind=kLoop, calls=%fused_computation.55 | loop fusion | bytes 786432 | tf_op jit(solution)/shard_map/squeeze | solution.py:474
  58.6 9.3 %all-to-all-done.1.got = f32[24,4,128]{2,1,0:T(4,128)S(1)} async-done(((f32[24,4,128]{2,1,0:T(4,128)}), f32[24,4,128]{2,1,0:T(4,128)S(1)}, u32[]{:S(2)}, u32[]{:S(2)}) %all-to-all-start.1) | async-done | bytes 49184 | tf_op jit(solution)/shard_map/all_to_all | solution.py:419
  67.9 0.9 %finish.1 = (f32[16,384]{1,0:T(8,128)}, f32[16,384]{1,0:T(8,128)}, f32[8,16,384]{2,1,0:T(8,128)}, f32[8,16,384]{2,1,0:T(8,128)}) custom-call(f32[4,16,384]{2,1,0:T(8,128)S(1)} %get-tuple-element.33.basis_ref, s32[2,8,128]{2,1,0:T(8,128)S(1)} %get-tuple-element.34.source, ...), custom_call_target="tpu_custom_call", output_to_operand_aliasing={{2}: (6, {}), {3}: (7, {})} | custom-call | tf_op jit(solution)/shard_map/finish/pallas_call | solution.py:452
  (10 shorter events, 0.2 us)
Async XLA Ops:
  0.6 15.1 %copy-start.4 = (s32[16,384]{1,0:T(8,128)S(1)}, s32[16,384]{1,0:T(8,128)}, u32[]{:S(2)}) copy-start(s32[16,384]{1,0:T(8,128)} %flag.3) | copy-start | bytes 73732
  0.6 15.1 %copy-start = (f32[8,16,384]{2,1,0:T(8,128)S(1)}, f32[8,16,384]{2,1,0:T(8,128)}, u32[]{:S(2)}) copy-start(f32[8,16,384]{2,1,0:T(8,128)} %t.3) | copy-start | bytes 589828
  0.7 15.1 %copy-start.1 = (f32[8,16,384]{2,1,0:T(8,128)S(1)}, f32[8,16,384]{2,1,0:T(8,128)}, u32[]{:S(2)}) copy-start(f32[8,16,384]{2,1,0:T(8,128)} %s.3) | copy-start | bytes 589828
  0.7 15.1 %copy-start.2 = (f32[8,16,384]{2,1,0:T(8,128)S(1)}, f32[8,16,384]{2,1,0:T(8,128)}, u32[]{:S(2)}) copy-start(f32[8,16,384]{2,1,0:T(8,128)} %u.3) | copy-start | bytes 589828
  0.7 15.1 %copy-start.5 = (f32[8,16,384]{2,1,0:T(8,128)S(1)}, f32[8,16,384]{2,1,0:T(8,128)}, u32[]{:S(2)}) copy-start(f32[8,16,384]{2,1,0:T(8,128)} %v.1) | copy-start | bytes 589828
  2.5 13.3 %copy-start.3 = (s32[16,384]{1,0:T(8,128)S(1)}, s32[16,384]{1,0:T(8,128)}, u32[]{:S(2)}) copy-start(s32[16,384]{1,0:T(8,128)} %depth.3) | copy-start | bytes 73732
  2.5 13.6 %collective-permute-start = (f32[16,128]{1,0:T(8,128)S(1)}, f32[16,128]{1,0:T(8,128)S(1)}, u32[]{:S(2)}, u32[]{:S(2)}) collective-permute-start(f32[16,128]{1,0:T(8,128)S(1)} %get-tuple-element.23), channel_id=1, source_target_pairs={{1,2},{2,1},{5,6},{6,5},{9,10},{10,9},{13,14},{14,13},{17,18},{18,... | collective-permute-start | bytes 24584 | tf_op jit(solution)/shard_map/ppermute | solution.py:386
  7.2 9.4 %collective-permute-start.1 = (f32[16,128]{1,0:T(8,128)S(1)}, f32[16,128]{1,0:T(8,128)S(1)}, u32[]{:S(2)}, u32[]{:S(2)}) collective-permute-start(f32[16,128]{1,0:T(8,128)S(1)} %get-tuple-element.24), channel_id=1, source_target_pairs={{0,1},{1,0},{2,3},{3,2},{4,5},{5,4},{6,7},{7,6},{8,9},{9,8},{10,11... | collective-permute-start | bytes 24584 | tf_op jit(solution)/shard_map/ppermute | solution.py:387
  16.8 17.3 %collective-permute-start.2 = (f32[72,384]{1,0:T(8,128)S(1)}, f32[72,384]{1,0:T(8,128)S(1)}, u32[]{:S(2)}, u32[]{:S(2)}) collective-permute-start(f32[72,384]{1,0:T(8,128)S(1)} %get-tuple-element.31), channel_id=1, source_target_pairs={{4,8},{8,4},{12,16},{16,12},{20,24},{24,20},{28,32},{32,28},{36,40... | collective-permute-start | bytes 331784 | tf_op jit(solution)/shard_map/ppermute | solution.py:408
  29.8 6.1 %collective-permute-start.3 = (f32[72,384]{1,0:T(8,128)S(1)}, f32[72,384]{1,0:T(8,128)S(1)}, u32[]{:S(2)}, u32[]{:S(2)}) collective-permute-start(f32[72,384]{1,0:T(8,128)S(1)} %get-tuple-element.32), channel_id=1, source_target_pairs={{0,4},{4,0},{8,12},{12,8},{16,20},{20,16},{24,28},{28,24},{32,36},... | collective-permute-start | bytes 331784 | tf_op jit(solution)/shard_map/ppermute | solution.py:407
  37.1 13.4 %all-to-all-start = ((f32[32,4,128]{2,1,0:T(4,128)}), f32[32,4,128]{2,1,0:T(4,128)S(1)}, u32[]{:S(2)}, u32[]{:S(2)}) async-start(f32[32,4,128]{2,1,0:T(4,128)} %get-tuple-element.35), calls=%async_computation | async-start | bytes 131072 | tf_op jit(solution)/shard_map/all_to_all | solution.py:415
  51.1 16.8 %all-to-all-start.1 = ((f32[24,4,128]{2,1,0:T(4,128)}), f32[24,4,128]{2,1,0:T(4,128)S(1)}, u32[]{:S(2)}, u32[]{:S(2)}) async-start(f32[24,4,128]{2,1,0:T(4,128)} %relay.1), calls=%async_computation.1 | async-start | bytes 98304 | tf_op jit(solution)/shard_map/all_to_all | solution.py:419
